TPU v7x, 32 devices: a whole 2x2x4 slice. The times are simulated.
32 devices in a mesh: bucket: 8 (over z, core), tok: 4 (over y, x).
Axes of the slice: x: 2, y: 2, z: 4, core: 2. Of those that a mesh axis runs over, the one named last changes fastest.
Arguments:
- tokens: bfloat16 [16, 1024, 1152], P('bucket', 'tok'), may hold values from -6 to 6
- cotangent: bfloat16 [16, 1024, 1152], P('bucket', 'tok'), may hold values from -6 to 6
- timesteps: int32 [16], P('bucket'), may hold values from 0 to 999, as said below
- bucket_ids: int32 [8], P('bucket'), may hold values from 0 to 7
- head_masks: int32 [8, 16], replicated, may hold values 0 or 1
- channel_masks: int32 [8, 36], replicated, may hold values 0 or 1
- skip_rows: int32 [16, 256], P('bucket'), may hold values from 0 to 1023, as said below
- w_qkv: bfloat16 [1152, 3456], replicated, may hold values from -0.1875 to 0.1875
- q_bias: bfloat16 [1152], replicated, may hold values from -6 to 6
- v_bias: bfloat16 [1152], replicated, may hold values from -0.75 to 0.75
- w_proj: bfloat16 [1152, 1152], replicated, may hold values from -2 to 2
- proj_bias: bfloat16 [1152], replicated, may hold values from -4 to 4
- w_fc1: bfloat16 [1152, 4608], replicated, may hold values from -0.1875 to 0.1875
- fc1_bias: bfloat16 [4608], replicated, may hold values from -4 to 4
- w_fc2: bfloat16 [4608, 1152], replicated, may hold values from -0.1875 to 0.1875
- fc2_bias: bfloat16 [1152], replicated, may hold values from -4 to 4
- ada_weight: bfloat16 [1152, 6912], P(None, 'tok'), may hold values from -0.25 to 0.25
- ada_bias: bfloat16 [6912], P('tok'), may hold values from -4 to 4
Outputs:
- output: bfloat16 [16, 1024, 1152], P('bucket', 'tok')
- grad_tokens: float32 [16, 1024, 1152], P('bucket', 'tok')
- grad_w_qkv: float32 [1152, 3456], P('bucket', 'tok')
- grad_q_bias: float32 [1152], P(('bucket', 'tok'))
- grad_v_bias: float32 [1152], P(('bucket', 'tok'))
- grad_w_proj: float32 [1152, 1152], P('bucket', 'tok')
- grad_proj_bias: float32 [1152], P(('bucket', 'tok'))
- grad_w_fc1: float32 [1152, 4608], P('bucket', 'tok')
- grad_fc1_bias: float32 [4608], P(('bucket', 'tok'))
- grad_w_fc2: float32 [4608, 1152], P('bucket', 'tok')
- grad_fc2_bias: float32 [1152], P(('bucket', 'tok'))
- grad_ada_weight: float32 [1152, 6912], P('bucket', 'tok')
- grad_ada_bias: float32 [6912], P('bucket')
Inputs may be any that keep to these rules, and one draw needn't show every extreme that they name: The timesteps of the items of group b lie from bucket_ids[b] * 125 to (bucket_ids[b] + 1) * 125 - 1. `skip_rows`: the entries of a row are distinct.
All inputs are finite; a program needn't handle non-finite values.
Results may differ from a plain program's by a relative error of at most 0.015.
The roundings to bfloat16 on the way count: a program that leaves them out, or rounds other values in their place, can miss the bound.
Values may be sent and summed in bfloat16 or wider, within the bound.
A program may use at most 320 MiB of HBM per device.

v0:
```python
import math

import jax
import jax.numpy as jnp
from jax import lax
from jax.sharding import PartitionSpec as P

HEADS = 16


EPSILON = 1e-06


def step_embedding(timesteps, model_width):
    half_width = model_width // 2
    frequency = jnp.exp(-math.log(10000.0) * jnp.arange(half_width, dtype=jnp.float32) / half_width)
    angles = timesteps.astype(jnp.float32)[:, None] * frequency[None, :]
    return jnp.concatenate([jnp.cos(angles), jnp.sin(angles)], axis=1)


def normalize(values):
    centred = values - jnp.mean(values, axis=-1, keepdims=True)
    inverse = lax.rsqrt(jnp.mean(centred * centred, axis=-1, keepdims=True) + EPSILON)
    return (centred * inverse, inverse)


def normalize_back(incoming, normed, inverse):
    return inverse * (
        incoming
        - jnp.mean(incoming, axis=-1, keepdims=True)
        - normed * jnp.mean(incoming * normed, axis=-1, keepdims=True)
    )


def gelu_tanh(values):
    return jax.nn.gelu(values, approximate=True)


def split_heads(key_value, model_width, head_dim):
    item_count, length = (key_value.shape[0], key_value.shape[1])
    key_rows = key_value[:, :, :model_width].reshape(
        item_count, length, model_width // head_dim, head_dim
    )
    value_rows = key_value[:, :, model_width:].reshape(
        item_count, length, model_width // head_dim, head_dim
    )
    return (key_rows, value_rows)


def scores_of(queries, key_rows, score_scale):
    return (
        jnp.einsum("nqhe,nkhe->nhqk", queries, key_rows, preferred_element_type=jnp.float32)
        * score_scale
    )


def to_blocks(values, per_step):
    return values.reshape((values.shape[0] // per_step, per_step) + values.shape[1:])


def from_blocks(values):
    return values.reshape((values.shape[0] * values.shape[1],) + values.shape[2:])


def on_device(
    tokens,
    cotangent,
    timesteps,
    bucket_ids,
    head_masks,
    channel_masks,
    skip_rows,
    w_qkv,
    q_bias,
    v_bias,
    w_proj,
    proj_bias,
    w_fc1,
    fc1_bias,
    w_fc2,
    fc2_bias,
    ada_weight,
    ada_bias,
):
    item_count, local_len, model_width = tokens.shape
    row_count = item_count * local_len
    head_dim = model_width // HEADS
    score_scale = 1.0 / math.sqrt(head_dim)
    hidden_width = w_fc1.shape[1]
    ada_cols = ada_weight.shape[1]
    tok_index = lax.axis_index("tok")
    per_step = 1
    for candidate in range(1, item_count + 1):
        per_step = candidate
    condition = jax.nn.silu(step_embedding(timesteps, model_width)).astype(jnp.bfloat16)
    mod_local = jnp.dot(
        condition, ada_weight, preferred_element_type=jnp.float32
    ) + ada_bias.astype(jnp.float32)
    modulation = lax.all_gather(mod_local, "tok", axis=1, tiled=True)
    pieces = modulation.reshape(item_count, 6, 1, model_width)
    shift_a = pieces[:, 0]
    scale_a = pieces[:, 1]
    gate_a = pieces[:, 2]
    shift_m = pieces[:, 3]
    scale_m = pieces[:, 4]
    gate_m = pieces[:, 5]
    chosen = (jnp.arange(head_masks.shape[0], dtype=jnp.int32) == bucket_ids[0]).astype(jnp.float32)
    head_on = jnp.sum(chosen[:, None] * head_masks.astype(jnp.float32), axis=0)
    group_on = jnp.sum(chosen[:, None] * channel_masks.astype(jnp.float32), axis=0)
    channel_on = jnp.repeat(group_on, hidden_width // group_on.shape[0])
    positions = tok_index * local_len + jnp.arange(local_len, dtype=jnp.int32)
    skipped = jnp.any(skip_rows[:, :, None] == positions[None, None, :], axis=1)
    kept_rows = 1.0 - skipped.astype(jnp.float32)
    inputs = tokens.astype(jnp.float32)
    normed, inverse = normalize(inputs)
    shifted = (
        (normed * (1.0 + scale_a) + shift_a).astype(jnp.bfloat16).reshape(row_count, model_width)
    )
    qkv_bias = jnp.concatenate([q_bias, jnp.zeros_like(q_bias), v_bias]).astype(jnp.float32)
    projected = (jnp.dot(shifted, w_qkv, preferred_element_type=jnp.float32) + qkv_bias).astype(
        jnp.bfloat16
    )
    projected = projected.reshape(item_count, local_len, 3 * model_width)
    queries = projected[:, :, :model_width].reshape(item_count, local_len, HEADS, head_dim)
    key_value = projected[:, :, model_width:]
    all_kv = lax.all_gather(key_value, "tok", axis=1, tiled=True)

    def forward_block(packed):
        query_block, kv_block = packed
        key_rows, value_rows = split_heads(kv_block, model_width, head_dim)
        scores = scores_of(query_block, key_rows, score_scale)
        top_score = jnp.max(scores, axis=-1, keepdims=True)
        expanded = jnp.exp(scores - top_score)
        totals = jnp.sum(expanded, axis=-1, keepdims=True)
        weights_low = (expanded / totals).astype(jnp.bfloat16)
        head_out = (
            jnp.einsum(
                "nhqk,nkhe->nqhe", weights_low, value_rows, preferred_element_type=jnp.float32
            )
            * head_on[:, None]
        )
        return (head_out.astype(jnp.bfloat16), top_score + jnp.log(totals))

    mixed_heads, log_total = lax.map(
        forward_block, (to_blocks(queries, per_step), to_blocks(all_kv, per_step))
    )
    log_total = from_blocks(log_total)
    mixed = from_blocks(mixed_heads).reshape(row_count, model_width)
    attn = (
        jnp.dot(mixed, w_proj, preferred_element_type=jnp.float32) + proj_bias.astype(jnp.float32)
    ).reshape(item_count, local_len, model_width)
    resid = inputs + gate_a * attn
    normed2, inverse2 = normalize(resid)
    shifted2 = (
        (normed2 * (1.0 + scale_m) + shift_m).astype(jnp.bfloat16).reshape(row_count, model_width)
    )
    pre = jnp.dot(shifted2, w_fc1, preferred_element_type=jnp.float32) + fc1_bias.astype(
        jnp.float32
    )
    activated, gelu_pull = jax.vjp(gelu_tanh, pre)
    hidden = (activated * channel_on).astype(jnp.bfloat16)
    branch = (
        jnp.dot(hidden, w_fc2, preferred_element_type=jnp.float32) + fc2_bias.astype(jnp.float32)
    ).reshape(item_count, local_len, model_width)
    gated = kept_rows[:, :, None] * gate_m
    output = (resid + gated * branch).astype(jnp.bfloat16)
    incoming = cotangent.astype(jnp.float32)
    d_gate_m = jnp.sum(kept_rows[:, :, None] * branch * incoming, axis=1)
    d_branch = (gated * incoming).astype(jnp.bfloat16).reshape(row_count, model_width)
    grad_w_fc2 = jnp.dot(hidden.T, d_branch, preferred_element_type=jnp.float32)
    grad_fc2_bias = jnp.sum(d_branch.astype(jnp.float32), axis=0)
    d_hidden = jnp.dot(d_branch, w_fc2.T, preferred_element_type=jnp.float32)
    d_pre = gelu_pull(d_hidden * channel_on)[0].astype(jnp.bfloat16)
    grad_w_fc1 = jnp.dot(shifted2.T, d_pre, preferred_element_type=jnp.float32)
    grad_fc1_bias = jnp.sum(d_pre.astype(jnp.float32), axis=0)
    d_shifted2 = jnp.dot(d_pre, w_fc1.T, preferred_element_type=jnp.float32).reshape(
        item_count, local_len, model_width
    )
    d_shift_m = jnp.sum(d_shifted2, axis=1)
    d_scale_m = jnp.sum(d_shifted2 * normed2, axis=1)
    d_resid = incoming + normalize_back(d_shifted2 * (1.0 + scale_m), normed2, inverse2)
    d_gate_a = jnp.sum(attn * d_resid, axis=1)
    d_attn = (gate_a * d_resid).astype(jnp.bfloat16).reshape(row_count, model_width)
    grad_w_proj = jnp.dot(mixed.T, d_attn, preferred_element_type=jnp.float32)
    grad_proj_bias = jnp.sum(d_attn.astype(jnp.float32), axis=0)
    d_mixed = jnp.dot(d_attn, w_proj.T, preferred_element_type=jnp.float32).astype(jnp.bfloat16)
    d_heads = d_mixed.reshape(item_count, local_len, HEADS, head_dim) * head_on[:, None].astype(
        jnp.bfloat16
    )
    again_kv = lax.all_gather(key_value, "tok", axis=1, tiled=True)

    def backward_block(packed):
        query_block, kv_block, head_grads, totals_log = packed
        key_rows, value_rows = split_heads(kv_block, model_width, head_dim)
        scores = scores_of(query_block, key_rows, score_scale)
        probs = jnp.exp(scores - totals_log)
        d_probs = jnp.einsum(
            "nqhe,nkhe->nhqk", head_grads, value_rows, preferred_element_type=jnp.float32
        )
        row_dot = jnp.sum(probs * d_probs, axis=-1, keepdims=True)
        d_scores = (probs * (d_probs - row_dot)).astype(jnp.bfloat16)
        d_queries = (
            jnp.einsum("nhqk,nkhe->nqhe", d_scores, key_rows, preferred_element_type=jnp.float32)
            * score_scale
        )
        return (d_queries, row_dot)

    mapped = lax.map(
        backward_block,
        (
            to_blocks(queries, per_step),
            to_blocks(again_kv, per_step),
            to_blocks(d_heads, per_step),
            to_blocks(log_total, per_step),
        ),
    )
    d_queries = from_blocks(mapped[0])
    row_dot = from_blocks(mapped[1])
    queries_all, head_grads_all = (
        lax.all_gather(queries, "tok", axis=1, tiled=True),
        lax.all_gather(d_heads, "tok", axis=1, tiled=True),
    )
    totals_all, row_dot_all = (
        lax.all_gather(log_total, "tok", axis=2, tiled=True),
        lax.all_gather(row_dot, "tok", axis=2, tiled=True),
    )

    def key_block(packed):
        kv_block, query_block, head_grads, totals_log, dots = packed
        key_rows, value_rows = split_heads(kv_block, model_width, head_dim)
        scores = (
            jnp.einsum("nkhe,nqhe->nhkq", key_rows, query_block, preferred_element_type=jnp.float32)
            * score_scale
        )
        probs = jnp.exp(scores - totals_log[:, :, None, :, 0])
        d_probs = jnp.einsum(
            "nkhe,nqhe->nhkq", value_rows, head_grads, preferred_element_type=jnp.float32
        )
        d_scores = (probs * (d_probs - dots[:, :, None, :, 0])).astype(jnp.bfloat16)
        d_keys = (
            jnp.einsum("nhkq,nqhe->nkhe", d_scores, query_block, preferred_element_type=jnp.float32)
            * score_scale
        )
        d_values = jnp.einsum(
            "nhkq,nqhe->nkhe",
            probs.astype(jnp.bfloat16),
            head_grads,
            preferred_element_type=jnp.float32,
        )
        return jnp.concatenate(
            [
                d_keys.reshape(d_keys.shape[0], local_len, model_width),
                d_values.reshape(d_values.shape[0], local_len, model_width),
            ],
            axis=2,
        )

    d_kv = from_blocks(
        lax.map(
            key_block,
            (
                to_blocks(key_value, per_step),
                to_blocks(queries_all, per_step),
                to_blocks(head_grads_all, per_step),
                to_blocks(totals_all, per_step),
                to_blocks(row_dot_all, per_step),
            ),
        )
    )
    d_qkv = jnp.concatenate([d_queries.reshape(item_count, local_len, model_width), d_kv], axis=2)
    d_qkv = d_qkv.astype(jnp.bfloat16).reshape(row_count, 3 * model_width)
    grad_w_qkv = jnp.dot(shifted.T, d_qkv, preferred_element_type=jnp.float32)
    qkv_sums = jnp.sum(d_qkv.astype(jnp.float32), axis=0)
    grad_q_bias = qkv_sums[:model_width]
    grad_v_bias = qkv_sums[2 * model_width :]
    d_shifted = jnp.dot(d_qkv, w_qkv.T, preferred_element_type=jnp.float32).reshape(
        item_count, local_len, model_width
    )
    d_shift_a = jnp.sum(d_shifted, axis=1)
    d_scale_a = jnp.sum(d_shifted * normed, axis=1)
    grad_tokens = d_resid + normalize_back(d_shifted * (1.0 + scale_a), normed, inverse)
    d_modulation = jnp.concatenate(
        [d_shift_a, d_scale_a, d_gate_a, d_shift_m, d_scale_m, d_gate_m], axis=1
    )
    d_modulation = lax.psum(d_modulation, "tok")
    mod_columns = lax.dynamic_slice_in_dim(d_modulation, tok_index * ada_cols, ada_cols, 1)
    grad_ada_weight = jnp.dot(
        condition.astype(jnp.float32).T, mod_columns, precision=lax.Precision.HIGHEST
    )
    grad_ada_bias = jnp.sum(d_modulation, axis=0)
    bucket_done = (
        lax.psum_scatter(grad_w_qkv, "bucket", scatter_dimension=0, tiled=True),
        lax.psum_scatter(grad_w_proj, "bucket", scatter_dimension=0, tiled=True),
        lax.psum_scatter(grad_w_fc1, "bucket", scatter_dimension=0, tiled=True),
        lax.psum_scatter(grad_w_fc2, "bucket", scatter_dimension=0, tiled=True),
        lax.psum_scatter(grad_q_bias, "bucket", scatter_dimension=0, tiled=True),
        lax.psum_scatter(grad_v_bias, "bucket", scatter_dimension=0, tiled=True),
        lax.psum_scatter(grad_proj_bias, "bucket", scatter_dimension=0, tiled=True),
        lax.psum_scatter(grad_fc1_bias, "bucket", scatter_dimension=0, tiled=True),
        lax.psum_scatter(grad_fc2_bias, "bucket", scatter_dimension=0, tiled=True),
        lax.psum_scatter(grad_ada_weight, "bucket", scatter_dimension=0, tiled=True),
        lax.psum_scatter(grad_ada_bias, "bucket", scatter_dimension=0, tiled=True),
    )
    token_done = (
        lax.psum_scatter(bucket_done[0], "tok", scatter_dimension=1, tiled=True),
        lax.psum_scatter(bucket_done[1], "tok", scatter_dimension=1, tiled=True),
        lax.psum_scatter(bucket_done[2], "tok", scatter_dimension=1, tiled=True),
        lax.psum_scatter(bucket_done[3], "tok", scatter_dimension=1, tiled=True),
        lax.psum_scatter(bucket_done[4].reshape(1, -1), "tok", scatter_dimension=1, tiled=True),
        lax.psum_scatter(bucket_done[5].reshape(1, -1), "tok", scatter_dimension=1, tiled=True),
        lax.psum_scatter(bucket_done[6].reshape(1, -1), "tok", scatter_dimension=1, tiled=True),
        lax.psum_scatter(bucket_done[7].reshape(1, -1), "tok", scatter_dimension=1, tiled=True),
        lax.psum_scatter(bucket_done[8].reshape(1, -1), "tok", scatter_dimension=1, tiled=True),
    )
    finished = (
        token_done[0],
        token_done[1],
        token_done[2],
        token_done[3],
        token_done[4],
        token_done[5],
        token_done[6],
        token_done[7],
        token_done[8],
        bucket_done[9],
        bucket_done[10],
    )
    return (
        output,
        grad_tokens,
        finished[0],
        finished[4].reshape(-1),
        finished[5].reshape(-1),
        finished[1],
        finished[6].reshape(-1),
        finished[2],
        finished[7].reshape(-1),
        finished[3],
        finished[8].reshape(-1),
        finished[9],
        finished[10],
    )


def solution(mesh):
    return jax.shard_map(
        on_device,
        mesh=mesh,
        in_specs=(
            P("bucket", "tok", None),
            P("bucket", "tok", None),
            P("bucket"),
            P("bucket"),
            P(),
            P(),
            P("bucket", None),
            P(),
            P(),
            P(),
            P(),
            P(),
            P(),
            P(),
            P(),
            P(),
            P(None, "tok"),
            P("tok"),
        ),
        out_specs=(
            P("bucket", "tok", None),
            P("bucket", "tok", None),
            P("bucket", "tok"),
            P(("bucket", "tok")),
            P(("bucket", "tok")),
            P("bucket", "tok"),
            P(("bucket", "tok")),
            P("bucket", "tok"),
            P(("bucket", "tok")),
            P("bucket", "tok"),
            P(("bucket", "tok")),
            P("bucket", "tok"),
            P("bucket"),
        ),
        check_vma=False,
    )
```

profile of v0, /device:TPU:0, one launch (start us, length us, event | category | flops | bytes accessed | tf_op | source)
XLA Modules:
  0.0 1289.2 jit_solution(18015488394110753029)
XLA Ops:
  51.9 84.6 %all-gather.7.cloned.1.call-done = bf16[2,1024,2304]{2,1,0:T(8,128)(2,1)} async-done(((bf16[2,256,2304]{2,1,0:T(8,128)(2,1)}), bf16[2,1024,2304]{2,1,0:T(8,128)(2,1)}) %all-gather.7.cloned.1.call-update) | async-done | bytes 9437200 | tf_op jit(solution)/shard_map/all_gather | solution.py:126
  151.5 18.8 %multiply_reduce_fusion.1 = (f32[2,16,256]{2,1,0:T(8,128)S(1)}, f32[2,16,256,1024]{3,2,1,0:T(8,128)}) fusion(bf16[2,256,16,72]{1,3,2,0:T(8,128)(2,1)} %bitcast.165, bf16[2,1024,16,72]{1,3,2,0:T(8,128)(2,1)} %bitcast.150), kind=kOutput, calls=%fused_computation.9 | convolution fusion | flops 1224728576 | bytes 39485440 | tf_op jit(solution)/shard_map/while/body/eval_jaxpr/nqhe,nkhe->nhqk/dot_general | solution.py:52
  177.1 14.3 %fusion = f32[2,16,256]{2,1,0:T(8,128)S(1)} fusion(f32[2,16,256,1024]{3,2,1,0:T(8,128)} %get-tuple-element.169, f32[2,16,256]{2,1,0:T(8,128)S(1)} %get-tuple-element.168), kind=kLoop, calls=%fused_computation.7 | loop fusion | flops 25157632 | bytes 33619968 | tf_op jit(solution)/shard_map/while/body/eval_jaxpr/reduce_sum | solution.py:134
  191.3 16.8 %fusion.42 = bf16[2,256,16,72]{1,3,2,0:T(8,128)(2,1)} fusion(bf16[2,1024,16,72]{1,3,2,0:T(8,128)(2,1)} %bitcast.152, f32[2,16,256,1024]{3,2,1,0:T(8,128)} %get-tuple-element.169, f32[2,16,256]{2,1,0:T(8,128)S(1)} %fusion, f32[2,16,256]{2,1,0:T(8,128)S(1)} %get-tuple-element.168, f32[16]{0:T(128)S(1)} %multiply_reduce_fusion.7), kind=kOutput, calls=%fused_computation.81 | convolution fusion | flops 1242693632 | bytes 39518272 | tf_op jit(solution)/shard_map/while/body/eval_jaxpr/nhqk,nkhe->nqhe/dot_general | solution.py:137
  215.6 13.1 %fusion.66 = f32[512,4608]{1,0:T(8,128)} fusion(bf16[512,1152]{1,0:T(8,128)(2,1)S(1)} %bitcast.170, bf16[1152,4608]{1,0:T(8,128)(2,1)} %param.30), kind=kOutput, calls=%fused_computation.144 | convolution fusion | flops 5435817984 | bytes 21233664 | tf_op jit(solution)/shard_map/dot_general | solution.py:157
  228.7 16.3 %convert_reduce_fusion = (f32[4608]{0:T(1024)}, bf16[512,4608]{1,0:T(8,128)(2,1)S(1)}) fusion(f32[512,4608]{1,0:T(8,128)} %fusion.66, f32[4608]{0:T(1024)S(1)} %convert_element_type.143, f32[4608]{0:T(1024)S(1)} %broadcast_bitcast_fusion, bf16[512,1152]{1,0:T(8,128)(2,1)S(1)} %bitcast.184, bf16[4608,1152]{1,0:T(8,128)(2,1)} %param.32), kind=kOutput, calls=%fused_computation.25 | convolution fusion | flops 5492436480 | bytes 26007552 | tf_op jit(solution)/shard_map/dot_general | solution.py:172
  245.0 12.4 fusion.36
  262.0 13.4 %convolution_add_fusion = f32[512,1152]{1,0:T(8,128)S(1)} fusion(bf16[4608,1152]{1,0:T(8,128)(2,1)} %param.32, f32[1152]{0:T(1024)S(1)} %convert_element_type.146, f32[512,4608]{1,0:T(8,128)} %fusion.66, f32[4608]{0:T(1024)S(1)} %broadcast_bitcast_fusion, f32[4608]{0:T(1024)S(1)} %convert_element_type.143), kind=kOutput, calls=%fused_computation.40 | convolution fusion | flops 5462360064 | bytes 22454784 | tf_op jit(solution)/shard_map/dot_general | solution.py:163
  304.5 15.8 %fusion.67 = f32[2,16,256,1024]{3,2,1,0:T(8,128)} fusion(bf16[2,256,16,72]{1,3,2,0:T(8,128)(2,1)S(1)} %bitcast.168, bf16[2,1024,16,72]{1,3,2,0:T(8,128)(2,1)} %all-gather.9.cloned.1.call-done), kind=kOutput, calls=%fused_computation.145 | convolution fusion | flops 1207959552 | bytes 39452672 | tf_op jit(solution)/shard_map/while/body/eval_jaxpr/nkhe,nqhe->nhkq/dot_general | solution.py:232
  320.3 23.2 %multiply_reduce_fusion = (f32[2,16,256]{2,1,0:T(8,128)S(1)}, f32[2,16,256,1024]{3,2,1,0:T(8,128)}) fusion(f32[2,16,256,1024]{3,2,1,0:T(8,128)} %get-tuple-element.169, f32[2,16,256]{2,1,0:T(8,128)S(1)} %log_add_fusion, bf16[2,256,16,72]{1,3,2,0:T(8,128)(2,1)S(1)} %copy-done.10, bf16[2,1024,16,72]{1,3,2,0:T(8,128)(2,1)S(1)} %bitcast.155), kind=kOutput, calls=%fused_computation.3 | convolution fusion | flops 1241505792 | bytes 73072640 | tf_op jit(solution)/shard_map/while/body/eval_jaxpr/nqhe,nkhe->nhqk/dot_general | solution.py:197
  343.5 24.6 %multiply_convert_fusion.5 = bf16[2,16,72,256]{3,2,1,0:T(8,128)(2,1)S(1)} fusion(bf16[2,1024,16,72]{1,3,2,0:T(8,128)(2,1)} %bitcast.151, f32[2,16,256,1024]{3,2,1,0:T(8,128)} %get-tuple-element.173, f32[2,16,256,1024]{3,2,1,0:T(8,128)} %get-tuple-element.169, f32[2,16,256]{2,1,0:T(8,128)S(1)} %get-tuple-element.172, f32[2,16,256]{2,1,0:T(8,128)S(1)} %log_add_fusion), kind=kOutput, calls=%fused_computation.70 | convolution fusion | flops 1251082240 | bytes 73072640 | tf_op jit(solution)/shard_map/while/body/eval_jaxpr/nhqk,nkhe->nqhe/dot_general | solution.py:203
  385.5 21.6 %multiply_convert_fusion.4 = bf16[2,16,72,256]{3,2,1,0:T(8,128)(2,1)S(1)} fusion(bf16[2,1024,16,72]{1,3,2,0:T(8,128)(2,1)} %all-gather.9.cloned.1.call-done, f32[2,16,256,1024]{3,2,1,0:T(8,128)} %fusion.67, bf16[2,256,16,72]{1,3,2,0:T(8,128)(2,1)} %bitcast.186, bf16[2,1024,16,72]{1,3,2,0:T(8,128)(2,1)} %all-gather.11.cloned.1.call-done, ...), kind=kOutput, calls=%fused_computation.69 | convolution fusion | flops 2459041792 | bytes 45613056 | tf_op jit(solution)/shard_map/while/body/eval_jaxpr/nhkq,nqhe->nkhe/dot_general | solution.py:241
  409.5 15.3 %fusion.39 = bf16[2,16,72,256]{3,2,1,0:T(8,128)(2,1)S(1)} fusion(bf16[2,1024,16,72]{1,3,2,0:T(8,128)(2,1)} %all-gather.11.cloned.1.call-done, f32[2,16,256,1024]{3,2,1,0:T(8,128)} %fusion.67, f32[2,16,1024]{2,1,0:T(8,128)S(1)} %all-gather), kind=kOutput, calls=%fused_computation.80 | convolution fusion | flops 1233715200 | bytes 39583744 | tf_op jit(solution)/shard_map/while/body/eval_jaxpr/nhkq,nqhe->nkhe/dot_general | solution.py:244
  439.8 12.3 fusion.69
  453.4 14.9 %fusion.59 = f32[4608,1152]{1,0:T(8,128)} fusion(bf16[512,1152]{1,0:T(8,128)(2,1)S(1)} %bitcast.185, f32[512,4608]{1,0:T(8,128)} %fusion.66, f32[4608]{0:T(1024)S(1)} %copy-done.41, f32[4608]{0:T(1024)S(1)} %copy-done.43), kind=kOutput, calls=%fused_computation.138 | convolution fusion | flops 5461770240 | bytes 31887360 | tf_op jit(solution)/shard_map/dot_general | solution.py:170
  471.0 128.3 %reduce-scatter.21.cloned.1.call-done = f32[144,3456]{1,0:T(8,128)} async-done(((f32[1152,3456]{1,0:T(8,128)}), f32[144,3456]{1,0:T(8,128)}) %reduce-scatter.21.cloned.1.call-update) | async-done | bytes 1990672 | tf_op jit(solution)/shard_map/reduce_scatter | solution.py:292
  614.9 17.1 %psum.7 = f32[2,6912]{1,0:T(2,128)S(1)} all-reduce(f32[2,6912]{1,0:T(2,128)S(1)} %constant_dynamic-update-slice_fusion), channel_id=1, replica_groups=mesh['bucket'=8,'tok'=4] {'tok'}, use_global_device_ids=true, to_apply=%region_42.43 | all-reduce | flops 13824 | bytes 110592 | tf_op jit(solution)/shard_map/psum | solution.py:285
  638.0 172.2 %reduce-scatter.25.cloned.1.call-done = f32[144,4608]{1,0:T(8,128)} async-done(((f32[1152,4608]{1,0:T(8,128)}), f32[144,4608]{1,0:T(8,128)}) %reduce-scatter.25.cloned.1.call-update) | async-done | bytes 2654224 | tf_op jit(solution)/shard_map/reduce_scatter | solution.py:294
  810.4 210.8 %reduce-scatter.29.cloned.1.call-done = f32[576,1152]{1,0:T(8,128)} async-done(((f32[4608,1152]{1,0:T(8,128)}), f32[576,1152]{1,0:T(8,128)}) %reduce-scatter.29.cloned.1.call-update) | async-done | bytes 2654224 | tf_op jit(solution)/shard_map/reduce_scatter | solution.py:295
  1036.2 26.9 %all-reduce.11 = (f32[1152]{0:T(1024)S(1)}, f32[1152]{0:T(1024)S(1)}, f32[1152]{0:T(1024)S(1)}, f32[4608]{0:T(1024)S(1)}, f32[1152]{0:T(1024)S(1)}, /*index=5*/f32[6912]{0:T(1024)S(1)}) all-reduce(f32[1152]{0:T(1024)S(1)} %get-tuple-element.165, ...), channel_id=6, replica_groups=mesh['bucket'=8,'tok'=4] {'bucket'}, use_global_device_ids=true, to_apply=%region_17.18.clone | all-reduce | flops 16128 | bytes 129024
  1084.5 18.0 %reduce-scatter.33.cloned.1.call-done = f32[864,144]{1,0:T(8,128)} async-done(((f32[3456,144]{1,0:T(8,128)}), f32[864,144]{1,0:T(8,128)}) %reduce-scatter.33.cloned.1.call-update) | async-done | bytes 497680
  1104.6 89.0 %reduce-scatter.31.cloned.1.call-done = f32[144,1728]{1,0:T(8,128)} async-done(((f32[1152,1728]{1,0:T(8,128)}), f32[144,1728]{1,0:T(8,128)}) %reduce-scatter.31.cloned.1.call-update) | async-done | bytes 995344 | tf_op jit(solution)/shard_map/reduce_scatter | solution.py:301
  1193.6 42.2 %reduce-scatter.27.cloned.1.call-done = f32[144,1152]{1,0:T(8,128)} async-done(((f32[144,4608]{1,0:T(8,128)}), f32[144,1152]{1,0:T(8,128)}) %reduce-scatter.27.cloned.1.call-update) | async-done | bytes 663568 | tf_op jit(solution)/shard_map/reduce_scatter | solution.py:307
  1235.8 46.1 %reduce-scatter.37.cloned.1.call-done = f32[288,576]{1,0:T(8,128)} async-done(((f32[1152,576]{1,0:T(8,128)}), f32[288,576]{1,0:T(8,128)}) %reduce-scatter.37.cloned.1.call-update) | async-done | bytes 663568
  (254 shorter events, 201.7 us)
Async XLA Ops:
  7.2 203.8 %copy-start = (bf16[1152,1152]{1,0:T(8,128)(2,1)S(1)}, bf16[1152,1152]{1,0:T(8,128)(2,1)}, u32[]{:S(2)}) copy-start(bf16[1152,1152]{1,0:T(8,128)(2,1)} %param.28) | copy-start | bytes 7962628
  7.2 129.3 %all-gather.7.cloned.1.call-start = ((), (), s32[]{:S(2)}) async-start(), calls=%async_computation.9 | async-start | bytes 11796480 | tf_op jit(solution)/shard_map/all_gather | solution.py:126
  39.7 264.7 %all-gather.9.cloned.1.call-start = ((), (), s32[]{:S(2)}) async-start(), calls=%async_computation.10 | async-start | bytes 5898240 | tf_op jit(solution)/shard_map/all_gather | solution.py:220
  46.2 339.3 %all-gather.11.cloned.1.call-start = ((), (), s32[]{:S(2)}) async-start(), calls=%async_computation.11 | async-start | bytes 5898240 | tf_op jit(solution)/shard_map/all_gather | solution.py:221
  47.9 214.1 %copy-start.40 = (f32[4608]{0:T(1024)}, f32[4608]{0:T(1024)S(1)}, u32[]{:S(2)}) copy-start(f32[4608]{0:T(1024)S(1)} %broadcast_bitcast_fusion) | copy-start | bytes 55300
  47.9 214.1 %copy-start.42 = (f32[4608]{0:T(1024)}, f32[4608]{0:T(1024)S(1)}, u32[]{:S(2)}) copy-start(f32[4608]{0:T(1024)S(1)} %convert_element_type.143) | copy-start | bytes 55300
  295.2 173.2 %reduce-scatter.23.cloned.1.call-start = ((), (), s32[]{:S(2)}) async-start(), calls=%async_computation.13 | async-start | bytes 5971968 | tf_op jit(solution)/shard_map/reduce_scatter | solution.py:293
  304.4 294.9 %reduce-scatter.21.cloned.1.call-start = ((), (), s32[]{:S(2)}) async-start(), calls=%async_computation.12 | async-start | bytes 17915904 | tf_op jit(solution)/shard_map/reduce_scatter | solution.py:292
  438.5 371.7 %reduce-scatter.25.cloned.1.call-start = ((), (), s32[]{:S(2)}) async-start(), calls=%async_computation.14 | async-start | bytes 23887872 | tf_op jit(solution)/shard_map/reduce_scatter | solution.py:294
  452.1 569.1 %reduce-scatter.29.cloned.1.call-start = ((), (), s32[]{:S(2)}) async-start(), calls=%async_computation.16 | async-start | bytes 23887872 | tf_op jit(solution)/shard_map/reduce_scatter | solution.py:295
  468.3 614.3 %reduce-scatter.35.cloned.1.call-start = ((), (), s32[]{:S(2)}) async-start(), calls=%async_computation.19 | async-start | bytes 1474560
  470.9 132.0 %copy-start.5 = (bf16[2,256,1152]{2,1,0:T(8,128)(2,1)S(1)}, bf16[2,256,1152]{2,1,0:T(8,128)(2,1)}, u32[]{:S(2)}) copy-start(bf16[2,256,1152]{2,1,0:T(8,128)(2,1)} %param.18) | copy-start | bytes 3538948
  471.0 132.0 %copy-start.26 = (f32[2,1152]{1,0:T(2,128)S(1)}, f32[2,1152]{1,0:T(2,128)}, u32[]{:S(2)}) copy-start(f32[2,1152]{1,0:T(2,128)} %copy-done.25) | copy-start | bytes 27652
  471.0 132.0 %copy-start.38 = (f32[2,256]{1,0:T(2,128)S(1)}, f32[2,256]{1,0:T(2,128)}, u32[]{:S(2)}) copy-start(f32[2,256]{1,0:T(2,128)} %copy-done.37) | copy-start | bytes 6148
  471.0 132.0 %copy-start.45 = (f32[2,256]{1,0:T(2,128)S(1)}, f32[2,256]{1,0:T(2,128)}, u32[]{:S(2)}) copy-start(f32[2,256]{1,0:T(2,128)} %copy-done.44) | copy-start | bytes 6148
  471.0 631.4 %reduce-scatter.33.cloned.1.call-start = ((), (), s32[]{:S(2)}) async-start(), calls=%async_computation.18 | async-start | bytes 4423680
  602.9 590.7 %reduce-scatter.31.cloned.1.call-start = ((), (), s32[]{:S(2)}) async-start(), calls=%async_computation.17 | async-start | bytes 9289728 | tf_op jit(solution)/shard_map/reduce_scatter | solution.py:301
  603.1 29.0 %copy-start.28 = (f32[2,576]{1,0:T(2,128)S(1)}, f32[2,576]{1,0:T(2,128)}, u32[]{:S(2)}) copy-start(f32[2,576]{1,0:T(2,128)} %copy-done.27) | copy-start | bytes 13828
  603.1 29.0 %copy-start.30 = (f32[2,576]{1,0:T(2,128)S(1)}, f32[2,576]{1,0:T(2,128)}, u32[]{:S(2)}) copy-start(f32[2,576]{1,0:T(2,128)} %copy-done.29) | copy-start | bytes 13828
  638.0 597.9 %reduce-scatter.27.cloned.1.call-start = ((), (), s32[]{:S(2)}) async-start(), calls=%async_computation.15 | async-start | bytes 3317760 | tf_op jit(solution)/shard_map/reduce_scatter | solution.py:307
  810.3 214.4 %copy-start.56 = (u32[32]{0:T(128)S(1)}, u32[32]{0:T(128)}, u32[]{:S(2)}) copy-start(u32[32]{0:T(128)} %constant.116) | copy-start | bytes 388
  810.3 216.3 %copy-start.55 = (u32[32]{0:T(128)S(1)}, u32[32]{0:T(128)}, u32[]{:S(2)}) copy-start(u32[32]{0:T(128)} %constant.120) | copy-start | bytes 388
  810.3 471.6 %reduce-scatter.37.cloned.1.call-start = ((), (), s32[]{:S(2)}) async-start(), calls=%async_computation.20 | async-start | bytes 3686400
  1077.5 204.4 %copy-start.1 = (bf16[1152,1152]{1,0:T(8,128)(2,1)S(1)}, bf16[1152,1152]{1,0:T(8,128)(2,1)}, u32[]{:S(2)}) copy-start(bf16[1152,1152]{1,0:T(8,128)(2,1)} %param.28) | copy-start | bytes 7962628
  (47 other events, 352.7 us)
Sparse Core Ops, SparseCore 0:
  39.8 96.6 all-gather.6
  138.3 56.9 all-gather.8
  295.3 56.8 all-gather.10
  354.4 60.5 reduce-scatter.22
  438.6 160.6 reduce-scatter.20
  601.7 208.5 reduce-scatter.24
  812.6 208.5 reduce-scatter.28
  1024.3 26.8 reduce-scatter.34
  1054.7 47.7 reduce-scatter.32
  1105.3 88.3 reduce-scatter.30
  1197.3 38.4 reduce-scatter.26
  1239.6 42.2 reduce-scatter.36
where the time goes:
time: 1290 us
  waiting for transfers between devices  791 us (61%)
  matrix products  271 us (21%)
  local copies, waits for them, and re-layouts  81.8 us (6%)
  blocking collectives  80.2 us (6%)
  other arithmetic  44.3 us (3%)
  between operations  19.6 us (2%)
    reduce_scatter x1, waiting for transfers between devices, on_device(): lax.psum_scatter(grad_w_fc2, 'bucket', scatter_dimension=0, tiled=True)  211 us
    reduce_scatter x1, waiting for transfers between devices, on_device(): lax.psum_scatter(grad_w_fc1, 'bucket', scatter_dimension=0, tiled=True)  172 us
    reduce_scatter x1, waiting for transfers between devices, on_device(): lax.psum_scatter(grad_w_qkv, 'bucket', scatter_dimension=0, tiled=True)  128 us
    reduce_scatter x1, waiting for transfers between devices, on_device(): lax.psum_scatter(grad_ada_weight, 'bucket', scatter_dimension=0, tiled=True)  89 us
    all_gather x1, waiting for transfers between devices, on_device(): all_kv = lax.all_gather(key_value, 'tok', axis=1, tiled=True)  84.6 us
    unnamed x15, waiting for transfers between devices  64.2 us
    reduce_scatter x1, waiting for transfers between devices, on_device(): lax.psum_scatter(bucket_done[2], 'tok', scatter_dimension=1, tiled=True)  42.2 us
    unnamed x2, blocking collectives  37.3 us
  transfers between devices with their start and end apart: 12, of which 8 were waited for; matrix products, arithmetic and copies ran while one was open for 28% of the time, Pallas kernels for 0%

commit v1 on v0

--- a/solution.py
+++ b/solution.py
@@ -1,14 +1,33 @@
+import functools
 import math
 
 import jax
 import jax.numpy as jnp
 from jax import lax
+from jax.experimental import pallas as pl
+from jax.experimental.pallas import tpu as pltpu
 from jax.sharding import PartitionSpec as P
 
 HEADS = 16
-
-
 EPSILON = 1e-06
+LOG2E = 1.4426950408889634
+GELU_K = math.sqrt(2.0 / math.pi)
+GELU_C = 0.044715
+LANES = 128
+BOTH = ("bucket", "tok")
+bf16, f32 = jnp.bfloat16, jnp.float32
+
+
+def dot_nn(a, b):
+    return lax.dot_general(a, b, (((1,), (0,)), ((), ())), preferred_element_type=f32)
+
+
+def dot_nt(a, b):
+    return lax.dot_general(a, b, (((1,), (1,)), ((), ())), preferred_element_type=f32)
+
+
+def dot_tn(a, b):
+    return lax.dot_general(a, b, (((0,), (0,)), ((), ())), preferred_element_type=f32)
 
 
 def step_embedding(timesteps, model_width):
@@ -30,6 +49,643 @@
         - jnp.mean(incoming, axis=-1, keepdims=True)
         - normed * jnp.mean(incoming * normed, axis=-1, keepdims=True)
     )
+
+
+D = 1152
+DC, DZ, TD = D // 8, D // 4, D // 4
+HD = D // HEADS
+HC = HEADS // 2
+WC = D // 2
+FF = 4608
+NF = 3
+FB = FF // 2 // NF
+FZ = FB // 4
+L = 1024
+LH = L // 2
+LB = L // 4
+G1R = 3 * DC
+G2R = 2 * FZ + FZ // 4
+PR = 2 * DC + DC // 3
+QR = 7 * DC + 16
+QA = QR // 2 + 176
+QB_ROWS = QR - QA
+VMEM_LIMIT = 58 * 1024 * 1024
+
+
+def call(kernel, name, out_shape, args, grid=None, in_specs=None, out_specs=None, scratch=(), grid_spec=None,
+         flops=0, nbytes=0):
+    whole = pl.BlockSpec(memory_space=pltpu.VMEM)
+    kwargs = {}
+    if grid_spec is not None:
+        kwargs["grid_spec"] = grid_spec
+    else:
+        kwargs["in_specs"] = in_specs if in_specs is not None else [whole] * len(args)
+        kwargs["out_specs"] = out_specs if out_specs is not None else jax.tree.map(lambda _: whole, out_shape)
+        kwargs["scratch_shapes"] = list(scratch)
+        if grid is not None:
+            kwargs["grid"] = grid
+    return pl.pallas_call(
+        kernel,
+        out_shape=out_shape,
+        compiler_params=pltpu.CompilerParams(vmem_limit_bytes=VMEM_LIMIT),
+        cost_estimate=pl.CostEstimate(flops=int(flops), bytes_accessed=int(nbytes), transcendentals=0),
+        name=name,
+        **kwargs,
+    )(*args)
+
+
+SMEM = pl.BlockSpec(memory_space=pltpu.SMEM)
+
+
+def full(shape):
+    return pl.BlockSpec(shape, lambda *_: (0,) * len(shape))
+
+
+def rows(block, width):
+    return pl.BlockSpec((block, width), lambda i: (i, 0))
+
+
+def prow(block, width):
+    return pl.BlockSpec((block, width), lambda i, s: (i, 0))
+
+
+def prep_kernel(sc, wq, w1, wq_o, w1_o):
+    for core in range(2):
+
+        @pl.when(sc[1] == core)
+        def _():
+            for k in range(12):
+                wq_o[:, DC * k : DC * (k + 1)] = wq[:, DZ * k + DC * core : DZ * k + DC * (core + 1)]
+            for f in range(NF):
+                for k in range(4):
+                    start = 4 * DZ * k + FF // 8 * core + FZ * f
+                    w1_o[f, :, FZ * k : FZ * (k + 1)] = w1[:, start : start + FZ]
+
+
+def qkv_kernel(tok, mod, w, bias, shifted_o, qkv_o):
+    normed, _ = normalize(tok[...].astype(f32))
+    shifted = (normed * (1.0 + mod[1:2, :]) + mod[0:1, :]).astype(bf16)
+    shifted_o[...] = shifted
+    qkv_o[...] = (dot_nn(shifted, w[...]) + bias[...]).astype(bf16)
+
+
+def attn_kernel(step, qkv, head_on, out, qs, ks, vs):
+    scale = LOG2E / math.sqrt(HD)
+    for h in range(HC):
+        qs[...] = qkv[:, h * HD : (h + 1) * HD]
+        ks[...] = qkv[:, WC + h * HD : WC + (h + 1) * HD]
+        vs[...] = qkv[:, 2 * WC + h * HD : 2 * WC + (h + 1) * HD]
+        on = head_on[h]
+
+        def body(i, carry):
+            part = pl.ds(pl.multiple_of(i * step, step), step)
+            s = dot_nt(qs[part, :], ks[...])
+            top = jnp.max(s, axis=1, keepdims=True)
+            p = jnp.exp2((s - top) * scale)
+            total = jnp.sum(p, axis=1, keepdims=True)
+            o = dot_nn(p.astype(bf16), vs[...])
+            out[part, h * HD : (h + 1) * HD] = (o * (on / total)).astype(bf16)
+            return carry
+
+        lax.fori_loop(0, L // step, body, 0)
+
+
+def proj_kernel(mine, other, w_mine, w_other, bias, tok, mod, shifted2_o, attn_o):
+    attn = (
+        dot_nn(mine[...], w_mine[...].reshape(WC, D))
+        + dot_nn(other[...], w_other[...].reshape(WC, D))
+        + bias[...]
+    )
+
+    @pl.when(pl.program_id(0) < 2)
+    def _():
+        attn_o[...] = attn
+
+    resid = tok[...].astype(f32) + mod[2:3, :] * attn
+    normed, _ = normalize(resid)
+    shifted2_o[...] = (normed * (1.0 + mod[4:5, :]) + mod[3:4, :]).astype(bf16)
+
+
+def mlp_kernel(steps, sc, sh2, g, kept, mod, w1, b1, chan, w2,
+               g1k, g1s, g2k, g2s, branch_o, ds2_o, sum1_o, sum2_o, acc1, acc2, t1, t2):
+    i = pl.program_id(0)
+    z, c, y, x = sc[0], sc[1], sc[2], sc[3]
+    w1v = w1[0]
+    w2v = w2[...].reshape(FB, D)
+    db = (g[...].astype(f32) * mod[5:6, :] * kept[...]).astype(bf16)
+    v = dot_nn(sh2[...], w1v) + b1[0]
+    v2 = v * v
+    th = jnp.tanh(GELU_K * v * (1.0 + GELU_C * v2))
+    half = 0.5 * (1.0 + th)
+    on = chan[0]
+    hidden = (v * half * on).astype(bf16)
+    slope = (half + (0.5 * GELU_K) * v * (1.0 - th * th) * (1.0 + (3.0 * GELU_C) * v2)) * on
+    branch_o[...] = dot_nn(hidden, w2v).astype(bf16)
+    d_pre = (dot_nt(db, w2v) * slope).astype(bf16)
+    ds2_o[...] = dot_nt(d_pre, w1v).astype(bf16)
+    p2 = dot_tn(hidden, db)
+    p1 = dot_tn(sh2[...], d_pre)
+    s1 = jnp.sum(d_pre.astype(f32), axis=0, keepdims=True)
+    s2 = jnp.sum(db.astype(f32), axis=0, keepdims=True)
+
+    @pl.when(i == 0)
+    def _():
+        acc1[...] = p1
+        acc2[...] = p2
+        sum1_o[...] = s1
+        sum2_o[...] = s2
+
+    @pl.when(i > 0)
+    def _():
+        acc1[...] += p1
+        acc2[...] += p2
+        sum1_o[...] += s1
+        sum2_o[...] += s2
+
+    @pl.when(i == steps - 1)
+    def _():
+        for t in range(4):
+            t1[t] = acc1[:, FZ * t : FZ * (t + 1)].astype(bf16)
+            t2[t] = acc2[:, TD * t : TD * (t + 1)].astype(bf16)
+        for rz in range(4):
+            zz = rz ^ z
+            for ry in range(2):
+                for rx in range(2):
+                    tt = (ry ^ y) * 2 + (rx ^ x)
+                    o1 = (g1k, g1s)[rx]
+                    tails = []
+                    for rc in range(2):
+                        start = pl.multiple_of(zz * DZ + (rc ^ c) * DC, 16)
+                        part = t1[tt, pl.ds(start, DC), :]
+                        o1[ry, rz, rc * DC : (rc + 1) * DC, :] = part[:, :LANES]
+                        tails.append(part[:, LANES:])
+                    o1[ry, rz, 2 * DC : 3 * DC, :] = jnp.concatenate(tails, axis=1)
+                    o2 = (g2k, g2s)[ry]
+                    part = t2[tt, pl.ds(pl.multiple_of(zz * FZ, 16), FZ), :]
+                    o2[rx, rz, :FZ, :] = part[:, :LANES]
+                    o2[rx, rz, FZ : 2 * FZ, :] = part[:, LANES : 2 * LANES]
+                    q = FZ // 4
+                    o2[rx, rz, 2 * FZ :, :] = jnp.concatenate(
+                        [part[q * k : q * (k + 1), 2 * LANES :] for k in range(4)], axis=1
+                    )
+
+
+def mid_kernel(ds_a, ds_b, ds_c, ds_r, br_a, br_b, br_c, br_r, attn, tok, g, kept, mod, bias2,
+               d_resid_o, d_attn_o, out_o, sums_o):
+    i = pl.program_id(0)
+    tokf, gf, at = tok[...].astype(f32), g[...].astype(f32), attn[...]
+    resid = tokf + mod[2:3, :] * at
+    normed2, inverse2 = normalize(resid)
+    ds2 = ds_a[...].astype(f32) + ds_b[...].astype(f32) + ds_c[...].astype(f32) + ds_r[...].astype(f32)
+    branch = (
+        br_a[...].astype(f32) + br_b[...].astype(f32) + br_c[...].astype(f32) + br_r[...].astype(f32) + bias2[...]
+    )
+    kb = kept[...] * branch
+    out_o[...] = (resid + mod[5:6, :] * kb).astype(bf16)
+    d_resid = gf + normalize_back(ds2 * (1.0 + mod[4:5, :]), normed2, inverse2)
+    d_resid_o[...] = d_resid
+    d_attn_o[...] = (mod[2:3, :] * d_resid).astype(bf16)
+    parts = [at * d_resid, ds2, ds2 * normed2, kb * gf]
+    sums = [jnp.sum(p, axis=0, keepdims=True) for p in parts]
+    sums = jnp.concatenate(sums + [jnp.zeros((4, D), f32)], axis=0)
+
+    @pl.when(i == 0)
+    def _():
+        sums_o[...] = sums
+
+    @pl.when(i > 0)
+    def _():
+        sums_o[...] += sums
+
+
+def heads_kernel(sc, da_mine, da_other, mixed, w, dh_o, pk, ps, sum_o, t1):
+    z, c, y, x = sc[0], sc[1], sc[2], sc[3]
+    wv = w[...].reshape(WC, D)
+    dh_o[:LH, :] = dot_nt(da_mine[...], wv).astype(bf16)
+    dh_o[LH:, :] = dot_nt(da_other[...], wv).astype(bf16)
+    grad = dot_tn(mixed[:LH, :], da_mine[...]) + dot_tn(mixed[LH:, :], da_other[...])
+    sum_o[...] = jnp.sum(da_mine[...].astype(f32), axis=0, keepdims=True) + jnp.sum(
+        da_other[...].astype(f32), axis=0, keepdims=True
+    )
+    for t in range(4):
+        t1[t] = grad[:, TD * t : TD * (t + 1)].astype(bf16)
+    for rz in range(4):
+        zz = rz ^ z
+        for ry in range(2):
+            for rx in range(2):
+                tt = (ry ^ y) * 2 + (rx ^ x)
+                o = (pk, ps)[ry]
+                part = t1[tt, pl.ds(pl.multiple_of(zz * DC, 16), DC), :]
+                o[rx, rz, :DC, :] = part[:, :LANES]
+                o[rx, rz, DC : 2 * DC, :] = part[:, LANES : 2 * LANES]
+                q = DC // 3
+                tails = [part[q * k : q * (k + 1), 2 * LANES :] for k in range(3)]
+                tails.append(jnp.zeros((q, 32), bf16))
+                o[rx, rz, 2 * DC :, :] = jnp.concatenate(tails, axis=1)
+
+
+def attn_back_kernel(step, qkv, dh, head_on, out, qs, ks, vs, dos, dq, dk, dv):
+    scale = LOG2E / math.sqrt(HD)
+    for h in range(HC):
+        qs[...] = qkv[:, h * HD : (h + 1) * HD]
+        ks[...] = qkv[:, WC + h * HD : WC + (h + 1) * HD]
+        vs[...] = qkv[:, 2 * WC + h * HD : 2 * WC + (h + 1) * HD]
+        dos[...] = (dh[:, h * HD : (h + 1) * HD].astype(f32) * head_on[h]).astype(bf16)
+        dk[...] = jnp.zeros_like(dk)
+        dv[...] = jnp.zeros_like(dv)
+
+        def body(i, carry):
+            part = pl.ds(pl.multiple_of(i * step, step), step)
+            q, do = qs[part, :], dos[part, :]
+            s = dot_nt(ks[...], q)
+            top = jnp.max(s, axis=0, keepdims=True)
+            p = jnp.exp2((s - top) * scale)
+            p = p * (1.0 / jnp.sum(p, axis=0, keepdims=True))
+            dp = dot_nt(vs[...], do)
+            row_dot = jnp.sum(p * dp, axis=0, keepdims=True)
+            ds = (p * (dp - row_dot)).astype(bf16)
+            dv[...] += dot_nn(p.astype(bf16), do)
+            dk[...] += dot_nn(ds, q)
+            dq[part, :] = dot_tn(ds, ks[...])
+            return carry
+
+        lax.fori_loop(0, L // step, body, 0)
+        out[:, h * HD : (h + 1) * HD] = (dq[...] * (1.0 / math.sqrt(HD))).astype(bf16)
+        out[:, WC + h * HD : WC + (h + 1) * HD] = (dk[...] * (1.0 / math.sqrt(HD))).astype(bf16)
+        out[:, 2 * WC + h * HD : 2 * WC + (h + 1) * HD] = dv[...].astype(bf16)
+
+
+def qkv_grad_kernel(sc, shifted, dqkv, extra, ak, as_, bk, bs, t1):
+    z, c, y, x = sc[0], sc[1], sc[2], sc[3]
+    for k in range(4):
+        grad = dot_tn(shifted[:, DZ * k : DZ * (k + 1)], dqkv[...])
+        for t in range(4):
+            t1[t, DZ * k : DZ * (k + 1), :] = grad[:, 3 * DC * t : 3 * DC * (t + 1)].astype(bf16)
+    ones = jnp.ones((16, L), bf16)
+    sums = dot_nn(ones, dqkv[...])[0:1, :]
+    for zs in range(4):
+        for ts in range(4):
+            piece = DC * zs + DC // 4 * ts
+            qsum = sums[:, piece : piece + DC // 4]
+            vsum = sums[:, 2 * WC + piece : 2 * WC + piece + DC // 4]
+            row1 = jnp.concatenate([jnp.zeros((1, 88), f32), qsum, jnp.zeros((1, 4), f32)], axis=1)
+            row2 = jnp.concatenate([vsum, jnp.zeros((1, LANES - DC // 4), f32)], axis=1)
+            add = jnp.concatenate([jnp.zeros((1, LANES), f32), row1, row2, jnp.zeros((13, LANES), f32)], axis=0)
+            rz, ry, rx = zs ^ z, (ts // 2) ^ y, (ts % 2) ^ x
+            block = (extra[zs, ts] + add).astype(bf16)
+
+            @pl.when(ry == 0)
+            def _():
+                bk[rx, rz, QB_ROWS - 16 :, :] = block
+
+            @pl.when(ry == 1)
+            def _():
+                bs[rx, rz, QB_ROWS - 16 :, :] = block
+
+    for rz in range(4):
+        zz = rz ^ z
+        for ry in range(2):
+            for rx in range(2):
+                tt = (ry ^ y) * 2 + (rx ^ x)
+                a, b = (ak, as_)[rx], (bk, bs)[ry]
+                parts = [
+                    t1[tt, pl.ds(pl.multiple_of(zz * DZ + (rc ^ c) * DC, 16), DC), :] for rc in range(2)
+                ]
+                for rc in range(2):
+                    for k in range(2):
+                        first = (2 * k + rc) * DC
+                        a[ry, rz, first : first + DC, :] = parts[rc][:, LANES * k : LANES * (k + 1)]
+                third = [part[:, 2 * LANES : 3 * LANES] for part in parts]
+                cut = QA - 4 * DC
+                a[ry, rz, 4 * DC : QA, :] = third[0][:cut, :]
+                b[rx, rz, : DC - cut, :] = third[0][cut:, :]
+                b[rx, rz, DC - cut : 2 * DC - cut, :] = third[1]
+                gap = jnp.zeros((DC, 16), bf16)
+                b[rx, rz, 2 * DC - cut : 3 * DC - cut, :] = jnp.concatenate(
+                    [parts[0][:, 3 * LANES :], gap, parts[1][:, 3 * LANES :], gap], axis=1
+                )
+
+
+def back_kernel(dqkv, w, out):
+    out[...] = dot_nt(dqkv[...], w[...]).astype(bf16)
+
+
+def last_kernel(mine, other, d_resid, tok, mod, grad_o, sums_o):
+    i = pl.program_id(0)
+    d_shifted = mine[...].astype(f32) + other[...].astype(f32)
+    normed, inverse = normalize(tok[...].astype(f32))
+    grad = d_resid[...] + normalize_back(d_shifted * (1.0 + mod[1:2, :]), normed, inverse)
+    grad_o[...] = grad.astype(bf16)
+    sums = [jnp.sum(p, axis=0, keepdims=True) for p in (d_shifted, d_shifted * normed)]
+    sums = jnp.concatenate(sums + [jnp.zeros((6, D), f32)], axis=0)
+
+    @pl.when(i == 0)
+    def _():
+        sums_o[...] = sums
+
+    @pl.when(i > 0)
+    def _():
+        sums_o[...] += sums
+
+
+def finish_kernel(sc, f0, f1, f2, fp, fq, s0, s1, s2, sq, gq_o, gp_o, g1_o, g2_o):
+    own = fq[...]
+    sib = sq[...].astype(f32)
+    mine = jnp.concatenate(
+        [own[0:DC], own[2 * DC : 3 * DC], own[4 * DC : 5 * DC], own[6 * DC : 7 * DC, : DC // 3]], axis=1
+    )
+    theirs = jnp.concatenate(
+        [sib[DC : 2 * DC], sib[3 * DC : 4 * DC], sib[5 * DC : 6 * DC], sib[6 * DC : 7 * DC, 64 : 64 + DC // 3]],
+        axis=1,
+    )
+    first = [f[...] for f in (f0, f1, f2)]
+    second = [s[...].astype(f32) for s in (s0, s1, s2)]
+    for core in range(2):
+
+        @pl.when(sc[1] == core)
+        def _():
+            for k in range(3):
+                a, b = DZ * k + DC * core, DZ * k + DC * (1 - core)
+                gq_o[:, a : a + DC] = mine[:, DC * k : DC * (k + 1)]
+                gq_o[:, b : b + DC] = theirs[:, DC * k : DC * (k + 1)]
+            for f in range(NF):
+                a, b = FF // 8 * core + FZ * f, FF // 8 * (1 - core) + FZ * f
+                g1_o[:, a : a + FZ] = jnp.concatenate(
+                    [first[f][:DC], first[f][2 * DC : 3 * DC, : FZ - LANES]], axis=1
+                )
+                g1_o[:, b : b + FZ] = jnp.concatenate(
+                    [second[f][DC : 2 * DC], second[f][2 * DC : 3 * DC, FZ - LANES :]], axis=1
+                )
+
+    for f in range(NF):
+        part = first[f][G1R:]
+        tail = part[2 * FZ :]
+        tail = jnp.concatenate([tail[:, 32 * k : 32 * (k + 1)] for k in range(4)], axis=0)
+        g2_o[FZ * f : FZ * (f + 1), :] = jnp.concatenate([part[:FZ], part[FZ : 2 * FZ], tail], axis=1)
+    part = fp[...]
+    tail = part[2 * DC :]
+    tail = jnp.concatenate([tail[:, 32 * k : 32 * (k + 1)] for k in range(3)], axis=0)
+    gp_o[...] = jnp.concatenate([part[:DC], part[DC : 2 * DC], tail], axis=1)
+
+
+def make_perm(move):
+    pairs = []
+    for b in range(8):
+        for t in range(4):
+            z, c, y, x = move(b // 2, b % 2, t // 2, t % 2)
+            pairs.append((b * 4 + t, (z * 2 + c) * 4 + y * 2 + x))
+    return pairs
+
+
+PERM_X = make_perm(lambda z, c, y, x: (z, c, y, 1 - x))
+PERM_Y = make_perm(lambda z, c, y, x: (z, c, 1 - y, x))
+PERM_XY = make_perm(lambda z, c, y, x: (z, c, 1 - y, 1 - x))
+PERM_C = make_perm(lambda z, c, y, x: (z, 1 - c, y, x))
+PERM_Z = [None] + [make_perm(lambda z, c, y, x, j=j: (z ^ j, c, y, x)) for j in (1, 2, 3)]
+PERM_T = [make_perm(lambda z, c, y, x, j=j: (z, y, c, x ^ j)) for j in (0, 1)]
+
+
+def send(value, perm):
+    return lax.ppermute(value, BOTH, perm)
+
+
+def reduce_streams(streams):
+    halves = []
+    for kept, sent, first, second in streams:
+        got = send(sent, first)
+        onward = (kept[1].astype(f32) + got[1].astype(f32)).astype(bf16)
+        halves.append((kept[0], got[0], send(onward, second)))
+    sums = [[a[k].astype(f32) + b[k].astype(f32) + c[k].astype(f32) for a, b, c in halves] for k in range(4)]
+    total = jnp.concatenate(sums[0], axis=0)
+    for k in (1, 2, 3):
+        total = total + send(jnp.concatenate([s.astype(bf16) for s in sums[k]], axis=0), PERM_Z[k]).astype(f32)
+    return total
+
+
+def one_item_per_chip(
+    tokens, cotangent, timesteps, bucket_ids, head_masks, channel_masks, skip_rows,
+    w_qkv, q_bias, v_bias, w_proj, proj_bias, w_fc1, fc1_bias, w_fc2, fc2_bias, ada_weight, ada_bias,
+):
+    b, t = lax.axis_index("bucket"), lax.axis_index("tok")
+    z, c, y, x = b // 2, b % 2, t // 2, t % 2
+    sc = jnp.stack([z, c, y, x]).astype(jnp.int32)
+    sds = jax.ShapeDtypeStruct
+
+    def gather(values):
+        here = lax.dynamic_index_in_dim(values, x, 0, keepdims=False)
+        there = lax.dynamic_index_in_dim(values, 1 - x, 0, keepdims=False)
+        mine = jnp.concatenate([send(here, PERM_T[0]), send(there, PERM_T[1])], axis=0)
+        return jnp.concatenate([mine, send(mine, PERM_C)], axis=0)
+
+    def scatter(values):
+        here, there = send(values[:LB], PERM_T[0]), send(values[LB:], PERM_T[1])
+        return jnp.where(x == 0, jnp.stack([here, there]), jnp.stack([there, here]))
+
+    tok = gather(tokens)
+    ints = jnp.concatenate([timesteps, bucket_ids, jnp.zeros((13,), jnp.int32), skip_rows.reshape(-1)])
+    ints_other = send(ints, PERM_C)
+    every_step = lax.all_gather(timesteps, "bucket", axis=0, tiled=True)
+    g_all = gather(cotangent)
+
+    steps4 = jnp.where(c == 0, jnp.concatenate([ints[:2], ints_other[:2]]), jnp.concatenate([ints_other[:2], ints[:2]]))
+    group_ints = jnp.where(c == y, ints, ints_other)
+    bucket = group_ints[2]
+    skip = lax.dynamic_slice_in_dim(group_ints, 16 + skip_rows.shape[1] * x, skip_rows.shape[1], 0)
+    blocks = jnp.stack([2 * c + x, 2 * c + 1 - x, 2 * (1 - c) + x, 2 * (1 - c) + 1 - x])
+    positions = (blocks[:, None] * LB + jnp.arange(LB)[None, :]).reshape(L, 1)
+    kept = 1.0 - jnp.any(positions == skip[None, :], axis=1, keepdims=True).astype(f32)
+    kept = kept.reshape(L, 1)
+
+    condition = jax.nn.silu(step_embedding(steps4, D)).astype(bf16)
+    mod4 = jnp.dot(condition, ada_weight, preferred_element_type=f32) + ada_bias.astype(f32)
+    pick = lambda k: lax.dynamic_index_in_dim(mod4, t ^ k, 0, keepdims=False)
+    shares = jnp.stack([pick(0), send(pick(1), PERM_X), send(pick(2), PERM_Y), send(pick(3), PERM_XY)])
+    mod = jnp.take(shares, jnp.arange(4) ^ t, axis=0).reshape(6, D)
+    mod = jnp.concatenate([mod, jnp.zeros((2, D), f32)], axis=0)
+
+    def core_half(v, *dims):
+        return lax.dynamic_index_in_dim(v.reshape(dims), c, 1, keepdims=False)
+
+    head_on = core_half(lax.dynamic_index_in_dim(head_masks, bucket, 0, keepdims=False).astype(f32), 4, 2, 2).reshape(HC)
+    group_on = lax.dynamic_index_in_dim(channel_masks, bucket, 0, keepdims=False).astype(f32)
+    channel_on = jnp.repeat(group_on, FF // group_on.shape[0])
+
+    def hidden_order(v):
+        return core_half(v, 4, 2, NF, FZ).transpose(1, 0, 2).reshape(NF, 1, FB)
+
+    chan = hidden_order(channel_on)
+    b1 = hidden_order(fc1_bias.astype(f32))
+    qkv_bias = jnp.concatenate([q_bias, jnp.zeros_like(q_bias), v_bias]).astype(f32)
+    qkv_bias = core_half(qkv_bias, 12, 2, DC).reshape(1, 3 * WC)
+
+    wq, w1 = call(
+        prep_kernel, "prep",
+        (sds((D, 3 * WC), bf16), sds((NF, D, FB), bf16)), (sc, w_qkv, w_fc1),
+        grid=(8,),
+        in_specs=[SMEM, rows(DC, 3 * D), rows(DC, FF)],
+        out_specs=(rows(DC, 3 * WC), pl.BlockSpec((NF, DC, FB), lambda i: (0, i, 0))),
+        nbytes=28e6,
+    )
+    w2 = w_fc2.reshape(4, 2, NF, FZ, D)
+    wp = w_proj.reshape(4, 2, DC, D)
+    wp_mine = lax.dynamic_index_in_dim(wp, c, 1, keepdims=False).reshape(WC, D)
+    wp_other = lax.dynamic_index_in_dim(wp, 1 - c, 1, keepdims=False).reshape(WC, D)
+
+    shifted, qkv = call(
+        qkv_kernel, "ln_qkv",
+        (sds((L, D), bf16), sds((L, 3 * WC), bf16)), (tok, mod, wq, qkv_bias),
+        grid=(4,),
+        in_specs=[rows(LB, D), full((8, D)), full((D, 3 * WC)), full((1, 3 * WC))],
+        out_specs=(rows(LB, D), rows(LB, 3 * WC)),
+        flops=2 * L * D * 3 * WC, nbytes=12e6,
+    )
+    mixed = call(
+        functools.partial(attn_kernel, 256), "attn",
+        sds((L, WC), bf16), (qkv, head_on),
+        in_specs=[pl.BlockSpec(memory_space=pltpu.VMEM), SMEM],
+        scratch=[pltpu.VMEM((L, HD), bf16)] * 3,
+        flops=16e9, nbytes=5e6,
+    )
+    mixed_other = send(mixed, PERM_C)
+    shifted2, attn = call(
+        proj_kernel, "proj_ln",
+        (sds((L, D), bf16), sds((LH, D), f32)),
+        (mixed, mixed_other, wp_mine, wp_other, proj_bias.astype(f32).reshape(1, D), tok, mod),
+        grid=(4,),
+        in_specs=[rows(LB, WC), pl.BlockSpec((LB, WC), lambda i: ((i + 2) % 4, 0)), full((WC, D)), full((WC, D)),
+                  full((1, D)), rows(LB, D), full((8, D))],
+        out_specs=(rows(LB, D), pl.BlockSpec((LB, D), lambda i: (jnp.minimum(i, 1), 0))),
+        flops=2 * L * D * D, nbytes=12e6,
+    )
+
+    mlp_steps = 2
+    block = L // mlp_steps
+    finals, branches, ds2s, sums1 = [], [], [], []
+    for f in range(NF):
+        slot1, slot2 = sds((2, 4, G1R, LANES), bf16), sds((2, 4, G2R, LANES), bf16)
+        g1k, g1s, g2k, g2s, branch_f, ds2_f, sum1, sum2 = call(
+            functools.partial(mlp_kernel, mlp_steps), f"mlp{f}",
+            (slot1, slot1, slot2, slot2, sds((L, D), bf16), sds((L, D), bf16), sds((1, FB), f32), sds((1, D), f32)),
+            (sc, shifted2, g_all, kept, mod, w1, b1, chan, w2),
+            grid_spec=pltpu.PrefetchScalarGridSpec(
+                num_scalar_prefetch=1,
+                grid=(mlp_steps,),
+                in_specs=[
+                    prow(block, D), prow(block, D), prow(block, 1), full((8, D)),
+                    pl.BlockSpec((1, D, FB), lambda i, s, f=f: (f, 0, 0)),
+                    pl.BlockSpec((1, 1, FB), lambda i, s, f=f: (f, 0, 0)),
+                    pl.BlockSpec((1, 1, FB), lambda i, s, f=f: (f, 0, 0)),
+                    pl.BlockSpec((4, 1, 1, FZ, D), lambda i, s, f=f: (0, s[1], f, 0, 0)),
+                ],
+                out_specs=(full(slot1.shape), full(slot1.shape), full(slot2.shape), full(slot2.shape),
+                           prow(block, D), prow(block, D), full((1, FB)), full((1, D))),
+                scratch_shapes=[pltpu.VMEM((D, FB), f32), pltpu.VMEM((FB, D), f32),
+                                pltpu.VMEM((4, D, FZ), bf16), pltpu.VMEM((4, FB, TD), bf16)],
+            ),
+            flops=12 * L * D * FB, nbytes=20e6,
+        )
+        finals.append(reduce_streams([(g1k, g1s, PERM_X, PERM_Y), (g2k, g2s, PERM_Y, PERM_X)]))
+        branches.append(branch_f)
+        ds2s.append(ds2_f)
+        sums1.append(sum1)
+
+    def far_half(parts):
+        return sum(p[LH:].astype(f32) for p in parts).astype(bf16)
+
+    ds2_r = send(far_half(ds2s), PERM_C)
+    branch_r = send(far_half(branches), PERM_C)
+    row = rows(LB, D)
+    d_resid, d_attn, out_rows, sums_mid = call(
+        mid_kernel, "mid",
+        (sds((LH, D), f32), sds((LH, D), bf16), sds((LH, D), bf16), sds((8, D), f32)),
+        (*ds2s, ds2_r, *branches, branch_r, attn, tok, g_all, kept, mod, fc2_bias.astype(f32).reshape(1, D)),
+        grid=(2,),
+        in_specs=[row] * 8 + [row, row, row, rows(LB, 1), full((8, D)), full((1, D))],
+        out_specs=(row, row, row, full((8, D))),
+        nbytes=20e6,
+    )
+    output = scatter(out_rows)
+    d_attn_other = send(d_attn, PERM_C)
+    slotp = sds((2, 4, PR, LANES), bf16)
+    dh, pk, ps, sum_attn = call(
+        heads_kernel, "heads_back",
+        (sds((L, WC), bf16), slotp, slotp, sds((1, D), f32)),
+        (sc, d_attn, d_attn_other, mixed, wp_mine),
+        in_specs=[SMEM] + [pl.BlockSpec(memory_space=pltpu.VMEM)] * 4,
+        scratch=[pltpu.VMEM((4, WC, TD), bf16)],
+        flops=4 * L * D * WC, nbytes=10e6,
+    )
+    final_p = reduce_streams([(pk, ps, PERM_Y, PERM_X)])
+    dqkv = call(
+        functools.partial(attn_back_kernel, 512), "attn_back",
+        sds((L, 3 * WC), bf16), (qkv, dh, head_on),
+        in_specs=[pl.BlockSpec(memory_space=pltpu.VMEM)] * 2 + [SMEM],
+        scratch=[pltpu.VMEM((L, HD), bf16)] * 4 + [pltpu.VMEM((L, HD), f32)] * 3,
+        flops=30e9, nbytes=9e6,
+    )
+    sum_fc1 = jnp.concatenate(sums1, axis=0).reshape(NF, 4, FZ).transpose(1, 0, 2).reshape(4, 4, FF // 32)
+    own = lambda v: core_half(v, 4, 2, 4, D // 32)
+    sum_fc2, sum_attn = own(sum2), own(sum_attn)
+    line = jnp.concatenate(
+        [sum_fc1, sum_fc2, sum_attn, jnp.zeros((4, 4, 3 * LANES - FF // 32 - D // 16), f32)], axis=2
+    ).reshape(4, 4, 3, LANES)
+    extra = jnp.concatenate([line, jnp.zeros((4, 4, 13, LANES), f32)], axis=2)
+    slota, slotb = sds((2, 4, QA, LANES), bf16), sds((2, 4, QB_ROWS, LANES), bf16)
+    ak, as_, bk, bs = call(
+        qkv_grad_kernel, "qkv_grad",
+        (slota, slota, slotb, slotb), (sc, shifted, dqkv, extra),
+        in_specs=[SMEM] + [pl.BlockSpec(memory_space=pltpu.VMEM)] * 3,
+        scratch=[pltpu.VMEM((4, D, 3 * DC), bf16)],
+        flops=2 * L * D * 3 * WC, nbytes=12e6,
+    )
+    final_q = reduce_streams([(ak, as_, PERM_X, PERM_Y), (bk, bs, PERM_Y, PERM_X)])
+    d_shifted = call(
+        back_kernel, "qkv_back",
+        sds((L, D), bf16), (dqkv, wq),
+        grid=(2,),
+        in_specs=[rows(LH, 3 * WC), full((D, 3 * WC))],
+        out_specs=rows(LH, D),
+        flops=2 * L * D * 3 * WC, nbytes=12e6,
+    )
+    d_shifted_r = send(d_shifted[LH:], PERM_C)
+    grad_rows, sums_last = call(
+        last_kernel, "last",
+        (sds((LH, D), bf16), sds((8, D), f32)),
+        (d_shifted, d_shifted_r, d_resid, tok, mod),
+        grid=(2,),
+        in_specs=[row, row, row, row, full((8, D))],
+        out_specs=(row, full((8, D))),
+        nbytes=10e6,
+    )
+    grad_tokens = scatter(grad_rows).astype(f32)
+
+    mine = jnp.concatenate([sums_last[:2], sums_mid[:4]], axis=0).reshape(1, 6 * D)
+    every = lax.all_gather(mine, BOTH, axis=0, tiled=True)
+    every = every.reshape(4, 2, 4, 6 * D).sum(axis=1).reshape(16, 6 * D)
+    ada_cols = ada_weight.shape[1]
+    cond_all = jax.nn.silu(step_embedding(every_step, D)).astype(bf16).astype(f32)
+    cond_rows = lax.dynamic_slice_in_dim(cond_all, b * DC, DC, 1)
+    columns = lax.dynamic_slice_in_dim(every, t * ada_cols, ada_cols, 1)
+    grad_ada_weight = lax.dot_general(
+        cond_rows, columns, (((0,), (0,)), ((), ())), precision=lax.Precision.HIGHEST
+    )
+    bias_cols = 6 * D // 8
+    grad_ada_bias = jnp.sum(lax.dynamic_slice_in_dim(every, b * bias_cols, bias_cols, 1), axis=0)
+
+    other = send(jnp.concatenate([f[:G1R].astype(bf16) for f in finals] + [final_q[: 7 * DC].astype(bf16)], axis=0), PERM_C)
+    others = [other[G1R * f : G1R * (f + 1)] for f in range(NF)]
+    gq, gp, g1, g2 = call(
+        finish_kernel, "finish",
+        (sds((DC, 3 * TD), f32), sds((DC, TD), f32), sds((DC, FF // 4), f32), sds((FF // 8, TD), f32)),
+        (sc, *finals, final_p, final_q, *others, other[NF * G1R :]),
+        in_specs=[SMEM] + [pl.BlockSpec(memory_space=pltpu.VMEM)] * 9,
+        nbytes=6e6,
+    )
+    line = final_q[7 * DC :].reshape(-1)
+    n1, n = FF // 32, D // 32
+    b_fc1, b_fc2, b_proj = line[:n1], line[n1 : n1 + n], line[n1 + n : n1 + 2 * n]
+    b_q, b_v = line[n1 + 2 * n : n1 + 3 * n], line[2 * LANES : 2 * LANES + n]
+    return (output, grad_tokens, gq, b_q, b_v, gp, b_proj, g1, b_fc1, g2, b_fc2, grad_ada_weight, grad_ada_bias)
 
 
 def gelu_tanh(values):
@@ -343,8 +999,9 @@
 
 
 def solution(mesh):
+    planned = mesh.shape["tok"] == 4 and mesh.shape["bucket"] == 8
     return jax.shard_map(
-        on_device,
+        one_item_per_chip if planned else on_device,
         mesh=mesh,
         in_specs=(
             P("bucket", "tok", None),

time: 1290 us -> 636 us (0.49)
  waiting for transfers between devices: 791 us -> 122 us
  matrix products: 271 us -> 2.84 us
  Pallas kernels: 0 us -> 229 us
  starting transfers between devices: 0.96 us -> 85.9 us
  local copies, waits for them, and re-layouts: 81.8 us -> 49.7 us
  between operations: 19.6 us -> 5.23 us
    reduce_scatter x6 -> x0, waiting for transfers between devices: 643 us -> none  [the longest x1 211 us: on_device(): lax.psum_scatter(grad_w_fc2, 'bucket', scatter_dimension=0, tiled=True)]
    dot_general x21 -> x2, matrix products: 271 us -> 2.84 us  [the longest x1 1.69 us: one_item_per_chip(): lax.dot_general(cond_rows, columns, (((0,), (0,)), ((), ())), precision=l...]
    pallas_call x0 -> x14, Pallas kernels: none -> 229 us  [call(): pl.pallas_call(kernel, out_shape=out_shape, compiler_params=pltpu.Compile...]
    ppermute x0 -> x53, waiting for transfers between devices: none -> 122 us  [send(): return lax.ppermute(value, BOTH, perm)]
    ppermute x0 -> x53, starting transfers between devices: none -> 85.9 us  [send(): return lax.ppermute(value, BOTH, perm)]
    all_gather x3 -> x0, waiting for transfers between devices: 84.6 us -> none  [the longest x1 84.6 us: on_device(): all_kv = lax.all_gather(key_value, 'tok', axis=1, tiled=True)]
    unnamed x15 -> x0, waiting for transfers between devices: 64.2 us -> none
    all_gather x3 -> x1, blocking collectives: 25.7 us -> 76.9 us  [one_item_per_chip(): every = lax.all_gather(mine, BOTH, axis=0, tiled=True)]
  transfers between devices with their start and end apart: 12 -> 53, of which waited for: 8 -> 13; matrix products, arithmetic and copies ran while one was open for 28% -> 14% of each run, Pallas kernels for 0% -> 23%
where the time goes in v1:
time: 636 us; the launch traced here: 629 us
  Pallas kernels  229 us (36%)
  waiting for transfers between devices  122 us (19%)
  blocking collectives  86 us (14%)
  starting transfers between devices  85.9 us (14%)
  local copies, waits for them, and re-layouts  49.7 us (8%)
  other arithmetic  48.5 us (8%)
    pallas_call x14, Pallas kernels, call(): pl.pallas_call(kernel, out_shape=out_shape, compiler_params=pltpu.Compile...  229 us
    ppermute x53, waiting for transfers between devices, send(): return lax.ppermute(value, BOTH, perm)  122 us
    ppermute x53, starting transfers between devices, send(): return lax.ppermute(value, BOTH, perm)  85.9 us
    all_gather x1, blocking collectives, one_item_per_chip(): every = lax.all_gather(mine, BOTH, axis=0, tiled=True)  76.9 us
    unnamed x139, local copies, waits for them, and re-layouts  12.7 us
  transfers between devices with their start and end apart: 53, of which 13 were waited for; matrix products, arithmetic and copies ran while one was open for 14% of the time, Pallas kernels for 23%

profile of v1, /device:TPU:0, one launch (start us, length us, event | category | flops | bytes accessed | tf_op | source)
XLA Modules:
  0.0 629.4 jit_solution(561417632582344357)
XLA Ops:
  15.6 9.2 %all-reduce.2 = s32[16]{0:T(128)S(1)} all-reduce(s32[16]{0:T(128)S(1)} %dynamic-update-slice), channel_id=1, replica_groups=mesh['bucket'=8,'tok'=4] {'bucket'}, use_global_device_ids=true, to_apply=%add.2 | all-reduce | flops 16 | bytes 128
  34.4 12.9 %prep.1 = (bf16[1152,1728]{1,0:T(8,128)(2,1)}, bf16[3,1152,768]{2,1,0:T(8,128)(2,1)}) custom-call(s32[4]{0:T(128)} %pad_add_fusion.1.sc, bf16[1152,3456]{1,0:T(8,128)(2,1)} %wq.1, bf16[1152,4608]{1,0:T(8,128)(2,1)} %w1.1), custom_call_target="tpu_custom_call" | custom-call | bytes 28000000 | tf_op jit(solution)/shard_map/prep/pallas_call | solution.py:87
  64.9 9.3 %collective-permute-done.9 = bf16[256,1152]{1,0:T(8,128)(2,1)S(1)} collective-permute-done((bf16[256,1152]{1,0:T(8,128)(2,1)}, bf16[256,1152]{1,0:T(8,128)(2,1)S(1)}, u32[]{:S(2)}, u32[]{:S(2)}) %collective-permute-start.9) | collective-permute-done | bytes 589856 | tf_op jit(solution)/shard_map/ppermute | solution.py:449
  79.2 10.2 %ln_qkv.1 = (bf16[1024,1152]{1,0:T(8,128)(2,1)}, bf16[1024,1728]{1,0:T(8,128)(2,1)}) custom-call(bf16[1024,1152]{1,0:T(8,128)(2,1)} %copy-done, f32[8,1152]{1,0:T(8,128)} %concatenate.121.mod, bf16[1152,1728]{1,0:T(8,128)(2,1)} %get-tuple-element.59.w, f32[1,1728]{1,0:T(1,128)} %reshape.597.bias), custom_call_target="tpu_custom_call" | custom-call | flops 4076863488 | bytes 12000000 | tf_op jit(solution)/shard_map/ln_qkv/pallas_call | solution.py:87
  89.4 29.1 %attn.1.mine.mixed = bf16[1024,576]{1,0:T(8,128)(2,1)} custom-call(bf16[1024,1728]{1,0:T(8,128)(2,1)} %get-tuple-element.60.qkv, f32[8]{0:T(128)} %reshape.598.head_on), custom_call_target="tpu_custom_call" | custom-call | flops 16000000000 | bytes 5000000 | tf_op jit(solution)/shard_map/attn/pallas_call | solution.py:87
  128.0 10.0 %proj_ln.1 = (bf16[1024,1152]{1,0:T(8,128)(2,1)}, f32[512,1152]{1,0:T(8,128)}) custom-call(bf16[1024,576]{1,0:T(8,128)(2,1)} %attn.1.mine.mixed, bf16[1024,576]{1,0:T(8,128)(2,1)} %copy.71.other, bf16[576,1152]{1,0:T(8,128)(2,1)} %bitcast.333, bf16[576,1152]{1,0:T(8,128)(2,1)} %bitcast.335, f32[1,1152]{1,0:T(1,128)} %reshape.621.bias, ...), custom_call_target="tpu_custom_call" | custom-call | flops 2717908992 | bytes 12000000 | tf_op jit(solution)/shard_map/proj_ln/pallas_call | solution.py:87
  138.0 23.4 %mlp2.1 = (bf16[2,4,432,128]{3,2,1,0:T(8,128)(2,1)}, bf16[2,4,432,128]{3,2,1,0:T(8,128)(2,1)}, bf16[2,4,432,128]{3,2,1,0:T(8,128)(2,1)}, bf16[2,4,432,128]{3,2,1...) custom-call(s32[4]{0:T(128)} %pad_add_fusion.1.sc, ...), custom_call_target="tpu_custom_call" | custom-call | flops 10871635968 | bytes 20000000 | tf_op jit(solution)/shard_map/mlp2/pallas_call | solution.py:87
  161.4 23.6 %mlp1.1 = (bf16[2,4,432,128]{3,2,1,0:T(8,128)(2,1)}, bf16[2,4,432,128]{3,2,1,0:T(8,128)(2,1)}, bf16[2,4,432,128]{3,2,1,0:T(8,128)(2,1)}, bf16[2,4,432,128]{3,2,1...) custom-call(s32[4]{0:T(128)} %pad_add_fusion.1.sc, ...), custom_call_target="tpu_custom_call" | custom-call | flops 10871635968 | bytes 20000000 | tf_op jit(solution)/shard_map/mlp1/pallas_call | solution.py:87
  185.0 23.5 %mlp0.1 = (bf16[2,4,432,128]{3,2,1,0:T(8,128)(2,1)}, bf16[2,4,432,128]{3,2,1,0:T(8,128)(2,1)}, bf16[2,4,432,128]{3,2,1,0:T(8,128)(2,1)}, bf16[2,4,432,128]{3,2,1...) custom-call(s32[4]{0:T(128)} %pad_add_fusion.1.sc, ...), custom_call_target="tpu_custom_call" | custom-call | flops 10871635968 | bytes 20000000 | tf_op jit(solution)/shard_map/mlp0/pallas_call | solution.py:87
  219.8 12.3 %collective-permute-done.33 = bf16[2,4,432,128]{3,2,1,0:T(8,128)(2,1)} collective-permute-done((bf16[2,4,432,128]{3,2,1,0:T(8,128)(2,1)}, bf16[2,4,432,128]{3,2,1,0:T(8,128)(2,1)}, u32[]{:S(2)}, u32[]{:S(2)}) %collective-permute-start.33) | collective-permute-done | bytes 884768 | tf_op jit(solution)/shard_map/ppermute | solution.py:449
  235.8 15.2 %collective-permute-done.19 = bf16[2,4,432,128]{3,2,1,0:T(8,128)(2,1)} collective-permute-done((bf16[2,4,432,128]{3,2,1,0:T(8,128)(2,1)}, bf16[2,4,432,128]{3,2,1,0:T(8,128)(2,1)}, u32[]{:S(2)}, u32[]{:S(2)}) %collective-permute-start.19) | collective-permute-done | bytes 884768 | tf_op jit(solution)/shard_map/ppermute | solution.py:449
  258.6 10.9 %collective-permute-done.26 = bf16[2,4,432,128]{3,2,1,0:T(8,128)(2,1)} collective-permute-done((bf16[2,4,432,128]{3,2,1,0:T(8,128)(2,1)}, bf16[2,4,432,128]{3,2,1,0:T(8,128)(2,1)}, u32[]{:S(2)}, u32[]{:S(2)}) %collective-permute-start.26) | collective-permute-done | bytes 884768 | tf_op jit(solution)/shard_map/ppermute | solution.py:449
  276.6 9.7 %mid.1 = (f32[512,1152]{1,0:T(8,128)}, bf16[512,1152]{1,0:T(8,128)(2,1)}, bf16[512,1152]{1,0:T(8,128)(2,1)}, f32[8,1152]{1,0:T(8,128)}) custom-call(bf16[1024,1152]{1,0:T(8,128)(2,1)} %get-tuple-element.63.ds_a, bf16[1024,1152]{1,0:T(8,128)(2,1)} %get-tuple-element.64.ds_b, bf16[1024,1152]{1,0:T(8,128)(2,1)} %get-tuple-element.65.ds_c, ...), custom_call_target="tpu_custom_call" | custom-call | bytes 20000000 | tf_op jit(solution)/shard_map/mid/pallas_call | solution.py:87
  307.7 11.7 %collective-permute-done.38 = bf16[864,128]{1,0:T(8,128)(2,1)S(1)} collective-permute-done((bf16[864,128]{1,0:T(8,128)(2,1)S(1)}, bf16[864,128]{1,0:T(8,128)(2,1)S(1)}, u32[]{:S(2)}, u32[]{:S(2)}) %collective-permute-start.38) | collective-permute-done | bytes 221216 | tf_op jit(solution)/shard_map/ppermute | solution.py:449
  323.4 10.8 %collective-permute-start.23 = (bf16[864,128]{1,0:T(8,128)(2,1)S(1)}, bf16[864,128]{1,0:T(8,128)(2,1)S(1)}, u32[]{:S(2)}, u32[]{:S(2)}) collective-permute-start(bf16[864,128]{1,0:T(8,128)(2,1)S(1)} %pad_maximum_fusion.6), channel_id=1, source_target_pairs={{0,8},{1,9},{2,10},{3,11},{4,12},{5,13},{6,14},{7,15},{8,0},{9,1},... | collective-permute-start | bytes 663560 | tf_op jit(solution)/shard_map/ppermute | solution.py:449
  343.1 10.1 %collective-permute-start.30 = (bf16[864,128]{1,0:T(8,128)(2,1)S(1)}, bf16[864,128]{1,0:T(8,128)(2,1)S(1)}, u32[]{:S(2)}, u32[]{:S(2)}) collective-permute-start(bf16[864,128]{1,0:T(8,128)(2,1)S(1)} %pad_maximum_fusion.9), channel_id=1, source_target_pairs={{0,8},{1,9},{2,10},{3,11},{4,12},{5,13},{6,14},{7,15},{8,0},{9,1},... | collective-permute-start | bytes 663560 | tf_op jit(solution)/shard_map/ppermute | solution.py:449
  354.4 8.0 %heads_back.1 = (bf16[1024,576]{1,0:T(8,128)(2,1)}, bf16[2,4,336,128]{3,2,1,0:T(8,128)(2,1)}, bf16[2,4,336,128]{3,2,1,0:T(8,128)(2,1)}, f32[1,1152]{1,0:T(1,128)}) custom-call(s32[4]{0:T(128)} %pad_add_fusion.1.sc, bf16[512,1152]{1,0:T(8,128)(2,1)} %get-tuple-element.71.da_mine, bf16[512,1152]{1,0:T(8,128)(2,1)} %copy-done.62, ...), custom_call_target="tpu_custom_call" | custom-call | flops 2717908992 | bytes 10000000 | tf_op jit(solution)/shard_map/heads_back/pallas_call | solution.py:87
  362.5 49.6 %attn_back.1.dqkv = bf16[1024,1728]{1,0:T(8,128)(2,1)} custom-call(bf16[1024,1728]{1,0:T(8,128)(2,1)} %get-tuple-element.60.qkv, bf16[1024,576]{1,0:T(8,128)(2,1)} %get-tuple-element.72.dh, f32[8]{0:T(128)} %reshape.598.head_on), custom_call_target="tpu_custom_call" | custom-call | flops 30000001024 | bytes 9000000 | tf_op jit(solution)/shard_map/attn_back/pallas_call | solution.py:87
  413.0 11.3 %qkv_grad.1 = (bf16[2,4,688,128]{3,2,1,0:T(8,128)(2,1)}, bf16[2,4,688,128]{3,2,1,0:T(8,128)(2,1)}, bf16[2,4,336,128]{3,2,1,0:T(8,128)(2,1)}, bf16[2,4,336,128]{3,2,1,0:T(8,128)(2,1)}) custom-call(s32[4]{0:T(128)} %pad_add_fusion.1.sc, bf16[1024,1152]{1,0:T(8,128)(2,1)} %get-tuple-element.89.shifted, bf16[1024,1728]{1,0:T(8,128)(2,1)} %attn_back.1.dqkv, ...), custom_call_target="tpu_custom_call" | custom-call | flops 4076863488 | bytes 12000000 | tf_op jit(solution)/shard_map/qkv_grad/pallas_call | solution.py:87
  430.2 9.0 %qkv_back.1.mine = bf16[1024,1152]{1,0:T(8,128)(2,1)} custom-call(bf16[1024,1728]{1,0:T(8,128)(2,1)} %attn_back.1.dqkv, bf16[1152,1728]{1,0:T(8,128)(2,1)} %get-tuple-element.59.w), custom_call_target="tpu_custom_call" | custom-call | flops 4076863488 | bytes 12000000 | tf_op jit(solution)/shard_map/qkv_back/pallas_call | solution.py:87
  443.4 8.0 %collective-permute-done.47 = bf16[2,4,336,128]{3,2,1,0:T(8,128)(2,1)S(1)} collective-permute-done((bf16[2,4,336,128]{3,2,1,0:T(8,128)(2,1)}, bf16[2,4,336,128]{3,2,1,0:T(8,128)(2,1)S(1)}, u32[]{:S(2)}, u32[]{:S(2)}) %collective-permute-start.47) | collective-permute-done | bytes 688160 | tf_op jit(solution)/shard_map/ppermute | solution.py:449
  456.5 25.7 %collective-permute-done.41 = bf16[4,336,128]{2,1,0:T(8,128)(2,1)S(1)} collective-permute-done((bf16[4,336,128]{2,1,0:T(8,128)(2,1)S(1)}, bf16[4,336,128]{2,1,0:T(8,128)(2,1)S(1)}, u32[]{:S(2)}, u32[]{:S(2)}) %collective-permute-start.41) | collective-permute-done | bytes 344096 | tf_op jit(solution)/shard_map/ppermute | solution.py:449
  517.2 10.7 %collective-permute-done.46 = bf16[4,688,128]{2,1,0:T(8,128)(2,1)} collective-permute-done((bf16[4,688,128]{2,1,0:T(8,128)(2,1)S(1)}, bf16[4,688,128]{2,1,0:T(8,128)(2,1)}, u32[]{:S(2)}, u32[]{:S(2)}) %collective-permute-start.46) | collective-permute-done | bytes 704544 | tf_op jit(solution)/shard_map/ppermute | solution.py:449
  533.9 76.9 %all-gather = f32[32,1,6912]{2,1,0:T(1,128)S(1)} all-gather(f32[1,1,6912]{2,1,0:T(1,128)S(1)} %copy-done.43), channel_id=1, replica_groups=mesh['bucket'=8,'tok'=4] {'bucket','tok'}, dimensions={0}, use_global_device_ids=true | all-gather | bytes 912384 | tf_op jit(solution)/shard_map/all_gather | solution.py:663
  (374 shorter events, 193.1 us)
Async XLA Ops:
  2.8 44.5 %collective-permute-start.3 = (s32[528]{0:T(1024)S(1)}, s32[528]{0:T(1024)S(1)}, u32[]{:S(2)}, u32[]{:S(2)}) collective-permute-start(s32[528]{0:T(1024)S(1)} %pad_add_fusion), channel_id=1, source_target_pairs={{0,4},{1,5},{2,6},{3,7},{4,0},{5,1},{6,2},{7,3},{8,12},{9,13},{10,... | collective-permute-start | bytes 6344 | tf_op jit(solution)/shard_map/ppermute | solution.py:449
  5.6 55.3 %collective-permute-start.1 = (bf16[256,1152]{1,0:T(8,128)(2,1)}, bf16[256,1152]{1,0:T(8,128)(2,1)S(1)}, u32[]{:S(2)}, u32[]{:S(2)}) collective-permute-start(bf16[256,1152]{1,0:T(8,128)(2,1)} %get-tuple-element.216), channel_id=1, source_target_pairs={{0,1},{1,0},{2,5},{3,4},{4,3},{5,2},{6,7},{7,6},{8,9},{9,8},{10,13... | collective-permute-start | bytes 1769480 | tf_op jit(solution)/shard_map/ppermute | solution.py:449
  8.1 52.8 %collective-permute-start = (bf16[256,1152]{1,0:T(8,128)(2,1)}, bf16[256,1152]{1,0:T(8,128)(2,1)}, u32[]{:S(2)}, u32[]{:S(2)}) collective-permute-start(bf16[256,1152]{1,0:T(8,128)(2,1)} %get-tuple-element.217), channel_id=1, source_target_pairs={{0,0},{1,1},{2,4},{3,5},{4,2},{5,3},{6,6},{7,7},{8,8},{9,9},{10,12... | collective-permute-start | bytes 1769480 | tf_op jit(solution)/shard_map/ppermute | solution.py:449
  75.4 48.0 %collective-permute-start.10 = (bf16[512,1152]{1,0:T(8,128)(2,1)}, bf16[512,1152]{1,0:T(8,128)(2,1)}, u32[]{:S(2)}, u32[]{:S(2)}) collective-permute-start(bf16[512,1152]{1,0:T(8,128)(2,1)} %pad_maximum_fusion.1), channel_id=1, source_target_pairs={{0,4},{1,5},{2,6},{3,7},{4,0},{5,1},{6,2},{7,3},{8,12},{9,13},{10,... | collective-permute-start | bytes 3538952 | tf_op jit(solution)/shard_map/ppermute | solution.py:449
  211.9 39.1 %collective-permute-start.19 = (bf16[2,4,432,128]{3,2,1,0:T(8,128)(2,1)}, bf16[2,4,432,128]{3,2,1,0:T(8,128)(2,1)}, u32[]{:S(2)}, u32[]{:S(2)}) collective-permute-start(bf16[2,4,432,128]{3,2,1,0:T(8,128)(2,1)} %get-tuple-element.76), channel_id=1, source_target_pairs={{0,1},{1,0},{2,3},{3,2},{4,5},{5,4},{6,7},{7,6},{8,9},{9,8},{10,11... | collective-permute-start | bytes 2654216 | tf_op jit(solution)/shard_map/ppermute | solution.py:449
  212.9 42.1 %collective-permute-start.21 = (bf16[2,4,432,128]{3,2,1,0:T(8,128)(2,1)}, bf16[2,4,432,128]{3,2,1,0:T(8,128)(2,1)}, u32[]{:S(2)}, u32[]{:S(2)}) collective-permute-start(bf16[2,4,432,128]{3,2,1,0:T(8,128)(2,1)} %get-tuple-element.78), channel_id=1, source_target_pairs={{0,2},{1,3},{2,0},{3,1},{4,6},{5,7},{6,4},{7,5},{8,10},{9,11},{10,... | collective-permute-start | bytes 2654216 | tf_op jit(solution)/shard_map/ppermute | solution.py:449
  213.3 56.2 %collective-permute-start.26 = (bf16[2,4,432,128]{3,2,1,0:T(8,128)(2,1)}, bf16[2,4,432,128]{3,2,1,0:T(8,128)(2,1)}, u32[]{:S(2)}, u32[]{:S(2)}) collective-permute-start(bf16[2,4,432,128]{3,2,1,0:T(8,128)(2,1)} %get-tuple-element.80), channel_id=1, source_target_pairs={{0,1},{1,0},{2,3},{3,2},{4,5},{5,4},{6,7},{7,6},{8,9},{9,8},{10,11... | collective-permute-start | bytes 2654216 | tf_op jit(solution)/shard_map/ppermute | solution.py:449
  232.0 40.8 %collective-permute-start.28 = (bf16[2,4,432,128]{3,2,1,0:T(8,128)(2,1)}, bf16[2,4,432,128]{3,2,1,0:T(8,128)(2,1)S(1)}, u32[]{:S(2)}, u32[]{:S(2)}) collective-permute-start(bf16[2,4,432,128]{3,2,1,0:T(8,128)(2,1)} %get-tuple-element.82), channel_id=1, source_target_pairs={{0,2},{1,3},{2,0},{3,1},{4,6},{5,7},{6,4},{7,5},{8,10},{9,11},{10,... | collective-permute-start | bytes 2654216 | tf_op jit(solution)/shard_map/ppermute | solution.py:449
  235.8 38.8 %collective-permute-start.12 = (bf16[512,1152]{1,0:T(8,128)(2,1)S(1)}, bf16[512,1152]{1,0:T(8,128)(2,1)S(1)}, u32[]{:S(2)}, u32[]{:S(2)}) collective-permute-start(bf16[512,1152]{1,0:T(8,128)(2,1)S(1)} %add_convert_fusion), channel_id=1, source_target_pairs={{0,4},{1,5},{2,6},{3,7},{4,0},{5,1},{6,2},{7,3},{8,12},{9,13},{10,... | collective-permute-start | bytes 3538952 | tf_op jit(solution)/shard_map/ppermute | solution.py:449
  255.0 34.3 %collective-permute-start.34 = (bf16[4,432,128]{2,1,0:T(8,128)(2,1)}, bf16[4,432,128]{2,1,0:T(8,128)(2,1)}, u32[]{:S(2)}, u32[]{:S(2)}) collective-permute-start(bf16[4,432,128]{2,1,0:T(8,128)(2,1)} %fusion.8), channel_id=1, source_target_pairs={{0,2},{1,3},{2,0},{3,1},{4,6},{5,7},{6,4},{7,5},{8,10},{9,11},{10,... | collective-permute-start | bytes 1327112 | tf_op jit(solution)/shard_map/ppermute | solution.py:449
  292.0 160.0 %collective-permute-start.13 = (bf16[256,1152]{1,0:T(8,128)(2,1)}, bf16[256,1152]{1,0:T(8,128)(2,1)}, u32[]{:S(2)}, u32[]{:S(2)}) collective-permute-start(bf16[256,1152]{1,0:T(8,128)(2,1)} %get-tuple-element.212), channel_id=1, source_target_pairs={{0,0},{1,1},{2,4},{3,5},{4,2},{5,3},{6,6},{7,7},{8,8},{9,9},{10,12... | collective-permute-start | bytes 1769480 | tf_op jit(solution)/shard_map/ppermute | solution.py:449
  299.6 53.7 %collective-permute-start.15 = (bf16[512,1152]{1,0:T(8,128)(2,1)S(1)}, bf16[512,1152]{1,0:T(8,128)(2,1)S(1)}, u32[]{:S(2)}, u32[]{:S(2)}) collective-permute-start(bf16[512,1152]{1,0:T(8,128)(2,1)S(1)} %copy-done.61), channel_id=1, source_target_pairs={{0,4},{1,5},{2,6},{3,7},{4,0},{5,1},{6,2},{7,3},{8,12},{9,13},{10,... | collective-permute-start | bytes 3538952 | tf_op jit(solution)/shard_map/ppermute | solution.py:449
  338.5 85.8 %collective-permute-start.31 = (bf16[864,128]{1,0:T(8,128)(2,1)S(1)}, bf16[864,128]{1,0:T(8,128)(2,1)S(1)}, u32[]{:S(2)}, u32[]{:S(2)}) collective-permute-start(bf16[864,128]{1,0:T(8,128)(2,1)S(1)} %pad_maximum_fusion.10), channel_id=1, source_target_pairs={{0,16},{1,17},{2,18},{3,19},{4,20},{5,21},{6,22},{7,23},{8,24},{9,... | collective-permute-start | bytes 663560 | tf_op jit(solution)/shard_map/ppermute | solution.py:449
  338.5 86.5 %collective-permute-start.32 = (bf16[864,128]{1,0:T(8,128)(2,1)S(1)}, bf16[864,128]{1,0:T(8,128)(2,1)S(1)}, u32[]{:S(2)}, u32[]{:S(2)}) collective-permute-start(bf16[864,128]{1,0:T(8,128)(2,1)S(1)} %pad_maximum_fusion.11), channel_id=1, source_target_pairs={{0,24},{1,25},{2,26},{3,27},{4,28},{5,29},{6,30},{7,31},{8,16},{9,... | collective-permute-start | bytes 663560 | tf_op jit(solution)/shard_map/ppermute | solution.py:449
  343.1 83.4 %collective-permute-start.30 = (bf16[864,128]{1,0:T(8,128)(2,1)S(1)}, bf16[864,128]{1,0:T(8,128)(2,1)S(1)}, u32[]{:S(2)}, u32[]{:S(2)}) collective-permute-start(bf16[864,128]{1,0:T(8,128)(2,1)S(1)} %pad_maximum_fusion.9), channel_id=1, source_target_pairs={{0,8},{1,9},{2,10},{3,11},{4,12},{5,13},{6,14},{7,15},{8,0},{9,1},... | collective-permute-start | bytes 663560 | tf_op jit(solution)/shard_map/ppermute | solution.py:449
  440.7 56.8 %collective-permute-start.16 = (bf16[512,1152]{1,0:T(8,128)(2,1)S(1)}, bf16[512,1152]{1,0:T(8,128)(2,1)S(1)}, u32[]{:S(2)}, u32[]{:S(2)}) collective-permute-start(bf16[512,1152]{1,0:T(8,128)(2,1)S(1)} %slice.789), channel_id=1, source_target_pairs={{0,4},{1,5},{2,6},{3,7},{4,0},{5,1},{6,2},{7,3},{8,12},{9,13},{10,... | collective-permute-start | bytes 3538952 | tf_op jit(solution)/shard_map/ppermute | solution.py:449
  440.9 63.3 %collective-permute-start.45 = (bf16[2,4,688,128]{3,2,1,0:T(8,128)(2,1)}, bf16[2,4,688,128]{3,2,1,0:T(8,128)(2,1)S(1)}, u32[]{:S(2)}, u32[]{:S(2)}) collective-permute-start(bf16[2,4,688,128]{3,2,1,0:T(8,128)(2,1)} %get-tuple-element.96), channel_id=1, source_target_pairs={{0,1},{1,0},{2,3},{3,2},{4,5},{5,4},{6,7},{7,6},{8,9},{9,8},{10,11... | collective-permute-start | bytes 4227080 | tf_op jit(solution)/shard_map/ppermute | solution.py:449
  451.3 30.8 %collective-permute-start.41 = (bf16[4,336,128]{2,1,0:T(8,128)(2,1)S(1)}, bf16[4,336,128]{2,1,0:T(8,128)(2,1)S(1)}, u32[]{:S(2)}, u32[]{:S(2)}) collective-permute-start(bf16[4,336,128]{2,1,0:T(8,128)(2,1)S(1)} %fusion.19), channel_id=1, source_target_pairs={{0,1},{1,0},{2,3},{3,2},{4,5},{5,4},{6,7},{7,6},{8,9},{9,8},{10,11... | collective-permute-start | bytes 1032200 | tf_op jit(solution)/shard_map/ppermute | solution.py:449
  452.1 37.0 %collective-permute-start.48 = (bf16[4,336,128]{2,1,0:T(8,128)(2,1)S(1)}, bf16[4,336,128]{2,1,0:T(8,128)(2,1)S(1)}, u32[]{:S(2)}, u32[]{:S(2)}) collective-permute-start(bf16[4,336,128]{2,1,0:T(8,128)(2,1)S(1)} %fusion.20), channel_id=1, source_target_pairs={{0,1},{1,0},{2,3},{3,2},{4,5},{5,4},{6,7},{7,6},{8,9},{9,8},{10,11... | collective-permute-start | bytes 1032200 | tf_op jit(solution)/shard_map/ppermute | solution.py:449
  509.8 107.4 %collective-permute-start.17 = (bf16[256,1152]{1,0:T(8,128)(2,1)}, bf16[256,1152]{1,0:T(8,128)(2,1)}, u32[]{:S(2)}, u32[]{:S(2)}) collective-permute-start(bf16[256,1152]{1,0:T(8,128)(2,1)} %get-tuple-element.210), channel_id=1, source_target_pairs={{0,0},{1,1},{2,4},{3,5},{4,2},{5,3},{6,6},{7,7},{8,8},{9,9},{10,12... | collective-permute-start | bytes 1769480 | tf_op jit(solution)/shard_map/ppermute | solution.py:449
  515.8 101.4 %collective-permute-start.18 = (bf16[256,1152]{1,0:T(8,128)(2,1)}, bf16[256,1152]{1,0:T(8,128)(2,1)}, u32[]{:S(2)}, u32[]{:S(2)}) collective-permute-start(bf16[256,1152]{1,0:T(8,128)(2,1)} %get-tuple-element.211), channel_id=1, source_target_pairs={{0,1},{1,0},{2,5},{3,4},{4,3},{5,2},{6,7},{7,6},{8,9},{9,8},{10,13... | collective-permute-start | bytes 1769480 | tf_op jit(solution)/shard_map/ppermute | solution.py:449
  529.5 86.5 %collective-permute-start.50 = (bf16[1024,128]{1,0:T(8,128)(2,1)S(1)}, bf16[1024,128]{1,0:T(8,128)(2,1)S(1)}, u32[]{:S(2)}, u32[]{:S(2)}) collective-permute-start(bf16[1024,128]{1,0:T(8,128)(2,1)S(1)} %pad_maximum_fusion.4), channel_id=1, source_target_pairs={{0,16},{1,17},{2,18},{3,19},{4,20},{5,21},{6,22},{7,23},{8,24},{9,... | collective-permute-start | bytes 786440 | tf_op jit(solution)/shard_map/ppermute | solution.py:449
  530.1 85.9 %collective-permute-start.51 = (bf16[1024,128]{1,0:T(8,128)(2,1)S(1)}, bf16[1024,128]{1,0:T(8,128)(2,1)S(1)}, u32[]{:S(2)}, u32[]{:S(2)}) collective-permute-start(bf16[1024,128]{1,0:T(8,128)(2,1)S(1)} %pad_maximum_fusion.5), channel_id=1, source_target_pairs={{0,24},{1,25},{2,26},{3,27},{4,28},{5,29},{6,30},{7,31},{8,16},{9,... | collective-permute-start | bytes 786440 | tf_op jit(solution)/shard_map/ppermute | solution.py:449
  532.8 83.3 %collective-permute-start.49 = (bf16[1024,128]{1,0:T(8,128)(2,1)}, bf16[1024,128]{1,0:T(8,128)(2,1)S(1)}, u32[]{:S(2)}, u32[]{:S(2)}) collective-permute-start(bf16[1024,128]{1,0:T(8,128)(2,1)} %pad_maximum_fusion.3), channel_id=1, source_target_pairs={{0,8},{1,9},{2,10},{3,11},{4,12},{5,13},{6,14},{7,15},{8,0},{9,1},... | collective-permute-start | bytes 786440 | tf_op jit(solution)/shard_map/ppermute | solution.py:449
  (93 other events, 1309.7 us)

commit v2 on v1

--- a/solution.py
+++ b/solution.py
@@ -66,32 +66,235 @@
 G1R = 3 * DC
 G2R = 2 * FZ + FZ // 4
 PR = 2 * DC + DC // 3
+PA = 176
 QR = 7 * DC + 16
-QA = QR // 2 + 176
-QB_ROWS = QR - QA
+QA = QR // 2
 VMEM_LIMIT = 58 * 1024 * 1024
 
 
-def call(kernel, name, out_shape, args, grid=None, in_specs=None, out_specs=None, scratch=(), grid_spec=None,
-         flops=0, nbytes=0):
+ANY = pl.BlockSpec(memory_space=pl.ANY)
+MESH = pl.DeviceIdType.MESH
+
+
+def place():
+    b, t = lax.axis_index("bucket"), lax.axis_index("tok")
+    return b // 2, b % 2, t // 2, t % 2
+
+
+def flip(value, other):
+    return (value // 2 + other // 2) % 2 * 2 + (value % 2 + other % 2) % 2
+
+
+def peer(name):
+    z, c, y, x = place()
+    if name == "x":
+        x = 1 - x
+    elif name == "y":
+        y = 1 - y
+    elif name == "xy":
+        x, y = 1 - x, 1 - y
+    elif name == "c":
+        c = 1 - c
+    elif name in ("t0", "t1"):
+        c, y, x = y, c, x if name == "t0" else 1 - x
+    else:
+        z = flip(z, int(name[1]))
+    return (z * 2 + c, y * 2 + x)
+
+
+def meet(names):
+    sem = pltpu.get_barrier_semaphore()
+    others = [name for name in names if name != "t0"]
+    for name in others:
+        pl.semaphore_signal(sem, inc=1, device_id=peer(name), device_id_type=MESH)
+    wanted = len(others)
+    if "t0" in names:
+        _, c, y, _ = place()
+        wanted = wanted + (c + y) % 2
+
+        @pl.when(c != y)
+        def _():
+            pl.semaphore_signal(sem, inc=1, device_id=peer("t0"), device_id_type=MESH)
+
+    pl.semaphore_wait(sem, wanted)
+
+
+def remote(src, dst, sems, k, name):
+    return pltpu.make_async_remote_copy(
+        src_ref=src, dst_ref=dst, send_sem=sems.at[0, k], recv_sem=sems.at[1, k],
+        device_id=peer(name), device_id_type=MESH,
+    )
+
+
+def vm(*shape, dtype=bf16):
+    return pltpu.VMEM(shape, dtype)
+
+
+class FirstSum:
+    peers = ("x", "y")
+
+    def __init__(self, keep_a, sent_a, keep_b, sent_b):
+        self.ins = [keep_a, sent_a, keep_b, sent_b]
+        shapes = [keep.shape[1:] for keep in (keep_a, keep_b)]
+        self.outs = [jax.ShapeDtypeStruct(s, bf16) for s in shapes for _ in range(2)]
+        self.scratch = [vm(*s) for s in shapes for _ in range(3)]
+        self.scratch += [pltpu.SemaphoreType.DMA((2, 4)), pltpu.SemaphoreType.DMA((4,))]
+
+    def plan(self, ins, outs, scratch):
+        ka, sa, kb, sb = ins
+        _, qa, _, qb = outs
+        kav, rav, _, kbv, rbv, _, sems, local = scratch
+        far = [
+            remote(sa.at[1], rav, sems, 0, "x"),
+            remote(sb.at[1], rbv, sems, 1, "y"),
+            remote(sa.at[0], qa, sems, 2, "x"),
+            remote(sb.at[0], qb, sems, 3, "y"),
+        ]
+        near = [
+            pltpu.make_async_copy(ka.at[1], kav, local.at[0]),
+            pltpu.make_async_copy(kb.at[1], kbv, local.at[1]),
+        ]
+        return far, near
+
+    def finish(self, ins, outs, scratch):
+        kav, rav, oav, kbv, rbv, obv, _, local = scratch
+        oav[...] = (kav[...].astype(f32) + rav[...].astype(f32)).astype(bf16)
+        obv[...] = (kbv[...].astype(f32) + rbv[...].astype(f32)).astype(bf16)
+        return [
+            pltpu.make_async_copy(oav, outs[0], local.at[2]),
+            pltpu.make_async_copy(obv, outs[2], local.at[3]),
+        ]
+
+
+class SecondSum:
+    peers = ("x", "y")
+
+    def __init__(self, on_a, q_a, on_b, q_b, keep_a, keep_b):
+        self.ins = [on_a, q_a, on_b, q_b, keep_a, keep_b]
+        self.rows = [on_a.shape[1], on_b.shape[1]]
+        total = sum(self.rows)
+        self.outs = [jax.ShapeDtypeStruct((3, total, LANES), bf16), jax.ShapeDtypeStruct((total, LANES), f32)]
+        self.scratch = [vm(4, r, LANES) for r in self.rows for _ in range(3)]
+        self.scratch += [vm(3, total, LANES), vm(total, LANES, dtype=f32)]
+        self.scratch += [pltpu.SemaphoreType.DMA((2, 2)), pltpu.SemaphoreType.DMA((6,))]
+
+    def plan(self, ins, outs, scratch):
+        oa, qa, ob, qb, ka, kb = ins
+        kav, qav, rav, kbv, qbv, rbv, _, _, sems, local = scratch
+        far = [remote(oa, rav, sems, 0, "y"), remote(ob, rbv, sems, 1, "x")]
+        pairs = [(ka.at[0], kav), (qa, qav), (kb.at[0], kbv), (qb, qbv)]
+        return far, [pltpu.make_async_copy(a, b, local.at[k]) for k, (a, b) in enumerate(pairs)]
+
+    def finish(self, ins, outs, scratch):
+        zs, zk, local = scratch[6], scratch[7], scratch[9]
+        start = 0
+        for k, r in enumerate(self.rows):
+            kv, qv, rv = scratch[3 * k : 3 * k + 3]
+            for j in range(4):
+                total = kv[j].astype(f32) + qv[j].astype(f32) + rv[j].astype(f32)
+                if j == 0:
+                    zk[start : start + r, :] = total
+                else:
+                    zs[j - 1, start : start + r, :] = total.astype(bf16)
+            start += r
+        return [
+            pltpu.make_async_copy(zs, outs[0], local.at[4]),
+            pltpu.make_async_copy(zk, outs[1], local.at[5]),
+        ]
+
+
+class ThirdSum:
+    peers = ("z1", "z2", "z3")
+
+    def __init__(self, sent, kept):
+        self.ins = [sent, kept]
+        self.outs = [jax.ShapeDtypeStruct(kept.shape, f32)]
+        self.scratch = [vm(*sent.shape), vm(*kept.shape, dtype=f32)]
+        self.scratch += [pltpu.SemaphoreType.DMA((2, 3)), pltpu.SemaphoreType.DMA((2,))]
+
+    def plan(self, ins, outs, scratch):
+        got, kept, sems, local = scratch
+        far = [remote(ins[0].at[k], got.at[k], sems, k, f"z{k + 1}") for k in (2, 1, 0)]
+        return far, [pltpu.make_async_copy(ins[1], kept, local.at[0])]
+
+    def finish(self, ins, outs, scratch):
+        got, kept, _, local = scratch
+        kept[...] = kept[...] + got[0].astype(f32) + got[1].astype(f32) + got[2].astype(f32)
+        return [pltpu.make_async_copy(kept, outs[0], local.at[1])]
+
+
+def call(kernel, name, out_shape, args, in_specs=None, out_specs=None, scratch=(), grid=None,
+         peers=(), jobs=(), cid=None, flops=0, nbytes=0):
     whole = pl.BlockSpec(memory_space=pltpu.VMEM)
-    kwargs = {}
-    if grid_spec is not None:
-        kwargs["grid_spec"] = grid_spec
-    else:
-        kwargs["in_specs"] = in_specs if in_specs is not None else [whole] * len(args)
-        kwargs["out_specs"] = out_specs if out_specs is not None else jax.tree.map(lambda _: whole, out_shape)
-        kwargs["scratch_shapes"] = list(scratch)
-        if grid is not None:
-            kwargs["grid"] = grid
-    return pl.pallas_call(
-        kernel,
-        out_shape=out_shape,
-        compiler_params=pltpu.CompilerParams(vmem_limit_bytes=VMEM_LIMIT),
+    single = not isinstance(out_shape, (tuple, list))
+    out_shape = [out_shape] if single else list(out_shape)
+    in_specs = list(in_specs) if in_specs is not None else [whole] * len(args)
+    out_specs = [whole] * len(out_shape) if out_specs is None else [out_specs] if single else list(out_specs)
+    counts = [len(args), sum(len(j.ins) for j in jobs), len(out_shape), sum(len(j.outs) for j in jobs), len(scratch)]
+    names = sorted(set(peers).union(*[j.peers for j in jobs]))
+
+    def run(*refs):
+        groups, at = [], 0
+        for n in counts:
+            groups.append(refs[at : at + n])
+            at += n
+        bound, ai, ao, asc = [], 0, 0, at
+        for j in jobs:
+            bound.append((
+                j, groups[1][ai : ai + len(j.ins)], groups[3][ao : ao + len(j.outs)], refs[asc : asc + len(j.scratch)]
+            ))
+            ai, ao, asc = ai + len(j.ins), ao + len(j.outs), asc + len(j.scratch)
+
+        def begin():
+            if names:
+                meet(names)
+            for j, *r in bound:
+                for group in j.plan(*r):
+                    for copy in group:
+                        copy.start()
+
+        def end():
+            last = []
+            for j, *r in bound:
+                far, near = j.plan(*r)
+                for copy in far:
+                    copy.wait()
+                for copy in near:
+                    copy.wait()
+                copies = j.finish(*r)
+                for copy in copies:
+                    copy.start()
+                last += copies
+            for copy in last:
+                copy.wait()
+
+        if grid is None:
+            begin()
+            kernel(*groups[0], *groups[2], *groups[4])
+            end()
+        else:
+            pl.when(pl.program_id(0) == 0)(begin)
+            kernel(*groups[0], *groups[2], *groups[4])
+            pl.when(pl.program_id(0) == grid[0] - 1)(end)
+
+    extra = {} if grid is None else {"grid": grid}
+    params = {"collective_id": cid, "has_side_effects": True} if names else {}
+    outs = pl.pallas_call(
+        run,
+        out_shape=out_shape + [o for j in jobs for o in j.outs],
+        in_specs=in_specs + [ANY] * counts[1],
+        out_specs=out_specs + [ANY] * counts[3],
+        scratch_shapes=list(scratch) + [q for j in jobs for q in j.scratch],
+        compiler_params=pltpu.CompilerParams(vmem_limit_bytes=VMEM_LIMIT, **params),
         cost_estimate=pl.CostEstimate(flops=int(flops), bytes_accessed=int(nbytes), transcendentals=0),
         name=name,
-        **kwargs,
-    )(*args)
+        **extra,
+    )(*args, *[a for j in jobs for a in j.ins])
+    own, rest, given = outs[: len(out_shape)], outs[len(out_shape) :], []
+    for j in jobs:
+        given.append(rest[: len(j.outs)])
+        rest = rest[len(j.outs) :]
+    return (own[0] if single else own), given
 
 
 SMEM = pl.BlockSpec(memory_space=pltpu.SMEM)
@@ -101,18 +304,19 @@
     return pl.BlockSpec(shape, lambda *_: (0,) * len(shape))
 
 
+def once(*shape):
+    return pl.BlockSpec(shape, lambda *_: (0,) * len(shape), pipeline_mode=pl.Buffered(1))
+
+
 def rows(block, width):
     return pl.BlockSpec((block, width), lambda i: (i, 0))
 
 
-def prow(block, width):
-    return pl.BlockSpec((block, width), lambda i, s: (i, 0))
-
-
-def prep_kernel(sc, wq, w1, wq_o, w1_o):
+def prep_kernel(wq, w1, wq_o, w1_o):
+    c = place()[1]
     for core in range(2):
 
-        @pl.when(sc[1] == core)
+        @pl.when(c == core)
         def _():
             for k in range(12):
                 wq_o[:, DC * k : DC * (k + 1)] = wq[:, DZ * k + DC * core : DZ * k + DC * (core + 1)]
@@ -166,87 +370,137 @@
     shifted2_o[...] = (normed * (1.0 + mod[4:5, :]) + mod[3:4, :]).astype(bf16)
 
 
-def mlp_kernel(steps, sc, sh2, g, kept, mod, w1, b1, chan, w2,
-               g1k, g1s, g2k, g2s, branch_o, ds2_o, sum1_o, sum2_o, acc1, acc2, t1, t2):
+def pack_hidden(block1, block2, o1, o2, ry, rx, rz):
+    o1[ry, rz, : 2 * DC, :] = block1[:, :LANES]
+    o1[ry, rz, 2 * DC :, :] = jnp.concatenate([block1[:DC, LANES:], block1[DC:, LANES:]], axis=1)
+    o2[rx, rz, :FZ, :] = block2[:, :LANES]
+    o2[rx, rz, FZ : 2 * FZ, :] = block2[:, LANES : 2 * LANES]
+    q = FZ // 4
+    o2[rx, rz, 2 * FZ :, :] = jnp.concatenate([block2[q * k : q * (k + 1), 2 * LANES :] for k in range(4)], axis=1)
+
+
+def mlp_kernel(f, *refs):
+    last = f == NF - 1
+    refs = list(refs)
+    sh2, g, kept, mod, w1, b1, chan, w2 = refs[:8]
+    del refs[:8]
+    before = None
+    if f > 0:
+        before = refs[:2]
+        del refs[:2]
+    slots, branch_o, ds2_o, sum1_o, sum2_o = refs[:4], refs[4], refs[5], refs[6], refs[7]
+    del refs[:8]
+    if last:
+        got = refs[:2]
+        del refs[:2]
+    hid, dpre, dbs, w2v, t1, t2, s1k, s1s, s2k, s2s, sems = refs[:11]
+    if last:
+        far, csems = refs[11:]
+        crossing = [remote(far.at[k], got[k], csems, k, "c") for k in range(2)]
+    stages = (s1k, s1s, s2k, s2s)
     i = pl.program_id(0)
-    z, c, y, x = sc[0], sc[1], sc[2], sc[3]
+    z, c, y, x = place()
+
+    @pl.when(i == 0)
+    def _():
+        copy = pltpu.make_async_copy(w2.at[:, c, f], w2v, sems.at[4])
+        copy.start()
+        copy.wait()
+
+    part = pl.ds(pl.multiple_of((1 - i) * LH, LH), LH)
     w1v = w1[0]
-    w2v = w2[...].reshape(FB, D)
+    w2f = w2v[...].reshape(FB, D)
     db = (g[...].astype(f32) * mod[5:6, :] * kept[...]).astype(bf16)
-    v = dot_nn(sh2[...], w1v) + b1[0]
+    dbs[part, :] = db
+    v = dot_nn(sh2[part, :], w1v) + b1[0]
     v2 = v * v
     th = jnp.tanh(GELU_K * v * (1.0 + GELU_C * v2))
     half = 0.5 * (1.0 + th)
     on = chan[0]
     hidden = (v * half * on).astype(bf16)
+    hid[part, :] = hidden
     slope = (half + (0.5 * GELU_K) * v * (1.0 - th * th) * (1.0 + (3.0 * GELU_C) * v2)) * on
-    branch_o[...] = dot_nn(hidden, w2v).astype(bf16)
-    d_pre = (dot_nt(db, w2v) * slope).astype(bf16)
-    ds2_o[...] = dot_nt(d_pre, w1v).astype(bf16)
-    p2 = dot_tn(hidden, db)
-    p1 = dot_tn(sh2[...], d_pre)
+    d_pre = (dot_nt(db, w2f) * slope).astype(bf16)
+    dpre[part, :] = d_pre
+    branch, ds2 = dot_nn(hidden, w2f), dot_nt(d_pre, w1v)
+    if before is not None:
+        branch = branch + before[0][...].astype(f32)
+        ds2 = ds2 + before[1][...].astype(f32)
+    branch, ds2 = branch.astype(bf16), ds2.astype(bf16)
+    if last:
+
+        @pl.when(i == 0)
+        def _():
+            far[0] = branch
+            far[1] = ds2
+            for copy in crossing:
+                copy.start()
+
+        @pl.when(i == 1)
+        def _():
+            branch_o[...] = branch
+            ds2_o[...] = ds2
+    else:
+        branch_o[...] = branch
+        ds2_o[...] = ds2
     s1 = jnp.sum(d_pre.astype(f32), axis=0, keepdims=True)
     s2 = jnp.sum(db.astype(f32), axis=0, keepdims=True)
 
     @pl.when(i == 0)
     def _():
-        acc1[...] = p1
-        acc2[...] = p2
         sum1_o[...] = s1
         sum2_o[...] = s2
 
-    @pl.when(i > 0)
+    @pl.when(i == 1)
     def _():
-        acc1[...] += p1
-        acc2[...] += p2
         sum1_o[...] += s1
         sum2_o[...] += s2
-
-    @pl.when(i == steps - 1)
-    def _():
-        for t in range(4):
-            t1[t] = acc1[:, FZ * t : FZ * (t + 1)].astype(bf16)
-            t2[t] = acc2[:, TD * t : TD * (t + 1)].astype(bf16)
+        for m in range(3):
+            cut = slice(m * D // 3, (m + 1) * D // 3)
+            p = dot_tn(sh2[:, cut], dpre[...]).astype(bf16)
+            for t in range(4):
+                t1[t, cut, :] = p[:, FZ * t : FZ * (t + 1)]
+        for m in range(3):
+            cut = slice(m * FB // 3, (m + 1) * FB // 3)
+            p = dot_tn(hid[:, cut], dbs[...]).astype(bf16)
+            for t in range(4):
+                t2[t, cut, :] = p[:, TD * t : TD * (t + 1)]
         for rz in range(4):
-            zz = rz ^ z
+            zz = flip(z, rz)
             for ry in range(2):
                 for rx in range(2):
-                    tt = (ry ^ y) * 2 + (rx ^ x)
-                    o1 = (g1k, g1s)[rx]
-                    tails = []
-                    for rc in range(2):
-                        start = pl.multiple_of(zz * DZ + (rc ^ c) * DC, 16)
-                        part = t1[tt, pl.ds(start, DC), :]
-                        o1[ry, rz, rc * DC : (rc + 1) * DC, :] = part[:, :LANES]
-                        tails.append(part[:, LANES:])
-                    o1[ry, rz, 2 * DC : 3 * DC, :] = jnp.concatenate(tails, axis=1)
-                    o2 = (g2k, g2s)[ry]
-                    part = t2[tt, pl.ds(pl.multiple_of(zz * FZ, 16), FZ), :]
-                    o2[rx, rz, :FZ, :] = part[:, :LANES]
-                    o2[rx, rz, FZ : 2 * FZ, :] = part[:, LANES : 2 * LANES]
-                    q = FZ // 4
-                    o2[rx, rz, 2 * FZ :, :] = jnp.concatenate(
-                        [part[q * k : q * (k + 1), 2 * LANES :] for k in range(4)], axis=1
-                    )
-
-
-def mid_kernel(ds_a, ds_b, ds_c, ds_r, br_a, br_b, br_c, br_r, attn, tok, g, kept, mod, bias2,
-               d_resid_o, d_attn_o, out_o, sums_o):
+                    tt = (ry + y) % 2 * 2 + (rx + x) % 2
+                    one = [
+                        t1[tt, pl.ds(pl.multiple_of(zz * DZ + (rc + c) % 2 * DC, 16), DC), :] for rc in range(2)
+                    ]
+                    two = t2[tt, pl.ds(pl.multiple_of(zz * FZ, 16), FZ), :]
+                    pack_hidden(jnp.concatenate(one, axis=0), two, (s1k, s1s)[rx], (s2k, s2s)[ry], ry, rx, rz)
+        copies = [pltpu.make_async_copy(a, b, sems.at[k]) for k, (a, b) in enumerate(zip(stages, slots))]
+        for copy in copies:
+            copy.start()
+        for copy in copies:
+            copy.wait()
+        if last:
+            for copy in crossing:
+                copy.wait()
+
+
+def middle_kernel(ds, ds_r, br, br_r, attn, tok, g, kept, mod, bias2, mixed, w,
+                  d_resid_o, out, dh_o, pka, psa, pkb, psb, sums_o, sum_o, da, ob, t1, csems, tsems, lsem):
     i = pl.program_id(0)
-    tokf, gf, at = tok[...].astype(f32), g[...].astype(f32), attn[...]
-    resid = tokf + mod[2:3, :] * at
+    n = LH // 4
+    z, c, y, x = place()
+    part = pl.ds(pl.multiple_of(i * n, n), n)
+    gf, at = g[...].astype(f32), attn[...]
+    resid = tok[...].astype(f32) + mod[2:3, :] * at
     normed2, inverse2 = normalize(resid)
-    ds2 = ds_a[...].astype(f32) + ds_b[...].astype(f32) + ds_c[...].astype(f32) + ds_r[...].astype(f32)
-    branch = (
-        br_a[...].astype(f32) + br_b[...].astype(f32) + br_c[...].astype(f32) + br_r[...].astype(f32) + bias2[...]
-    )
-    kb = kept[...] * branch
-    out_o[...] = (resid + mod[5:6, :] * kb).astype(bf16)
+    ds2 = ds[...].astype(f32) + ds_r[...].astype(f32)
+    kb = kept[...] * (br[...].astype(f32) + br_r[...].astype(f32) + bias2[...])
+    ob[part, :] = (resid + mod[5:6, :] * kb).astype(bf16)
     d_resid = gf + normalize_back(ds2 * (1.0 + mod[4:5, :]), normed2, inverse2)
     d_resid_o[...] = d_resid
-    d_attn_o[...] = (mod[2:3, :] * d_resid).astype(bf16)
-    parts = [at * d_resid, ds2, ds2 * normed2, kb * gf]
-    sums = [jnp.sum(p, axis=0, keepdims=True) for p in parts]
+    da[part, :] = (mod[2:3, :] * d_resid).astype(bf16)
+    sums = [jnp.sum(p, axis=0, keepdims=True) for p in (at * d_resid, ds2, ds2 * normed2, kb * gf)]
     sums = jnp.concatenate(sums + [jnp.zeros((4, D), f32)], axis=0)
 
     @pl.when(i == 0)
@@ -257,31 +511,50 @@
     def _():
         sums_o[...] += sums
 
-
-def heads_kernel(sc, da_mine, da_other, mixed, w, dh_o, pk, ps, sum_o, t1):
-    z, c, y, x = sc[0], sc[1], sc[2], sc[3]
-    wv = w[...].reshape(WC, D)
-    dh_o[:LH, :] = dot_nt(da_mine[...], wv).astype(bf16)
-    dh_o[LH:, :] = dot_nt(da_other[...], wv).astype(bf16)
-    grad = dot_tn(mixed[:LH, :], da_mine[...]) + dot_tn(mixed[LH:, :], da_other[...])
-    sum_o[...] = jnp.sum(da_mine[...].astype(f32), axis=0, keepdims=True) + jnp.sum(
-        da_other[...].astype(f32), axis=0, keepdims=True
-    )
-    for t in range(4):
-        t1[t] = grad[:, TD * t : TD * (t + 1)].astype(bf16)
-    for rz in range(4):
-        zz = rz ^ z
-        for ry in range(2):
-            for rx in range(2):
-                tt = (ry ^ y) * 2 + (rx ^ x)
-                o = (pk, ps)[ry]
-                part = t1[tt, pl.ds(pl.multiple_of(zz * DC, 16), DC), :]
-                o[rx, rz, :DC, :] = part[:, :LANES]
-                o[rx, rz, DC : 2 * DC, :] = part[:, LANES : 2 * LANES]
-                q = DC // 3
-                tails = [part[q * k : q * (k + 1), 2 * LANES :] for k in range(3)]
-                tails.append(jnp.zeros((q, 32), bf16))
-                o[rx, rz, 2 * DC :, :] = jnp.concatenate(tails, axis=1)
+    crossing = [
+        remote(da.at[pl.ds(n * k, n)], da.at[pl.ds(LH + n * k, n)], csems, k, "c") for k in range(4)
+    ]
+    home0 = remote(ob.at[pl.ds(0, LB)], out.at[x], tsems, 0, "t0")
+    stay0 = pltpu.make_async_copy(ob.at[pl.ds(0, LB)], out.at[x], lsem)
+    home1 = remote(ob.at[pl.ds(LB, LB)], out.at[x], tsems, 1, "t1")
+    for k in range(4):
+
+        @pl.when(i == k)
+        def _():
+            crossing[k].start()
+            if k == 1:
+                pl.when(c != y)(home0.start)
+                pl.when(c == y)(stay0.start)
+            if k == 3:
+                home1.start()
+
+    @pl.when(i == 3)
+    def _():
+        for copy in crossing:
+            copy.wait()
+        wv = w[...].reshape(WC, D)
+        dh_o[...] = dot_nt(da[...], wv).astype(bf16)
+        sum_o[...] = dot_nn(jnp.ones((16, L), bf16), da[...])[:8]
+        grad = dot_tn(mixed[...], da[...]).astype(bf16)
+        for t in range(4):
+            t1[t] = grad[:, TD * t : TD * (t + 1)]
+        for rz in range(4):
+            zz = flip(z, rz)
+            for ry in range(2):
+                for rx in range(2):
+                    tt = (ry + y) % 2 * 2 + (rx + x) % 2
+                    a, b = (pka, psa)[rx], (pkb, psb)[ry]
+                    block = t1[tt, pl.ds(pl.multiple_of(zz * DC, 16), DC), :]
+                    a[ry, rz, :DC, :] = block[:, :LANES]
+                    a[ry, rz, DC:, :] = block[: PA - DC, LANES : 2 * LANES]
+                    b[rx, rz, : 2 * DC - PA, :] = block[PA - DC :, LANES : 2 * LANES]
+                    q = DC // 3
+                    tails = [block[q * k : q * (k + 1), 2 * LANES :] for k in range(3)]
+                    tails.append(jnp.zeros((q, 32), bf16))
+                    b[rx, rz, 2 * DC - PA :, :] = jnp.concatenate(tails, axis=1)
+        pl.when(c != y)(home0.wait)
+        pl.when(c == y)(stay0.wait)
+        home1.wait()
 
 
 def attn_back_kernel(step, qkv, dh, head_on, out, qs, ks, vs, dos, dq, dk, dv):
@@ -315,14 +588,13 @@
         out[:, 2 * WC + h * HD : 2 * WC + (h + 1) * HD] = dv[...].astype(bf16)
 
 
-def qkv_grad_kernel(sc, shifted, dqkv, extra, ak, as_, bk, bs, t1):
-    z, c, y, x = sc[0], sc[1], sc[2], sc[3]
+def qkv_grad_kernel(shifted, dqkv, extra, ka, sa, kb, sb, t1):
+    z, c, y, x = place()
     for k in range(4):
-        grad = dot_tn(shifted[:, DZ * k : DZ * (k + 1)], dqkv[...])
+        grad = dot_tn(shifted[:, DZ * k : DZ * (k + 1)], dqkv[...]).astype(bf16)
         for t in range(4):
-            t1[t, DZ * k : DZ * (k + 1), :] = grad[:, 3 * DC * t : 3 * DC * (t + 1)].astype(bf16)
-    ones = jnp.ones((16, L), bf16)
-    sums = dot_nn(ones, dqkv[...])[0:1, :]
+            t1[t, DZ * k : DZ * (k + 1), :] = grad[:, 3 * DC * t : 3 * DC * (t + 1)]
+    sums = dot_nn(jnp.ones((16, L), bf16), dqkv[...])[0:1, :]
     for zs in range(4):
         for ts in range(4):
             piece = DC * zs + DC // 4 * ts
@@ -331,94 +603,132 @@
             row1 = jnp.concatenate([jnp.zeros((1, 88), f32), qsum, jnp.zeros((1, 4), f32)], axis=1)
             row2 = jnp.concatenate([vsum, jnp.zeros((1, LANES - DC // 4), f32)], axis=1)
             add = jnp.concatenate([jnp.zeros((1, LANES), f32), row1, row2, jnp.zeros((13, LANES), f32)], axis=0)
-            rz, ry, rx = zs ^ z, (ts // 2) ^ y, (ts % 2) ^ x
+            rz, ry, rx = flip(z, zs), (ts // 2 + y) % 2, (ts % 2 + x) % 2
             block = (extra[zs, ts] + add).astype(bf16)
 
             @pl.when(ry == 0)
             def _():
-                bk[rx, rz, QB_ROWS - 16 :, :] = block
+                kb[rx, rz, QA - 16 :, :] = block
 
             @pl.when(ry == 1)
             def _():
-                bs[rx, rz, QB_ROWS - 16 :, :] = block
+                sb[rx, rz, QA - 16 :, :] = block
 
     for rz in range(4):
-        zz = rz ^ z
+        zz = flip(z, rz)
         for ry in range(2):
             for rx in range(2):
-                tt = (ry ^ y) * 2 + (rx ^ x)
-                a, b = (ak, as_)[rx], (bk, bs)[ry]
+                tt = (ry + y) % 2 * 2 + (rx + x) % 2
+                a, b = (ka, sa)[rx], (kb, sb)[ry]
                 parts = [
-                    t1[tt, pl.ds(pl.multiple_of(zz * DZ + (rc ^ c) * DC, 16), DC), :] for rc in range(2)
+                    t1[tt, pl.ds(pl.multiple_of(zz * DZ + (rc + c) % 2 * DC, 16), DC), :] for rc in range(2)
                 ]
-                for rc in range(2):
-                    for k in range(2):
-                        first = (2 * k + rc) * DC
-                        a[ry, rz, first : first + DC, :] = parts[rc][:, LANES * k : LANES * (k + 1)]
-                third = [part[:, 2 * LANES : 3 * LANES] for part in parts]
-                cut = QA - 4 * DC
-                a[ry, rz, 4 * DC : QA, :] = third[0][:cut, :]
-                b[rx, rz, : DC - cut, :] = third[0][cut:, :]
-                b[rx, rz, DC - cut : 2 * DC - cut, :] = third[1]
+                strips = [p[:, LANES * k : LANES * (k + 1)] for k in range(3) for p in parts]
                 gap = jnp.zeros((DC, 16), bf16)
-                b[rx, rz, 2 * DC - cut : 3 * DC - cut, :] = jnp.concatenate(
-                    [parts[0][:, 3 * LANES :], gap, parts[1][:, 3 * LANES :], gap], axis=1
-                )
-
-
-def back_kernel(dqkv, w, out):
-    out[...] = dot_nt(dqkv[...], w[...]).astype(bf16)
-
-
-def last_kernel(mine, other, d_resid, tok, mod, grad_o, sums_o):
+                strips.append(jnp.concatenate([parts[0][:, 3 * LANES :], gap, parts[1][:, 3 * LANES :], gap], axis=1))
+                for k, strip in enumerate(strips):
+                    first = DC * k
+                    if first + DC <= QA:
+                        a[ry, rz, first : first + DC, :] = strip
+                    elif first >= QA:
+                        b[rx, rz, first - QA : first - QA + DC, :] = strip
+                    else:
+                        a[ry, rz, first:, :] = strip[: QA - first]
+                        b[rx, rz, : first + DC - QA, :] = strip[QA - first :]
+
+
+def tail_kernel(dqkv, w, d_resid, tok, mod, sums_mid, grad, item_o, got, far, gb, other, csems, tsems, lsem):
     i = pl.program_id(0)
-    d_shifted = mine[...].astype(f32) + other[...].astype(f32)
-    normed, inverse = normalize(tok[...].astype(f32))
-    grad = d_resid[...] + normalize_back(d_shifted * (1.0 + mod[1:2, :]), normed, inverse)
-    grad_o[...] = grad.astype(bf16)
-    sums = [jnp.sum(p, axis=0, keepdims=True) for p in (d_shifted, d_shifted * normed)]
-    sums = jnp.concatenate(sums + [jnp.zeros((6, D), f32)], axis=0)
-
-    @pl.when(i == 0)
-    def _():
-        sums_o[...] = sums
-
-    @pl.when(i > 0)
-    def _():
-        sums_o[...] += sums
-
-
-def finish_kernel(sc, f0, f1, f2, fp, fq, s0, s1, s2, sq, gq_o, gp_o, g1_o, g2_o):
-    own = fq[...]
-    sib = sq[...].astype(f32)
-    mine = jnp.concatenate(
-        [own[0:DC], own[2 * DC : 3 * DC], own[4 * DC : 5 * DC], own[6 * DC : 7 * DC, : DC // 3]], axis=1
-    )
-    theirs = jnp.concatenate(
-        [sib[DC : 2 * DC], sib[3 * DC : 4 * DC], sib[5 * DC : 6 * DC], sib[6 * DC : 7 * DC, 64 : 64 + DC // 3]],
-        axis=1,
-    )
-    first = [f[...] for f in (f0, f1, f2)]
-    second = [s[...].astype(f32) for s in (s0, s1, s2)]
-    for core in range(2):
-
-        @pl.when(sc[1] == core)
+    c, y, x = place()[1:]
+    d_shifted = dot_nt(dqkv[...], w[...])
+    crossing = [remote(far.at[k], got.at[k], csems, k, "c") for k in range(2)]
+    sums_over = remote(item_o, other, csems, 2, "c")
+    home0 = remote(gb.at[0], grad.at[x], tsems, 0, "t0")
+    stay0 = pltpu.make_async_copy(gb.at[0], grad.at[x], lsem)
+    home1 = remote(gb.at[1], grad.at[x], tsems, 1, "t1")
+    for k in range(2):
+
+        @pl.when(i == k)
         def _():
-            for k in range(3):
-                a, b = DZ * k + DC * core, DZ * k + DC * (1 - core)
-                gq_o[:, a : a + DC] = mine[:, DC * k : DC * (k + 1)]
-                gq_o[:, b : b + DC] = theirs[:, DC * k : DC * (k + 1)]
-            for f in range(NF):
-                a, b = FF // 8 * core + FZ * f, FF // 8 * (1 - core) + FZ * f
-                g1_o[:, a : a + FZ] = jnp.concatenate(
-                    [first[f][:DC], first[f][2 * DC : 3 * DC, : FZ - LANES]], axis=1
-                )
-                g1_o[:, b : b + FZ] = jnp.concatenate(
-                    [second[f][DC : 2 * DC], second[f][2 * DC : 3 * DC, FZ - LANES :]], axis=1
-                )
-
-    for f in range(NF):
-        part = first[f][G1R:]
+            far[k] = d_shifted.astype(bf16)
+            crossing[k].start()
+
+        @pl.when(i == k + 2)
+        def _():
+            crossing[k].wait()
+            total = d_shifted + got[k].astype(f32)
+            normed, inverse = normalize(tok[...].astype(f32))
+            back = d_resid[...] + normalize_back(total * (1.0 + mod[1:2, :]), normed, inverse)
+            gb[k] = back.astype(bf16)
+            sums = [jnp.sum(p, axis=0, keepdims=True) for p in (total, total * normed)]
+            if k == 0:
+                pl.when(c != y)(home0.start)
+                pl.when(c == y)(stay0.start)
+                item_o[...] = jnp.concatenate(sums + [sums_mid[0:4, :], jnp.zeros((2, D), f32)], axis=0)
+            else:
+                home1.start()
+                item_o[0:2, :] += jnp.concatenate(sums, axis=0)
+                sums_over.start()
+                sums_over.wait()
+                item_o[...] += other[...]
+                pl.when(c != y)(home0.wait)
+                pl.when(c == y)(stay0.wait)
+                home1.wait()
+
+
+def square_kernel(item, square, sems, lsem):
+    t = lax.axis_index("tok")
+    here = pltpu.make_async_copy(item, square.at[t], lsem)
+    copies = [remote(item, square.at[t], sems, k, name) for k, name in enumerate(("x", "y", "xy"))]
+    here.start()
+    for copy in copies:
+        copy.start()
+    here.wait()
+    for copy in copies:
+        copy.wait()
+
+
+def every_kernel(square, every, sems, lsem):
+    z = place()[0]
+    here = pltpu.make_async_copy(square, every.at[z], lsem)
+    copies = [remote(square, every.at[z], sems, k, f"z{k + 1}") for k in range(3)]
+    here.start()
+    for copy in copies:
+        copy.start()
+    here.wait()
+    for copy in copies:
+        copy.wait()
+
+
+def finish_kernel(f0, f1, f2, fp, fq, gq_o, gp_o, g1_o, g2_o, mine, theirs, sems):
+    c = place()[1]
+    for f, ref in enumerate((f0, f1, f2)):
+        mine[G1R * f : G1R * (f + 1), :] = ref[:G1R, :].astype(bf16)
+    mine[NF * G1R :, :] = fq[: 7 * DC, :].astype(bf16)
+    copy = remote(mine, theirs, sems, 0, "c")
+    copy.start()
+
+    def place_columns(own, q, first):
+        columns = jnp.concatenate(q, axis=1)
+        for core in range(2):
+
+            @pl.when(c == core)
+            def _():
+                at = core if own else 1 - core
+                for k in range(3):
+                    gq_o[:, DZ * k + DC * at : DZ * k + DC * (at + 1)] = columns[:, DC * k : DC * (k + 1)]
+                for f in range(NF):
+                    start = FF // 8 * at + FZ * f
+                    g1_o[:, start : start + FZ] = jnp.concatenate(first[f], axis=1)
+
+    q = fq[...]
+    place_columns(
+        True,
+        [q[0:DC], q[2 * DC : 3 * DC], q[4 * DC : 5 * DC], q[6 * DC : 7 * DC, : DC // 3]],
+        [[f[:DC, :], f[2 * DC : 3 * DC, : FZ - LANES]] for f in (f0, f1, f2)],
+    )
+    for f, ref in enumerate((f0, f1, f2)):
+        part = ref[G1R:, :]
         tail = part[2 * FZ :]
         tail = jnp.concatenate([tail[:, 32 * k : 32 * (k + 1)] for k in range(4)], axis=0)
         g2_o[FZ * f : FZ * (f + 1), :] = jnp.concatenate([part[:FZ], part[FZ : 2 * FZ], tail], axis=1)
@@ -426,6 +736,17 @@
     tail = part[2 * DC :]
     tail = jnp.concatenate([tail[:, 32 * k : 32 * (k + 1)] for k in range(3)], axis=0)
     gp_o[...] = jnp.concatenate([part[:DC], part[DC : 2 * DC], tail], axis=1)
+    copy.wait()
+    got = theirs[...].astype(f32)
+    q = got[NF * G1R :]
+    place_columns(
+        False,
+        [q[DC : 2 * DC], q[3 * DC : 4 * DC], q[5 * DC : 6 * DC], q[6 * DC :, 64 : 64 + DC // 3]],
+        [
+            [got[G1R * f + DC : G1R * f + 2 * DC], got[G1R * f + 2 * DC : G1R * (f + 1), FZ - LANES :]]
+            for f in range(NF)
+        ],
+    )
 
 
 def make_perm(move):
@@ -449,26 +770,12 @@
     return lax.ppermute(value, BOTH, perm)
 
 
-def reduce_streams(streams):
-    halves = []
-    for kept, sent, first, second in streams:
-        got = send(sent, first)
-        onward = (kept[1].astype(f32) + got[1].astype(f32)).astype(bf16)
-        halves.append((kept[0], got[0], send(onward, second)))
-    sums = [[a[k].astype(f32) + b[k].astype(f32) + c[k].astype(f32) for a, b, c in halves] for k in range(4)]
-    total = jnp.concatenate(sums[0], axis=0)
-    for k in (1, 2, 3):
-        total = total + send(jnp.concatenate([s.astype(bf16) for s in sums[k]], axis=0), PERM_Z[k]).astype(f32)
-    return total
-
-
 def one_item_per_chip(
     tokens, cotangent, timesteps, bucket_ids, head_masks, channel_masks, skip_rows,
     w_qkv, q_bias, v_bias, w_proj, proj_bias, w_fc1, fc1_bias, w_fc2, fc2_bias, ada_weight, ada_bias,
 ):
     b, t = lax.axis_index("bucket"), lax.axis_index("tok")
     z, c, y, x = b // 2, b % 2, t // 2, t % 2
-    sc = jnp.stack([z, c, y, x]).astype(jnp.int32)
     sds = jax.ShapeDtypeStruct
 
     def gather(values):
@@ -476,10 +783,6 @@
         there = lax.dynamic_index_in_dim(values, 1 - x, 0, keepdims=False)
         mine = jnp.concatenate([send(here, PERM_T[0]), send(there, PERM_T[1])], axis=0)
         return jnp.concatenate([mine, send(mine, PERM_C)], axis=0)
-
-    def scatter(values):
-        here, there = send(values[:LB], PERM_T[0]), send(values[LB:], PERM_T[1])
-        return jnp.where(x == 0, jnp.stack([here, there]), jnp.stack([there, here]))
 
     tok = gather(tokens)
     ints = jnp.concatenate([timesteps, bucket_ids, jnp.zeros((13,), jnp.int32), skip_rows.reshape(-1)])
@@ -518,11 +821,11 @@
     qkv_bias = jnp.concatenate([q_bias, jnp.zeros_like(q_bias), v_bias]).astype(f32)
     qkv_bias = core_half(qkv_bias, 12, 2, DC).reshape(1, 3 * WC)
 
-    wq, w1 = call(
+    (wq, w1), _ = call(
         prep_kernel, "prep",
-        (sds((D, 3 * WC), bf16), sds((NF, D, FB), bf16)), (sc, w_qkv, w_fc1),
+        (sds((D, 3 * WC), bf16), sds((NF, D, FB), bf16)), (w_qkv, w_fc1),
         grid=(8,),
-        in_specs=[SMEM, rows(DC, 3 * D), rows(DC, FF)],
+        in_specs=[rows(DC, 3 * D), rows(DC, FF)],
         out_specs=(rows(DC, 3 * WC), pl.BlockSpec((NF, DC, FB), lambda i: (0, i, 0))),
         nbytes=28e6,
     )
@@ -531,7 +834,7 @@
     wp_mine = lax.dynamic_index_in_dim(wp, c, 1, keepdims=False).reshape(WC, D)
     wp_other = lax.dynamic_index_in_dim(wp, 1 - c, 1, keepdims=False).reshape(WC, D)
 
-    shifted, qkv = call(
+    (shifted, qkv), _ = call(
         qkv_kernel, "ln_qkv",
         (sds((L, D), bf16), sds((L, 3 * WC), bf16)), (tok, mod, wq, qkv_bias),
         grid=(4,),
@@ -539,15 +842,16 @@
         out_specs=(rows(LB, D), rows(LB, 3 * WC)),
         flops=2 * L * D * 3 * WC, nbytes=12e6,
     )
-    mixed = call(
+    vmem = pl.BlockSpec(memory_space=pltpu.VMEM)
+    mixed, _ = call(
         functools.partial(attn_kernel, 256), "attn",
         sds((L, WC), bf16), (qkv, head_on),
-        in_specs=[pl.BlockSpec(memory_space=pltpu.VMEM), SMEM],
-        scratch=[pltpu.VMEM((L, HD), bf16)] * 3,
+        in_specs=[vmem, SMEM],
+        scratch=[vm(L, HD)] * 3,
         flops=16e9, nbytes=5e6,
     )
     mixed_other = send(mixed, PERM_C)
-    shifted2, attn = call(
+    (shifted2, attn), _ = call(
         proj_kernel, "proj_ln",
         (sds((L, D), bf16), sds((LH, D), f32)),
         (mixed, mixed_other, wp_mine, wp_other, proj_bias.astype(f32).reshape(1, D), tok, mod),
@@ -558,110 +862,123 @@
         flops=2 * L * D * D, nbytes=12e6,
     )
 
-    mlp_steps = 2
-    block = L // mlp_steps
-    finals, branches, ds2s, sums1 = [], [], [], []
+    firsts, kepts, sums1, results, before = [], [], [], [], []
+    half = pl.BlockSpec((LH, D), lambda i: (1 - i, 0))
+    slot1, slot2 = sds((2, 4, G1R, LANES), bf16), sds((2, 4, G2R, LANES), bf16)
     for f in range(NF):
-        slot1, slot2 = sds((2, 4, G1R, LANES), bf16), sds((2, 4, G2R, LANES), bf16)
-        g1k, g1s, g2k, g2s, branch_f, ds2_f, sum1, sum2 = call(
-            functools.partial(mlp_kernel, mlp_steps), f"mlp{f}",
-            (slot1, slot1, slot2, slot2, sds((L, D), bf16), sds((L, D), bf16), sds((1, FB), f32), sds((1, D), f32)),
-            (sc, shifted2, g_all, kept, mod, w1, b1, chan, w2),
-            grid_spec=pltpu.PrefetchScalarGridSpec(
-                num_scalar_prefetch=1,
-                grid=(mlp_steps,),
-                in_specs=[
-                    prow(block, D), prow(block, D), prow(block, 1), full((8, D)),
-                    pl.BlockSpec((1, D, FB), lambda i, s, f=f: (f, 0, 0)),
-                    pl.BlockSpec((1, 1, FB), lambda i, s, f=f: (f, 0, 0)),
-                    pl.BlockSpec((1, 1, FB), lambda i, s, f=f: (f, 0, 0)),
-                    pl.BlockSpec((4, 1, 1, FZ, D), lambda i, s, f=f: (0, s[1], f, 0, 0)),
-                ],
-                out_specs=(full(slot1.shape), full(slot1.shape), full(slot2.shape), full(slot2.shape),
-                           prow(block, D), prow(block, D), full((1, FB)), full((1, D))),
-                scratch_shapes=[pltpu.VMEM((D, FB), f32), pltpu.VMEM((FB, D), f32),
-                                pltpu.VMEM((4, D, FZ), bf16), pltpu.VMEM((4, FB, TD), bf16)],
-            ),
+        jobs = []
+        if f > 0:
+            jobs.append(FirstSum(*slots))
+        if f > 1:
+            jobs.append(SecondSum(*firsts[f - 2], *kepts[f - 2]))
+        last = f == NF - 1
+        pick = lambda i, f=f: (f, 0, 0)
+        out_shape = [slot1, slot1, slot2, slot2] + [sds((LH if last else L, D), bf16)] * 2
+        out_shape += [sds((1, FB), f32), sds((1, D), f32)] + [sds((LH, D), bf16)] * (2 * last)
+        own, given = call(
+            functools.partial(mlp_kernel, f), f"mlp{f}",
+            out_shape, (shifted2, g_all, kept, mod, w1, b1, chan, w2, *before),
+            grid=(2,),
+            in_specs=[once(L, D), half, pl.BlockSpec((LH, 1), lambda i: (1 - i, 0)), full((8, D)),
+                      pl.BlockSpec((1, D, FB), pick, pipeline_mode=pl.Buffered(1)),
+                      pl.BlockSpec((1, 1, FB), pick), pl.BlockSpec((1, 1, FB), pick), ANY] + [half] * len(before),
+            out_specs=[ANY] * 4 + [full((LH, D)) if last else half] * 2 + [full((1, FB)), full((1, D))]
+            + [ANY] * (2 * last),
+            scratch=[vm(L, FB), vm(L, FB), vm(L, D), vm(4, FZ, D), vm(4, D, FZ), vm(4, FB, TD)]
+            + [vm(*s.shape) for s in (slot1, slot1, slot2, slot2)] + [pltpu.SemaphoreType.DMA((5,))]
+            + ([vm(2, LH, D), pltpu.SemaphoreType.DMA((2, 2))] if last else []),
+            peers=("c",) if last else (), jobs=jobs, cid=f,
             flops=12 * L * D * FB, nbytes=20e6,
         )
-        finals.append(reduce_streams([(g1k, g1s, PERM_X, PERM_Y), (g2k, g2s, PERM_Y, PERM_X)]))
-        branches.append(branch_f)
-        ds2s.append(ds2_f)
-        sums1.append(sum1)
-
-    def far_half(parts):
-        return sum(p[LH:].astype(f32) for p in parts).astype(bf16)
-
-    ds2_r = send(far_half(ds2s), PERM_C)
-    branch_r = send(far_half(branches), PERM_C)
-    row = rows(LB, D)
-    d_resid, d_attn, out_rows, sums_mid = call(
-        mid_kernel, "mid",
-        (sds((LH, D), f32), sds((LH, D), bf16), sds((LH, D), bf16), sds((8, D), f32)),
-        (*ds2s, ds2_r, *branches, branch_r, attn, tok, g_all, kept, mod, fc2_bias.astype(f32).reshape(1, D)),
-        grid=(2,),
-        in_specs=[row] * 8 + [row, row, row, rows(LB, 1), full((8, D)), full((1, D))],
-        out_specs=(row, row, row, full((8, D))),
-        nbytes=20e6,
-    )
-    output = scatter(out_rows)
-    d_attn_other = send(d_attn, PERM_C)
-    slotp = sds((2, 4, PR, LANES), bf16)
-    dh, pk, ps, sum_attn = call(
-        heads_kernel, "heads_back",
-        (sds((L, WC), bf16), slotp, slotp, sds((1, D), f32)),
-        (sc, d_attn, d_attn_other, mixed, wp_mine),
-        in_specs=[SMEM] + [pl.BlockSpec(memory_space=pltpu.VMEM)] * 4,
-        scratch=[pltpu.VMEM((4, WC, TD), bf16)],
-        flops=4 * L * D * WC, nbytes=10e6,
-    )
-    final_p = reduce_streams([(pk, ps, PERM_Y, PERM_X)])
-    dqkv = call(
+        slots, before = own[:4], own[4:6]
+        kepts.append((slots[0], slots[2]))
+        sums1.append(own[6])
+        if f > 0:
+            firsts.append(given[0])
+        if f > 1:
+            results.append(given[1])
+    sum2 = own[7]
+    branch_r, ds2_r = own[8:]
+
+    n = LH // 4
+    row = rows(n, D)
+    slot_a, slot_b = sds((2, 4, PA, LANES), bf16), sds((2, 4, PR - PA, LANES), bf16)
+    own, given = call(
+        middle_kernel, "middle",
+        (sds((LH, D), f32), sds((2, LB, D), bf16), sds((L, WC), bf16), slot_a, slot_a, slot_b, slot_b,
+         sds((8, D), f32), sds((8, D), f32)),
+        (before[1], ds2_r, before[0], branch_r, attn, tok, g_all, kept, mod, fc2_bias.astype(f32).reshape(1, D),
+         mixed, wp_mine),
+        grid=(4,),
+        in_specs=[row] * 7 + [rows(n, 1), full((8, D)), full((1, D)), once(L, WC), once(WC, D)],
+        out_specs=(row, ANY, full((L, WC)), full(slot_a.shape), full(slot_a.shape), full(slot_b.shape),
+                   full(slot_b.shape), full((8, D)), full((8, D))),
+        scratch=[vm(L, D), vm(LH, D), vm(4, WC, TD), pltpu.SemaphoreType.DMA((2, 4)), pltpu.SemaphoreType.DMA((2, 2)),
+                 pltpu.SemaphoreType.DMA],
+        peers=("c", "t0", "t1"), cid=3,
+        jobs=[FirstSum(*slots), SecondSum(*firsts[1], *kepts[1]), ThirdSum(*results[0])],
+        flops=4 * L * D * WC, nbytes=20e6,
+    )
+    d_resid, output, dh, *slots_p, sums_mid, sum_attn = own
+    firsts.append(given[0])
+    results.append(given[1])
+    finals = [given[2][0]]
+    dqkv, given = call(
         functools.partial(attn_back_kernel, 512), "attn_back",
         sds((L, 3 * WC), bf16), (qkv, dh, head_on),
-        in_specs=[pl.BlockSpec(memory_space=pltpu.VMEM)] * 2 + [SMEM],
-        scratch=[pltpu.VMEM((L, HD), bf16)] * 4 + [pltpu.VMEM((L, HD), f32)] * 3,
+        in_specs=[vmem, vmem, SMEM],
+        scratch=[vm(L, HD)] * 4 + [vm(L, HD, dtype=f32)] * 3,
+        cid=4, jobs=[FirstSum(*slots_p), SecondSum(*firsts[2], *kepts[2]), ThirdSum(*results[1])],
         flops=30e9, nbytes=9e6,
     )
+    first_p = given[0]
+    results.append(given[1])
+    finals.append(given[2][0])
     sum_fc1 = jnp.concatenate(sums1, axis=0).reshape(NF, 4, FZ).transpose(1, 0, 2).reshape(4, 4, FF // 32)
-    own = lambda v: core_half(v, 4, 2, 4, D // 32)
-    sum_fc2, sum_attn = own(sum2), own(sum_attn)
+    own_part = lambda v: core_half(v, 4, 2, 4, D // 32)
     line = jnp.concatenate(
-        [sum_fc1, sum_fc2, sum_attn, jnp.zeros((4, 4, 3 * LANES - FF // 32 - D // 16), f32)], axis=2
+        [sum_fc1, own_part(sum2), own_part(sum_attn[0]), jnp.zeros((4, 4, 3 * LANES - FF // 32 - D // 16), f32)], axis=2
     ).reshape(4, 4, 3, LANES)
     extra = jnp.concatenate([line, jnp.zeros((4, 4, 13, LANES), f32)], axis=2)
-    slota, slotb = sds((2, 4, QA, LANES), bf16), sds((2, 4, QB_ROWS, LANES), bf16)
-    ak, as_, bk, bs = call(
+    slot_q = sds((2, 4, QA, LANES), bf16)
+    slots_q, given = call(
         qkv_grad_kernel, "qkv_grad",
-        (slota, slota, slotb, slotb), (sc, shifted, dqkv, extra),
-        in_specs=[SMEM] + [pl.BlockSpec(memory_space=pltpu.VMEM)] * 3,
-        scratch=[pltpu.VMEM((4, D, 3 * DC), bf16)],
+        (slot_q,) * 4, (shifted, dqkv, extra),
+        scratch=[vm(4, D, 3 * DC)],
+        cid=5, jobs=[SecondSum(*first_p, slots_p[0], slots_p[2]), ThirdSum(*results[2])],
         flops=2 * L * D * 3 * WC, nbytes=12e6,
     )
-    final_q = reduce_streams([(ak, as_, PERM_X, PERM_Y), (bk, bs, PERM_Y, PERM_X)])
-    d_shifted = call(
-        back_kernel, "qkv_back",
-        sds((L, D), bf16), (dqkv, wq),
-        grid=(2,),
-        in_specs=[rows(LH, 3 * WC), full((D, 3 * WC))],
-        out_specs=rows(LH, D),
+    result_p = given[0]
+    finals.append(given[1][0])
+    near = pl.BlockSpec((LB, D), lambda i: (jnp.maximum(i - 2, 0), 0))
+    (grad_rows, item), given = call(
+        tail_kernel, "tail",
+        (sds((2, LB, D), bf16), sds((8, D), f32)),
+        (dqkv, wq, d_resid, tok, mod, sums_mid),
+        grid=(4,),
+        in_specs=[pl.BlockSpec((LB, 3 * WC), lambda i: ((i + 2) % 4, 0)), once(D, 3 * WC), near, near, full((8, D)),
+                  full((8, D))],
+        out_specs=(ANY, full((8, D))),
+        scratch=[vm(2, LB, D), vm(2, LB, D), vm(2, LB, D), vm(8, D, dtype=f32), pltpu.SemaphoreType.DMA((2, 3)),
+                 pltpu.SemaphoreType.DMA((2, 2)), pltpu.SemaphoreType.DMA],
+        peers=("c", "t0", "t1"), cid=6, jobs=[FirstSum(*slots_q), ThirdSum(*result_p)],
         flops=2 * L * D * 3 * WC, nbytes=12e6,
     )
-    d_shifted_r = send(d_shifted[LH:], PERM_C)
-    grad_rows, sums_last = call(
-        last_kernel, "last",
-        (sds((LH, D), bf16), sds((8, D), f32)),
-        (d_shifted, d_shifted_r, d_resid, tok, mod),
-        grid=(2,),
-        in_specs=[row, row, row, row, full((8, D))],
-        out_specs=(row, full((8, D))),
-        nbytes=10e6,
-    )
-    grad_tokens = scatter(grad_rows).astype(f32)
-
-    mine = jnp.concatenate([sums_last[:2], sums_mid[:4]], axis=0).reshape(1, 6 * D)
-    every = lax.all_gather(mine, BOTH, axis=0, tiled=True)
-    every = every.reshape(4, 2, 4, 6 * D).sum(axis=1).reshape(16, 6 * D)
+    first_q, final_p = given[0], given[1][0]
+    grad_tokens = grad_rows.astype(f32)
+    square, given = call(
+        square_kernel, "square", sds((4, 8, D), f32), (item,),
+        scratch=[pltpu.SemaphoreType.DMA((2, 3)), pltpu.SemaphoreType.DMA],
+        peers=("x", "y", "xy"), cid=7, jobs=[SecondSum(*first_q, slots_q[0], slots_q[2])],
+    )
+    every, given = call(
+        every_kernel, "every", sds((4, 4, 8, D), f32), (square,),
+        scratch=[pltpu.SemaphoreType.DMA((2, 3)), pltpu.SemaphoreType.DMA],
+        peers=("z1", "z2", "z3"), cid=8, jobs=[ThirdSum(*given[0])],
+    )
+    final_q = given[0][0]
+
+    every = every.reshape(16, 8, D)[:, :6].reshape(16, 6 * D)
     ada_cols = ada_weight.shape[1]
     cond_all = jax.nn.silu(step_embedding(every_step, D)).astype(bf16).astype(f32)
     cond_rows = lax.dynamic_slice_in_dim(cond_all, b * DC, DC, 1)
@@ -672,14 +989,12 @@
     bias_cols = 6 * D // 8
     grad_ada_bias = jnp.sum(lax.dynamic_slice_in_dim(every, b * bias_cols, bias_cols, 1), axis=0)
 
-    other = send(jnp.concatenate([f[:G1R].astype(bf16) for f in finals] + [final_q[: 7 * DC].astype(bf16)], axis=0), PERM_C)
-    others = [other[G1R * f : G1R * (f + 1)] for f in range(NF)]
-    gq, gp, g1, g2 = call(
+    (gq, gp, g1, g2), _ = call(
         finish_kernel, "finish",
         (sds((DC, 3 * TD), f32), sds((DC, TD), f32), sds((DC, FF // 4), f32), sds((FF // 8, TD), f32)),
-        (sc, *finals, final_p, final_q, *others, other[NF * G1R :]),
-        in_specs=[SMEM] + [pl.BlockSpec(memory_space=pltpu.VMEM)] * 9,
-        nbytes=6e6,
+        (*finals, final_p, final_q),
+        scratch=[vm(NF * G1R + 7 * DC, LANES), vm(NF * G1R + 7 * DC, LANES), pltpu.SemaphoreType.DMA((2, 1))],
+        peers=("c",), cid=9, nbytes=6e6,
     )
     line = final_q[7 * DC :].reshape(-1)
     n1, n = FF // 32, D // 32

time: 636 us -> 486 us (0.76)
  Pallas kernels: 229 us -> 390 us
  waiting for transfers between devices: 122 us -> 4.41 us
  blocking collectives: 86 us -> 9.17 us
  starting transfers between devices: 85.9 us -> 15.8 us
  other arithmetic: 48.5 us -> 12.8 us
  local copies, waits for them, and re-layouts: 49.7 us -> 39 us
    pallas_call x14, Pallas kernels: 229 us -> 390 us  [call(): pl.pallas_call(run, out_shape=out_shape + [o for j in jobs for o in j.out...]
    ppermute x53 -> x11, waiting for transfers between devices: 122 us -> 4.41 us  [send(): return lax.ppermute(value, BOTH, perm)]
    all_gather x1 -> x0, blocking collectives: 76.9 us -> none  [one_item_per_chip(): every = lax.all_gather(mine, BOTH, axis=0, tiled=True)]
    ppermute x53 -> x11, starting transfers between devices: 85.9 us -> 15.8 us  [send(): return lax.ppermute(value, BOTH, perm)]
    convert_element_type x21 -> x1, other arithmetic: 29.6 us -> 1.57 us  [one_item_per_chip(): grad_tokens = grad_rows.astype(f32)]
    slice x11 -> x1, local copies, waits for them, and re-layouts: 11.2 us -> 0.79 us  [one_item_per_chip(): sum_attn[0]]
    unnamed x139 -> x81, local copies, waits for them, and re-layouts: 12.7 us -> 9.42 us
  transfers between devices with their start and end apart: 53 -> 11, of which waited for: 13 -> 1; matrix products, arithmetic and copies ran while one was open for 14% -> 7% of each run, Pallas kernels for 23% -> 11%
where the time goes in v2:
time: 486 us; the launch traced here: 481 us
  Pallas kernels  390 us (80%)
  local copies, waits for them, and re-layouts  39 us (8%)
  starting transfers between devices  15.8 us (3%)
  other arithmetic  12.8 us (3%)
  blocking collectives  9.17 us (2%)
  matrix products  4.96 us (1%)
    pallas_call x14, Pallas kernels, call(): pl.pallas_call(run, out_shape=out_shape + [o for j in jobs for o in j.out...  390 us
    ppermute x11, starting transfers between devices, send(): return lax.ppermute(value, BOTH, perm)  15.8 us
  transfers between devices with their start and end apart: 11, of which 1 were waited for; matrix products, arithmetic and copies ran while one was open for 7% of the time, Pallas kernels for 11%

profile of v2, /device:TPU:0, one launch (start us, length us, event | category | flops | bytes accessed | tf_op | source)
XLA Modules:
  0.0 480.8 jit_solution(12223581375580482879)
XLA Ops:
  0.8 2.5 dynamic-slice_bitcast_fusion.2
  5.0 2.9 collective-permute-start.1
  12.8 2.3 dynamic-slice_bitcast_fusion
  17.0 9.2 %all-reduce.2 = s32[16]{0:T(128)S(1)} all-reduce(s32[16]{0:T(128)S(1)} %dynamic-update-slice), channel_id=1, replica_groups=mesh['bucket'=8,'tok'=4] {'bucket'}, use_global_device_ids=true, to_apply=%add.2 | all-reduce | flops 16 | bytes 128
  30.6 12.6 %prep.1 = (bf16[1152,1728]{1,0:T(8,128)(2,1)}, bf16[3,1152,768]{2,1,0:T(8,128)(2,1)}) custom-call(bf16[1152,3456]{1,0:T(8,128)(2,1)} %refs_0_.1, bf16[1152,4608]{1,0:T(8,128)(2,1)} %refs_1_.1), custom_call_target="tpu_custom_call" | custom-call | bytes 28000000 | tf_op jit(solution)/shard_map/prep/pallas_call | solution.py:282
  44.8 3.3 convolution_add_fusion
  60.0 2.2 pad_maximum_fusion
  68.4 4.4 collective-permute-done.9
  78.6 10.3 %ln_qkv.1 = (bf16[1024,1152]{1,0:T(8,128)(2,1)}, bf16[1024,1728]{1,0:T(8,128)(2,1)}) custom-call(bf16[1024,1152]{1,0:T(8,128)(2,1)} %copy-done, f32[8,1152]{1,0:T(8,128)} %concatenate.67.refs_1_.refs_6_.refs_3_.refs_8_.refs_4_, bf16[1152,1728]{1,0:T(8,128)(2,1)} %get-tuple-element.100.refs_2_.refs_1_, f32[1,1728]{1,0:T(1,128)} %reshape.231.refs_3_), custom_call_target="tpu_custom_call" | custom-call | flops 4076863488 | bytes 12000000 | tf_op jit(solution)/shard_map/ln_qkv/pallas_call | solution.py:282
  88.9 29.2 %attn.1.refs_0_.refs_10_ = bf16[1024,576]{1,0:T(8,128)(2,1)} custom-call(bf16[1024,1728]{1,0:T(8,128)(2,1)} %get-tuple-element.101.refs_0_, f32[8]{0:T(128)} %reshape.232.refs_1_.refs_2_), custom_call_target="tpu_custom_call" | custom-call | flops 16000000000 | bytes 5000000 | tf_op jit(solution)/shard_map/attn/pallas_call | solution.py:282
  118.1 2.5 copy.68
  124.8 3.2 copy.71.refs_1_
  128.1 9.9 %proj_ln.1 = (bf16[1024,1152]{1,0:T(8,128)(2,1)}, f32[512,1152]{1,0:T(8,128)}) custom-call(bf16[1024,576]{1,0:T(8,128)(2,1)} %attn.1.refs_0_.refs_10_, bf16[1024,576]{1,0:T(8,128)(2,1)} %copy.71.refs_1_, bf16[576,1152]{1,0:T(8,128)(2,1)} %bitcast.58, bf16[576,1152]{1,0:T(8,128)(2,1)} %bitcast.61, f32[1,1152]{1,0:T(1,128)} %reshape.253.refs_4_, ...), custom_call_target="tpu_custom_call" | custom-call | flops 2717908992 | bytes 12000000 | tf_op jit(solution)/shard_map/proj_ln/pallas_call | solution.py:282
  137.9 21.5 %mlp0.1 = (bf16[2,4,432,128]{3,2,1,0:T(8,128)(2,1)}, bf16[2,4,432,128]{3,2,1,0:T(8,128)(2,1)}, bf16[2,4,432,128]{3,2,1,0:T(8,128)(2,1)}, bf16[2,4,432,128]{3,2,1...) custom-call(bf16[1024,1152]{1,0:T(8,128)(2,1)} %get-tuple-element.10, ...), custom_call_target="tpu_custom_call" | custom-call | flops 10871635968 | bytes 20000000 | tf_op jit(solution)/shard_map/mlp0/pallas_call | solution.py:282
  159.4 28.8 %mlp1.1 = (bf16[2,4,432,128]{3,2,1,0:T(8,128)(2,1)}, bf16[2,4,432,128]{3,2,1,0:T(8,128)(2,1)}, bf16[2,4,432,128]{3,2,1,0:T(8,128)(2,1)}, bf16[2,4,432,128]{3,2,1...) custom-call(bf16[1024,1152]{1,0:T(8,128)(2,1)} %get-tuple-element.10, ...), custom_call_target="tpu_custom_call" | custom-call | flops 10871635968 | bytes 20000000 | tf_op jit(solution)/shard_map/mlp1/pallas_call | solution.py:282
  188.3 38.3 %mlp2.1 = (bf16[2,4,432,128]{3,2,1,0:T(8,128)(2,1)}, bf16[2,4,432,128]{3,2,1,0:T(8,128)(2,1)}, bf16[2,4,432,128]{3,2,1,0:T(8,128)(2,1)}, bf16[2,4,432,128]{3,2,1...) custom-call(bf16[1024,1152]{1,0:T(8,128)(2,1)} %get-tuple-element.10, ...), custom_call_target="tpu_custom_call" | custom-call | flops 10871635968 | bytes 20000000 | tf_op jit(solution)/shard_map/mlp2/pallas_call | solution.py:282
  227.5 51.5 %middle.1 = (f32[512,1152]{1,0:T(8,128)}, bf16[2,256,1152]{2,1,0:T(8,128)(2,1)}, bf16[1024,576]{1,0:T(8,128)(2,1)}, bf16[2,4,176,128]{3,2,1,0:T(8,128)(2,1)}, bf...) custom-call(bf16[512,1152]{1,0:T(8,128)(2,1)} %get-tuple-element.120, ...), custom_call_target="tpu_custom_call" | custom-call | flops 2717908992 | bytes 20000000 | tf_op jit(solution)/shard_map/middle/pallas_call | solution.py:282
  280.8 52.4 %attn_back.1 = (bf16[1024,1728]{1,0:T(8,128)(2,1)}, bf16[4,176,128]{2,1,0:T(8,128)(2,1)}, bf16[4,176,128]{2,1,0:T(8,128)(2,1)}, bf16[4,160,128]{2,1,0:T(8,128)(2...) custom-call(bf16[1024,1728]{1,0:T(8,128)(2,1)} %get-tuple-element.10, ...), custom_call_target="tpu_custom_call" | custom-call | flops 30000001024 | bytes 9000000 | tf_op jit(solution)/shard_map/attn_back/pallas_call | solution.py:282
  333.2 29.0 %qkv_grad.1 = (bf16[2,4,512,128]{3,2,1,0:T(8,128)(2,1)}, bf16[2,4,512,128]{3,2,1,0:T(8,128)(2,1)}, bf16[2,4,512,128]{3,2,1,0:T(8,128)(2,1)}, bf16[2,4,512,128]{3...) custom-call(bf16[1024,1152]{1,0:T(8,128)(2,1)} %get-tuple-element.150.refs_0_, ...), custom_call_target="tpu_custom_call" | custom-call | flops 4076863488 | bytes 12000000 | tf_op jit(solution)/shard_map/qkv_grad/pallas_call | solution.py:282
  362.2 43.0 %tail.1 = (bf16[2,256,1152]{2,1,0:T(8,128)(2,1)}, f32[8,1152]{1,0:T(8,128)}, bf16[4,512,128]{2,1,0:T(8,128)(2,1)}, bf16[4,512,128]{2,1,0:T(8,128)(2,1)}, bf16[4,...) custom-call(bf16[1024,1728]{1,0:T(8,128)(2,1)} %get-tuple-element.147.refs_1_.refs_0_, ...), custom_call_target="tpu_custom_call" | custom-call | flops 4076863488 | bytes 12000000 | tf_op jit(solution)/shard_map/tail/pallas_call | solution.py:282
  405.3 19.6 %square.1 = (f32[4,8,1152]{2,1,0:T(8,128)}, bf16[3,1024,128]{2,1,0:T(8,128)(2,1)}, f32[1024,128]{1,0:T(8,128)}) custom-call(f32[8,1152]{1,0:T(8,128)} %get-tuple-element.173.refs_0_, bf16[4,512,128]{2,1,0:T(8,128)(2,1)} %get-tuple-element.174.refs_1_, bf16[4,512,128]{2,1,0:T(8,128)(2,1)} %get-tuple-element.175.refs_2_, ...), custom_call_target="tpu_custom_call" | custom-call | tf_op jit(solution)/shard_map/square/pallas_call | solution.py:282
  424.9 38.5 %every.1 = (f32[4,4,8,1152]{3,2,1,0:T(8,128)}, f32[1024,128]{1,0:T(8,128)}) custom-call(f32[4,8,1152]{2,1,0:T(8,128)} %get-tuple-element.178.refs_0_, bf16[3,1024,128]{2,1,0:T(8,128)(2,1)} %get-tuple-element.179.refs_1_, f32[1024,128]{1,0:T(8,128)} %get-tuple-element.180.refs_2_), custom_call_target="tpu_custom_call" | custom-call | tf_op jit(solution)/shard_map/every/pallas_call | solution.py:282
  465.4 5.4 %finish.1 = (f32[144,864]{1,0:T(8,128)}, f32[144,288]{1,0:T(8,128)}, f32[144,1152]{1,0:T(8,128)}, f32[576,288]{1,0:T(8,128)}) custom-call(f32[864,128]{1,0:T(8,128)} %get-tuple-element.169.refs_0_, f32[864,128]{1,0:T(8,128)} %get-tuple-element.170.refs_1_, f32[864,128]{1,0:T(8,128)} %get-tuple-element.171.refs_2_, f32[336,128]{1,0:T(8,128)} %get-tuple-element.172.refs_3_, ...), custom_call_target="tpu_custom_call" | custom-call | bytes 6000000 | tf_op jit(solution)/shard_map/finish/pallas_call | solution.py:282
  470.7 2.3 copy.80
  (175 shorter events, 51.4 us)
Async XLA Ops:
  0.7 10.5 %copy-start.22 = (bf16[1728]{0:T(1024)(128)(2,1)S(1)}, bf16[1728]{0:T(1024)(128)(2,1)}, u32[]{:S(2)}) copy-start(bf16[1728]{0:T(1024)(128)(2,1)} %param.35) | copy-start | bytes 10372
  0.7 11.1 %copy-start.23 = (bf16[1152]{0:T(1024)(128)(2,1)S(1)}, bf16[1152]{0:T(1024)(128)(2,1)}, u32[]{:S(2)}) copy-start(bf16[1152]{0:T(1024)(128)(2,1)} %param.26) | copy-start | bytes 6916
  0.7 11.2 %copy-start.24 = (bf16[1152]{0:T(1024)(128)(2,1)S(1)}, bf16[1152]{0:T(1024)(128)(2,1)}, u32[]{:S(2)}) copy-start(bf16[1152]{0:T(1024)(128)(2,1)} %param.27) | copy-start | bytes 6916
  0.7 14.6 %copy-start.17 = (bf16[4608]{0:T(1024)(128)(2,1)S(1)}, bf16[4608]{0:T(1024)(128)(2,1)}, u32[]{:S(2)}) copy-start(bf16[4608]{0:T(1024)(128)(2,1)} %param.31) | copy-start | bytes 27652
  0.7 14.7 %copy-start.32 = (u32[32]{0:T(128)S(1)}, u32[32]{0:T(128)}, u32[]{:S(2)}) copy-start(u32[32]{0:T(128)} %constant.162) | copy-start | bytes 388
  0.7 25.4 %copy-start.2 = (bf16[1152,1152]{1,0:T(8,128)(2,1)S(1)}, bf16[1152,1152]{1,0:T(8,128)(2,1)}, u32[]{:S(2)}) copy-start(bf16[1152,1152]{1,0:T(8,128)(2,1)} %param.28) | copy-start | bytes 7962628
  3.3 56.7 %collective-permute-start = (bf16[256,1152]{1,0:T(8,128)(2,1)}, bf16[256,1152]{1,0:T(8,128)(2,1)S(1)}, u32[]{:S(2)}, u32[]{:S(2)}) collective-permute-start(bf16[256,1152]{1,0:T(8,128)(2,1)} %get-tuple-element.260), channel_id=1, source_target_pairs={{0,0},{1,1},{2,4},{3,5},{4,2},{5,3},{6,6},{7,7},{8,8},{9,9},{10,12... | collective-permute-start | bytes 1769480 | tf_op jit(solution)/shard_map/ppermute | solution.py:770
  5.0 55.0 %collective-permute-start.1 = (bf16[256,1152]{1,0:T(8,128)(2,1)}, bf16[256,1152]{1,0:T(8,128)(2,1)}, u32[]{:S(2)}, u32[]{:S(2)}) collective-permute-start(bf16[256,1152]{1,0:T(8,128)(2,1)} %get-tuple-element.259), channel_id=1, source_target_pairs={{0,1},{1,0},{2,5},{3,4},{4,3},{5,2},{6,7},{7,6},{8,9},{9,8},{10,13... | collective-permute-start | bytes 1769480 | tf_op jit(solution)/shard_map/ppermute | solution.py:770
  9.3 34.6 %collective-permute-start.3 = (s32[528]{0:T(1024)}, s32[528]{0:T(1024)}, u32[]{:S(2)}, u32[]{:S(2)}) collective-permute-start(s32[528]{0:T(1024)} %pad_add_fusion), channel_id=1, source_target_pairs={{0,4},{1,5},{2,6},{3,7},{4,0},{5,1},{6,2},{7,3},{8,12},{9,13},{10,... | collective-permute-start | bytes 6344 | tf_op jit(solution)/shard_map/ppermute | solution.py:770
  30.6 13.9 %copy-start.21 = (s32[2]{0:T(128)S(1)}, s32[2]{0:T(128)}, u32[]{:S(2)}) copy-start(s32[2]{0:T(128)} %param.20) | copy-start | bytes 28
  43.2 14.7 %copy-start.11 = (bf16[256,1152]{1,0:T(8,128)(2,1)S(1)}, bf16[256,1152]{1,0:T(8,128)(2,1)}, u32[]{:S(2)}) copy-start(bf16[256,1152]{1,0:T(8,128)(2,1)} %get-tuple-element.257) | copy-start | bytes 1769476
  48.2 8.0 %collective-permute-start.4 = (f32[1728]{0:T(1024)S(1)}, f32[1728]{0:T(1024)S(1)}, u32[]{:S(2)}, u32[]{:S(2)}) collective-permute-start(f32[1728]{0:T(1024)S(1)} %get-tuple-element.252), channel_id=1, source_target_pairs={{0,1},{1,0},{2,3},{3,2},{4,5},{5,4},{6,7},{7,6},{8,9},{9,8},{10,11... | collective-permute-start | bytes 20744 | tf_op jit(solution)/shard_map/ppermute | solution.py:770
  48.8 9.1 %collective-permute-start.5 = (f32[1728]{0:T(1024)S(1)}, f32[1728]{0:T(1024)S(1)}, u32[]{:S(2)}, u32[]{:S(2)}) collective-permute-start(f32[1728]{0:T(1024)S(1)} %get-tuple-element.254), channel_id=1, source_target_pairs={{0,2},{1,3},{2,0},{3,1},{4,6},{5,7},{6,4},{7,5},{8,10},{9,11},{10,... | collective-permute-start | bytes 20744 | tf_op jit(solution)/shard_map/ppermute | solution.py:770
  50.4 8.2 %collective-permute-start.6 = (f32[1728]{0:T(1024)S(1)}, f32[1728]{0:T(1024)S(1)}, u32[]{:S(2)}, u32[]{:S(2)}) collective-permute-start(f32[1728]{0:T(1024)S(1)} %get-tuple-element.253), channel_id=1, source_target_pairs={{0,3},{1,2},{2,1},{3,0},{4,7},{5,6},{6,5},{7,4},{8,11},{9,10},{10,... | collective-permute-start | bytes 20744 | tf_op jit(solution)/shard_map/ppermute | solution.py:770
  56.2 12.2 %collective-permute-start.8 = (bf16[256,1152]{1,0:T(8,128)(2,1)}, bf16[256,1152]{1,0:T(8,128)(2,1)S(1)}, u32[]{:S(2)}, u32[]{:S(2)}) collective-permute-start(bf16[256,1152]{1,0:T(8,128)(2,1)} %get-tuple-element.258), channel_id=1, source_target_pairs={{0,0},{1,1},{2,4},{3,5},{4,2},{5,3},{6,6},{7,7},{8,8},{9,9},{10,12... | collective-permute-start | bytes 1769480 | tf_op jit(solution)/shard_map/ppermute | solution.py:770
  57.9 14.8 %collective-permute-start.9 = (bf16[256,1152]{1,0:T(8,128)(2,1)S(1)}, bf16[256,1152]{1,0:T(8,128)(2,1)S(1)}, u32[]{:S(2)}, u32[]{:S(2)}) collective-permute-start(bf16[256,1152]{1,0:T(8,128)(2,1)S(1)} %copy-done.11), channel_id=1, source_target_pairs={{0,1},{1,0},{2,5},{3,4},{4,3},{5,2},{6,7},{7,6},{8,9},{9,8},{10,13... | collective-permute-start | bytes 1769480 | tf_op jit(solution)/shard_map/ppermute | solution.py:770
  62.1 14.9 %collective-permute-start.2 = (bf16[512,1152]{1,0:T(8,128)(2,1)}, bf16[512,1152]{1,0:T(8,128)(2,1)S(1)}, u32[]{:S(2)}, u32[]{:S(2)}) collective-permute-start(bf16[512,1152]{1,0:T(8,128)(2,1)} %pad_maximum_fusion), channel_id=1, source_target_pairs={{0,4},{1,5},{2,6},{3,7},{4,0},{5,1},{6,2},{7,3},{8,12},{9,13},{10,... | collective-permute-start | bytes 3538952 | tf_op jit(solution)/shard_map/ppermute | solution.py:770
  74.0 49.3 %collective-permute-start.10 = (bf16[512,1152]{1,0:T(8,128)(2,1)}, bf16[512,1152]{1,0:T(8,128)(2,1)}, u32[]{:S(2)}, u32[]{:S(2)}) collective-permute-start(bf16[512,1152]{1,0:T(8,128)(2,1)} %pad_maximum_fusion.1), channel_id=1, source_target_pairs={{0,4},{1,5},{2,6},{3,7},{4,0},{5,1},{6,2},{7,3},{8,12},{9,13},{10,... | collective-permute-start | bytes 3538952 | tf_op jit(solution)/shard_map/ppermute | solution.py:770
  120.6 4.3 collective-permute-start.7
  124.8 13.1 %copy-start.1 = (bf16[1024,1152]{1,0:T(8,128)(2,1)}, bf16[1024,1152]{1,0:T(8,128)(2,1)S(1)}, u32[]{:S(2)}) copy-start(bf16[1024,1152]{1,0:T(8,128)(2,1)S(1)} %constant_dynamic-update-slice_fusion.3.refs_1_.refs_6_) | copy-start | bytes 7077892
  188.3 38.3 %copy-start.27 = (f32[1,768]{1,0:T(1,128)S(1)}, f32[1,768]{1,0:T(1,128)}, u32[]{:S(2)}) copy-start(f32[1,768]{1,0:T(1,128)} %get-tuple-element.151) | copy-start | bytes 9220
  188.3 38.3 %copy-start.28 = (f32[1,768]{1,0:T(1,128)S(1)}, f32[1,768]{1,0:T(1,128)}, u32[]{:S(2)}) copy-start(f32[1,768]{1,0:T(1,128)} %get-tuple-element.152) | copy-start | bytes 9220
  227.4 52.4 %copy-start.19 = (f32[1,1152]{1,0:T(1,128)S(1)}, f32[1,1152]{1,0:T(1,128)}, u32[]{:S(2)}) copy-start(f32[1,1152]{1,0:T(1,128)} %get-tuple-element.154) | copy-start | bytes 13828
  227.4 52.6 %copy-start.18 = (f32[384]{0:T(512)S(1)}, f32[384]{0:T(512)}, u32[]{:S(2)}) copy-start(f32[384]{0:T(512)} %pad.7.clone) | copy-start | bytes 4612
  (20 other events, 105.8 us)

commit v3 on v2

--- a/solution.py
+++ b/solution.py
@@ -14,7 +14,6 @@
 GELU_K = math.sqrt(2.0 / math.pi)
 GELU_C = 0.044715
 LANES = 128
-BOTH = ("bucket", "tok")
 bf16, f32 = jnp.bfloat16, jnp.float32
 
 
@@ -297,9 +296,6 @@
     return (own[0] if single else own), given
 
 
-SMEM = pl.BlockSpec(memory_space=pltpu.SMEM)
-
-
 def full(shape):
     return pl.BlockSpec(shape, lambda *_: (0,) * len(shape))
 
@@ -312,62 +308,216 @@
     return pl.BlockSpec((block, width), lambda i: (i, 0))
 
 
-def prep_kernel(wq, w1, wq_o, w1_o):
-    c = place()[1]
+def column(n):
+    return lax.broadcasted_iota(jnp.int32, (n, 1), 0)
+
+
+def front_kernel(tokens, cotangent, ints, ada_w, ada_b, freq, heads_t, channels_t, w_qkv, w_fc1, q_bias, v_bias, b1,
+                 tok_o, cot_o, shifted_o, qkv_o, wq_o, w1_o, mod_o, kept_o, hmask_o, chan_o, b1_o,
+                 tk, ck, wqv, wqc, w1v, w1c, adav, ints_other, m4, to_send, shares, csems, tsems, ssems, lsems):
+    z, c, y, x = place()
+    t = 2 * y + x
+    loads = [
+        pltpu.make_async_copy(a, b, lsems.at[k])
+        for k, (a, b) in enumerate(((ada_w, adav), (w_qkv, wqv), (w_fc1, w1v)))
+    ]
+
+    def arrivals(src, dst, k):
+        block = [dst.at[pl.ds(LB * j, LB)] for j in range(4)]
+        first = remote(src.at[x], block[0], tsems, k, "t0")
+        stay = pltpu.make_async_copy(src.at[x], block[0], lsems.at[3 + k])
+        second = remote(src.at[1 - x], block[1], tsems, 2 + k, "t1")
+        onward = [remote(block[j], block[2 + j], csems, 2 * k + j, "c") for j in range(2)]
+        return first, stay, second, onward
+
+    def leave(first, stay, second, onward):
+        pl.when(c != y)(first.start)
+        pl.when(c == y)(stay.start)
+        second.start()
+
+    def pass_on(first, stay, second, onward):
+        pl.when(c != y)(first.wait_recv)
+        pl.when(c == y)(stay.wait)
+        onward[0].start()
+        second.wait_recv()
+        onward[1].start()
+
+    def settle(first, stay, second, onward):
+        pl.when(c != y)(first.wait_send)
+        second.wait_send()
+        for copy in onward:
+            copy.wait_send()
+
+    tok_moves, cot_moves = arrivals(tokens, tk, 0), arrivals(cotangent, ck, 1)
+    leave(*tok_moves)
+    swap = remote(ints, ints_other, csems, 4, "c")
+    swap.start()
+    for load in loads:
+        load.start()
+    swap.wait()
+
+    mine, other = ints[...], ints_other[...]
+    mine_t, other_t = mine[4:5, :].astype(f32), other[4:5, :].astype(f32)
+    r = column(8)
+    steps = jnp.zeros((8, 1), f32)
+    for k in range(2):
+        steps = jnp.where(r == 2 * c + k, mine_t[:, k : k + 1], steps)
+        steps = jnp.where(r == 2 * (1 - c) + k, other_t[:, k : k + 1], steps)
+    angles = steps * freq[...]
+    condition = jax.nn.silu(jnp.concatenate([jnp.cos(angles), jnp.sin(angles)], axis=1))
+    condition = jnp.concatenate([condition, jnp.zeros_like(condition)], axis=0).astype(bf16)
+    loads[0].wait()
+    m4[...] = dot_nn(condition, adav[...])[:8] + ada_b[...].astype(f32)
+    moves = []
+    for k in range(4):
+        to = (y + k // 2) % 2 * 2 + (x + k) % 2
+        row = jnp.broadcast_to(m4[pl.ds(to, 1), :], to_send.shape[1:])
+        if k == 0:
+            shares[t] = row
+        else:
+            to_send[k - 1] = row
+            moves.append(remote(to_send.at[k - 1], shares.at[t], ssems, k - 1, ("x", "y", "xy")[k - 1]))
+            moves[-1].start()
+
+    group = jnp.where(c == y, mine, other)
+    bucket = group[4:5, 2:3]
+    skip = jnp.where(x == 0, group[0:2], group[2:4])
+    for j in range(4):
+        block = 2 * ((c + j // 2) % 2) + (x + j) % 2
+        position = column(LB) + LB * block
+        hit = jnp.where((position == skip[0:1, :]) | (position == skip[1:2, :]), 1.0, 0.0)
+        kept_o[LB * j : LB * (j + 1), :] = 1.0 - jnp.max(hit, axis=1, keepdims=True)
+
+    def chosen(masks):
+        lane = lax.broadcasted_iota(jnp.int32, masks.shape, 1)
+        return jnp.sum(jnp.where(lane == bucket, masks[...].astype(f32), 0.0), axis=1, keepdims=True)
+
+    def spread(on, low, width):
+        first = width * lax.broadcasted_iota(jnp.int32, (on.shape[0], low.shape[1]), 0)
+        return jnp.sum(jnp.where((low >= first) & (low < first + width), on, 0.0), axis=0, keepdims=True)
+
+    lane = lax.broadcasted_iota(jnp.int32, (1, WC), 1)
+    share = sum(jnp.where(lane >= DC * k, 1, 0) for k in range(1, 4))
+    hmask_o[...] = spread(chosen(heads_t), lane + DC * (share + c), HD)
+    channels = chosen(channels_t)
+    lane = lax.broadcasted_iota(jnp.int32, (1, FB), 1)
+    share = sum(jnp.where(lane >= FZ * k, 1, 0) for k in range(1, 4))
+    for f in range(NF):
+        low = lane + (4 * DZ - FZ) * share + FF // 8 * c + FZ * f
+        chan_o[f] = spread(channels, low, FF // channels.shape[0])
+
+    def half(v, k, width):
+        v = v[:, 2 * width * k : 2 * width * (k + 1)].astype(f32)
+        return jnp.where(c == 0, v[:, :width], v[:, width:])
+
+    bias = [half(q_bias[...], k, DC) for k in range(4)]
+    bias += [jnp.zeros((1, WC), f32)] + [half(v_bias[...], k, DC) for k in range(4)]
+    bias = jnp.concatenate(bias, axis=1)
+    b1v = [half(b1[...], k, FF // 8) for k in range(4)]
+    for f in range(NF):
+        b1_o[f] = jnp.concatenate([v[:, FZ * f : FZ * (f + 1)] for v in b1v], axis=1)
+    loads[1].wait()
+    loads[2].wait()
     for core in range(2):
 
         @pl.when(c == core)
         def _():
             for k in range(12):
-                wq_o[:, DC * k : DC * (k + 1)] = wq[:, DZ * k + DC * core : DZ * k + DC * (core + 1)]
+                wqc[:, DC * k : DC * (k + 1)] = wqv[:, DZ * k + DC * core : DZ * k + DC * (core + 1)]
             for f in range(NF):
                 for k in range(4):
                     start = 4 * DZ * k + FF // 8 * core + FZ * f
-                    w1_o[f, :, FZ * k : FZ * (k + 1)] = w1[:, start : start + FZ]
-
-
-def qkv_kernel(tok, mod, w, bias, shifted_o, qkv_o):
-    normed, _ = normalize(tok[...].astype(f32))
-    shifted = (normed * (1.0 + mod[1:2, :]) + mod[0:1, :]).astype(bf16)
-    shifted_o[...] = shifted
-    qkv_o[...] = (dot_nn(shifted, w[...]) + bias[...]).astype(bf16)
-
-
-def attn_kernel(step, qkv, head_on, out, qs, ks, vs):
+                    w1c[f, :, FZ * k : FZ * (k + 1)] = w1v[:, start : start + FZ]
+
+    stores = [
+        pltpu.make_async_copy(a, b, lsems.at[k]) for k, (a, b) in enumerate(((wqc, wq_o), (w1c, w1_o)))
+    ]
+    for store in stores:
+        store.start()
+    pass_on(*tok_moves)
+    leave(*cot_moves)
+    for copy in moves:
+        copy.wait()
+    share_rows = [shares[k][0:1, :] for k in range(4)]
+    n, m = D // 2, 3 * D // 2
+    mod = [share_rows[0][:, :D], jnp.concatenate([share_rows[0][:, D:], share_rows[1][:, :n]], axis=1),
+           share_rows[1][:, n:], share_rows[2][:, :D],
+           jnp.concatenate([share_rows[2][:, D:], share_rows[3][:, :n]], axis=1), share_rows[3][:, n:]]
+    own_step = 0.5 * jnp.sum(jnp.where(r == t, steps, 0.0), axis=0, keepdims=True)
+    mod += [jnp.broadcast_to(own_step, (1, D)), jnp.zeros((1, D), f32)]
+    mod_o[...] = jnp.concatenate(mod, axis=0)
+    for j in range(4):
+        if j >= 2:
+            tok_moves[3][j - 2].wait_recv()
+        part = slice(LB * j, LB * (j + 1))
+        normed, _ = normalize(tk[part, :].astype(f32))
+        shifted = (normed * (1.0 + mod[1]) + mod[0]).astype(bf16)
+        shifted_o[part, :] = shifted
+        qkv_o[part, :] = (dot_nn(shifted, wqc[...]) + bias).astype(bf16)
+    keep = pltpu.make_async_copy(tk, tok_o, lsems.at[2])
+    keep.start()
+    pass_on(*cot_moves)
+    for copy in cot_moves[3]:
+        copy.wait_recv()
+    keep_cot = pltpu.make_async_copy(ck, cot_o, lsems.at[5])
+    keep_cot.start()
+    settle(*tok_moves)
+    settle(*cot_moves)
+    for store in stores:
+        store.wait()
+    keep.wait()
+    keep_cot.wait()
+
+
+def attn_kernel(step, qkv, hmask, wp, bias, tok, mod, mixed_o, shifted2_o, attn_o,
+                qh, kh, vh, mx, mo, wpv, tkv, csems, lsems):
+    c = place()[1]
+    loads = [
+        pltpu.make_async_copy(wp.at[:, c], wpv.at[0], lsems.at[0]),
+        pltpu.make_async_copy(wp.at[:, 1 - c], wpv.at[1], lsems.at[1]),
+        pltpu.make_async_copy(tok, tkv, lsems.at[2]),
+    ]
+    for load in loads:
+        load.start()
     scale = LOG2E / math.sqrt(HD)
     for h in range(HC):
-        qs[...] = qkv[:, h * HD : (h + 1) * HD]
-        ks[...] = qkv[:, WC + h * HD : WC + (h + 1) * HD]
-        vs[...] = qkv[:, 2 * WC + h * HD : 2 * WC + (h + 1) * HD]
-        on = head_on[h]
-
-        def body(i, carry):
-            part = pl.ds(pl.multiple_of(i * step, step), step)
-            s = dot_nt(qs[part, :], ks[...])
+        for k, ref in enumerate((qh, kh, vh)):
+            ref[h] = qkv[:, WC * k + HD * h : WC * k + HD * (h + 1)]
+
+    def crossing(i):
+        src = mx.at[pl.ds(pl.multiple_of(i * step, step), step)]
+        dst = mo.at[pl.ds(pl.multiple_of((i * step + LH) % L, step), step)]
+        return remote(src, dst, csems, i, "c")
+
+    def body(i, carry):
+        part = pl.ds(pl.multiple_of(i * step, step), step)
+        outs = []
+        for h in range(HC):
+            s = dot_nt(qh[h, part, :], kh[h])
             top = jnp.max(s, axis=1, keepdims=True)
             p = jnp.exp2((s - top) * scale)
             total = jnp.sum(p, axis=1, keepdims=True)
-            o = dot_nn(p.astype(bf16), vs[...])
-            out[part, h * HD : (h + 1) * HD] = (o * (on / total)).astype(bf16)
-            return carry
-
-        lax.fori_loop(0, L // step, body, 0)
-
-
-def proj_kernel(mine, other, w_mine, w_other, bias, tok, mod, shifted2_o, attn_o):
-    attn = (
-        dot_nn(mine[...], w_mine[...].reshape(WC, D))
-        + dot_nn(other[...], w_other[...].reshape(WC, D))
-        + bias[...]
-    )
-
-    @pl.when(pl.program_id(0) < 2)
-    def _():
-        attn_o[...] = attn
-
-    resid = tok[...].astype(f32) + mod[2:3, :] * attn
-    normed, _ = normalize(resid)
-    shifted2_o[...] = (normed * (1.0 + mod[4:5, :]) + mod[3:4, :]).astype(bf16)
+            outs.append(dot_nn(p.astype(bf16), vh[h]) * (1.0 / total))
+        mx[part, :] = (jnp.concatenate(outs, axis=1) * hmask[...]).astype(bf16)
+        crossing(i).start()
+        return carry
+
+    lax.fori_loop(0, L // step, body, 0)
+    keep = pltpu.make_async_copy(mx, mixed_o, lsems.at[3])
+    keep.start()
+    for load in loads:
+        load.wait()
+    for i in range(L // step):
+        crossing(i).wait()
+    w_mine, w_other = wpv[0].reshape(WC, D), wpv[1].reshape(WC, D)
+    for j in range(4):
+        part = slice(LB * j, LB * (j + 1))
+        attn = dot_nn(mx[part, :], w_mine) + dot_nn(mo[part, :], w_other) + bias[...]
+        if j < 2:
+            attn_o[part, :] = attn
+        normed, _ = normalize(tkv[part, :].astype(f32) + mod[2:3, :] * attn)
+        shifted2_o[part, :] = (normed * (1.0 + mod[4:5, :]) + mod[3:4, :]).astype(bf16)
+    keep.wait()
 
 
 def pack_hidden(block1, block2, o1, o2, ry, rx, rz):
@@ -485,8 +635,8 @@
                 copy.wait()
 
 
-def middle_kernel(ds, ds_r, br, br_r, attn, tok, g, kept, mod, bias2, mixed, w,
-                  d_resid_o, out, dh_o, pka, psa, pkb, psb, sums_o, sum_o, da, ob, t1, csems, tsems, lsem):
+def middle_kernel(ds, ds_r, br, br_r, attn, tok, g, kept, mod, bias2, mixed, wp,
+                  d_resid_o, out, dh_o, pka, psa, pkb, psb, sums_o, sum_o, da, ob, t1, wpv, csems, tsems, lsems):
     i = pl.program_id(0)
     n = LH // 4
     z, c, y, x = place()
@@ -515,7 +665,9 @@
         remote(da.at[pl.ds(n * k, n)], da.at[pl.ds(LH + n * k, n)], csems, k, "c") for k in range(4)
     ]
     home0 = remote(ob.at[pl.ds(0, LB)], out.at[x], tsems, 0, "t0")
-    stay0 = pltpu.make_async_copy(ob.at[pl.ds(0, LB)], out.at[x], lsem)
+    stay0 = pltpu.make_async_copy(ob.at[pl.ds(0, LB)], out.at[x], lsems.at[0])
+    load = pltpu.make_async_copy(wp.at[:, c], wpv, lsems.at[1])
+    pl.when(i == 0)(load.start)
     home1 = remote(ob.at[pl.ds(LB, LB)], out.at[x], tsems, 1, "t1")
     for k in range(4):
 
@@ -532,7 +684,8 @@
     def _():
         for copy in crossing:
             copy.wait()
-        wv = w[...].reshape(WC, D)
+        load.wait()
+        wv = wpv[...].reshape(WC, D)
         dh_o[...] = dot_nt(da[...], wv).astype(bf16)
         sum_o[...] = dot_nn(jnp.ones((16, L), bf16), da[...])[:8]
         grad = dot_tn(mixed[...], da[...]).astype(bf16)
@@ -557,35 +710,38 @@
         home1.wait()
 
 
-def attn_back_kernel(step, qkv, dh, head_on, out, qs, ks, vs, dos, dq, dk, dv):
+def attn_back_kernel(step, qkv, dh, hmask, out, qh, kh, vh, doh, dk, dv):
     scale = LOG2E / math.sqrt(HD)
     for h in range(HC):
-        qs[...] = qkv[:, h * HD : (h + 1) * HD]
-        ks[...] = qkv[:, WC + h * HD : WC + (h + 1) * HD]
-        vs[...] = qkv[:, 2 * WC + h * HD : 2 * WC + (h + 1) * HD]
-        dos[...] = (dh[:, h * HD : (h + 1) * HD].astype(f32) * head_on[h]).astype(bf16)
-        dk[...] = jnp.zeros_like(dk)
-        dv[...] = jnp.zeros_like(dv)
-
-        def body(i, carry):
-            part = pl.ds(pl.multiple_of(i * step, step), step)
-            q, do = qs[part, :], dos[part, :]
-            s = dot_nt(ks[...], q)
+        for k, ref in enumerate((qh, kh, vh)):
+            ref[h] = qkv[:, WC * k + HD * h : WC * k + HD * (h + 1)]
+        cut = slice(HD * h, HD * (h + 1))
+        doh[h] = (dh[:, cut].astype(f32) * hmask[:, cut]).astype(bf16)
+    dk[...] = jnp.zeros_like(dk)
+    dv[...] = jnp.zeros_like(dv)
+
+    def body(i, carry):
+        part = pl.ds(pl.multiple_of(i * step, step), step)
+        outs = []
+        for h in range(HC):
+            q, do = qh[h, part, :], doh[h, part, :]
+            s = dot_nt(kh[h], q)
             top = jnp.max(s, axis=0, keepdims=True)
             p = jnp.exp2((s - top) * scale)
             p = p * (1.0 / jnp.sum(p, axis=0, keepdims=True))
-            dp = dot_nt(vs[...], do)
+            dp = dot_nt(vh[h], do)
             row_dot = jnp.sum(p * dp, axis=0, keepdims=True)
             ds = (p * (dp - row_dot)).astype(bf16)
-            dv[...] += dot_nn(p.astype(bf16), do)
-            dk[...] += dot_nn(ds, q)
-            dq[part, :] = dot_tn(ds, ks[...])
-            return carry
-
-        lax.fori_loop(0, L // step, body, 0)
-        out[:, h * HD : (h + 1) * HD] = (dq[...] * (1.0 / math.sqrt(HD))).astype(bf16)
-        out[:, WC + h * HD : WC + (h + 1) * HD] = (dk[...] * (1.0 / math.sqrt(HD))).astype(bf16)
-        out[:, 2 * WC + h * HD : 2 * WC + (h + 1) * HD] = dv[...].astype(bf16)
+            dv[h] += dot_nn(p.astype(bf16), do)
+            dk[h] += dot_nn(ds, q)
+            outs.append(dot_tn(ds, kh[h]))
+        out[part, :WC] = (jnp.concatenate(outs, axis=1) * (1.0 / math.sqrt(HD))).astype(bf16)
+        return carry
+
+    lax.fori_loop(0, L // step, body, 0)
+    for h in range(HC):
+        out[:, WC + HD * h : WC + HD * (h + 1)] = (dk[h] * (1.0 / math.sqrt(HD))).astype(bf16)
+        out[:, 2 * WC + HD * h : 2 * WC + HD * (h + 1)] = dv[h].astype(bf16)
 
 
 def qkv_grad_kernel(shifted, dqkv, extra, ka, sa, kb, sb, t1):
@@ -664,7 +820,7 @@
             if k == 0:
                 pl.when(c != y)(home0.start)
                 pl.when(c == y)(stay0.start)
-                item_o[...] = jnp.concatenate(sums + [sums_mid[0:4, :], jnp.zeros((2, D), f32)], axis=0)
+                item_o[...] = jnp.concatenate(sums + [sums_mid[0:4, :], mod[6:8, :]], axis=0)
             else:
                 home1.start()
                 item_o[0:2, :] += jnp.concatenate(sums, axis=0)
@@ -749,27 +905,6 @@
     )
 
 
-def make_perm(move):
-    pairs = []
-    for b in range(8):
-        for t in range(4):
-            z, c, y, x = move(b // 2, b % 2, t // 2, t % 2)
-            pairs.append((b * 4 + t, (z * 2 + c) * 4 + y * 2 + x))
-    return pairs
-
-
-PERM_X = make_perm(lambda z, c, y, x: (z, c, y, 1 - x))
-PERM_Y = make_perm(lambda z, c, y, x: (z, c, 1 - y, x))
-PERM_XY = make_perm(lambda z, c, y, x: (z, c, 1 - y, 1 - x))
-PERM_C = make_perm(lambda z, c, y, x: (z, 1 - c, y, x))
-PERM_Z = [None] + [make_perm(lambda z, c, y, x, j=j: (z ^ j, c, y, x)) for j in (1, 2, 3)]
-PERM_T = [make_perm(lambda z, c, y, x, j=j: (z, y, c, x ^ j)) for j in (0, 1)]
-
-
-def send(value, perm):
-    return lax.ppermute(value, BOTH, perm)
-
-
 def one_item_per_chip(
     tokens, cotangent, timesteps, bucket_ids, head_masks, channel_masks, skip_rows,
     w_qkv, q_bias, v_bias, w_proj, proj_bias, w_fc1, fc1_bias, w_fc2, fc2_bias, ada_weight, ada_bias,
@@ -778,88 +913,42 @@
     z, c, y, x = b // 2, b % 2, t // 2, t % 2
     sds = jax.ShapeDtypeStruct
 
-    def gather(values):
-        here = lax.dynamic_index_in_dim(values, x, 0, keepdims=False)
-        there = lax.dynamic_index_in_dim(values, 1 - x, 0, keepdims=False)
-        mine = jnp.concatenate([send(here, PERM_T[0]), send(there, PERM_T[1])], axis=0)
-        return jnp.concatenate([mine, send(mine, PERM_C)], axis=0)
-
-    tok = gather(tokens)
-    ints = jnp.concatenate([timesteps, bucket_ids, jnp.zeros((13,), jnp.int32), skip_rows.reshape(-1)])
-    ints_other = send(ints, PERM_C)
-    every_step = lax.all_gather(timesteps, "bucket", axis=0, tiled=True)
-    g_all = gather(cotangent)
-
-    steps4 = jnp.where(c == 0, jnp.concatenate([ints[:2], ints_other[:2]]), jnp.concatenate([ints_other[:2], ints[:2]]))
-    group_ints = jnp.where(c == y, ints, ints_other)
-    bucket = group_ints[2]
-    skip = lax.dynamic_slice_in_dim(group_ints, 16 + skip_rows.shape[1] * x, skip_rows.shape[1], 0)
-    blocks = jnp.stack([2 * c + x, 2 * c + 1 - x, 2 * (1 - c) + x, 2 * (1 - c) + 1 - x])
-    positions = (blocks[:, None] * LB + jnp.arange(LB)[None, :]).reshape(L, 1)
-    kept = 1.0 - jnp.any(positions == skip[None, :], axis=1, keepdims=True).astype(f32)
-    kept = kept.reshape(L, 1)
-
-    condition = jax.nn.silu(step_embedding(steps4, D)).astype(bf16)
-    mod4 = jnp.dot(condition, ada_weight, preferred_element_type=f32) + ada_bias.astype(f32)
-    pick = lambda k: lax.dynamic_index_in_dim(mod4, t ^ k, 0, keepdims=False)
-    shares = jnp.stack([pick(0), send(pick(1), PERM_X), send(pick(2), PERM_Y), send(pick(3), PERM_XY)])
-    mod = jnp.take(shares, jnp.arange(4) ^ t, axis=0).reshape(6, D)
-    mod = jnp.concatenate([mod, jnp.zeros((2, D), f32)], axis=0)
-
     def core_half(v, *dims):
         return lax.dynamic_index_in_dim(v.reshape(dims), c, 1, keepdims=False)
 
-    head_on = core_half(lax.dynamic_index_in_dim(head_masks, bucket, 0, keepdims=False).astype(f32), 4, 2, 2).reshape(HC)
-    group_on = lax.dynamic_index_in_dim(channel_masks, bucket, 0, keepdims=False).astype(f32)
-    channel_on = jnp.repeat(group_on, FF // group_on.shape[0])
-
-    def hidden_order(v):
-        return core_half(v, 4, 2, NF, FZ).transpose(1, 0, 2).reshape(NF, 1, FB)
-
-    chan = hidden_order(channel_on)
-    b1 = hidden_order(fc1_bias.astype(f32))
-    qkv_bias = jnp.concatenate([q_bias, jnp.zeros_like(q_bias), v_bias]).astype(f32)
-    qkv_bias = core_half(qkv_bias, 12, 2, DC).reshape(1, 3 * WC)
-
-    (wq, w1), _ = call(
-        prep_kernel, "prep",
-        (sds((D, 3 * WC), bf16), sds((NF, D, FB), bf16)), (w_qkv, w_fc1),
-        grid=(8,),
-        in_specs=[rows(DC, 3 * D), rows(DC, FF)],
-        out_specs=(rows(DC, 3 * WC), pl.BlockSpec((NF, DC, FB), lambda i: (0, i, 0))),
-        nbytes=28e6,
-    )
+    vmem = pl.BlockSpec(memory_space=pltpu.VMEM)
+    skips = skip_rows.reshape(-1, LANES)
+    ints = jnp.concatenate([timesteps, bucket_ids, jnp.zeros((LANES - 3,), jnp.int32)]).reshape(1, LANES)
+    ints = jnp.concatenate([skips, ints, jnp.zeros((7 - skips.shape[0], LANES), jnp.int32)], axis=0)
+    freq = jnp.exp(-math.log(10000.0) * jnp.arange(D // 2, dtype=f32) / (D // 2)).reshape(1, D // 2)
+    ada_cols = ada_weight.shape[1]
+    front, _ = call(
+        front_kernel, "front",
+        (sds((L, D), bf16), sds((L, D), bf16), sds((L, D), bf16), sds((L, 3 * WC), bf16), sds((D, 3 * WC), bf16),
+         sds((NF, D, FB), bf16), sds((8, D), f32), sds((L, 1), f32), sds((1, WC), f32), sds((NF, 1, FB), f32),
+         sds((NF, 1, FB), f32)),
+        (tokens, cotangent, ints, ada_weight, ada_bias.reshape(1, ada_cols), freq, head_masks.T, channel_masks.T,
+         w_qkv, w_fc1, q_bias.reshape(1, D), v_bias.reshape(1, D), fc1_bias.reshape(1, FF)),
+        in_specs=[ANY, ANY, vmem, ANY, vmem, vmem, vmem, vmem, ANY, ANY, vmem, vmem, vmem],
+        out_specs=[ANY, ANY, vmem, vmem, ANY, ANY] + [vmem] * 5,
+        scratch=[vm(L, D), vm(L, D), vm(D, 3 * D), vm(D, 3 * WC), vm(D, FF), vm(NF, D, FB), vm(D, ada_cols),
+                 vm(8, LANES, dtype=jnp.int32), vm(8, ada_cols, dtype=f32), vm(3, 8, ada_cols, dtype=f32),
+                 vm(4, 8, ada_cols, dtype=f32), pltpu.SemaphoreType.DMA((2, 5)), pltpu.SemaphoreType.DMA((2, 4)),
+                 pltpu.SemaphoreType.DMA((2, 3)), pltpu.SemaphoreType.DMA((6,))],
+        peers=("c", "t0", "t1", "x", "y", "xy"), cid=10, flops=2 * L * D * 3 * WC, nbytes=50e6,
+    )
+    tok, g_all, shifted, qkv, wq, w1, mod, kept, hmask, chan, b1 = front
     w2 = w_fc2.reshape(4, 2, NF, FZ, D)
     wp = w_proj.reshape(4, 2, DC, D)
-    wp_mine = lax.dynamic_index_in_dim(wp, c, 1, keepdims=False).reshape(WC, D)
-    wp_other = lax.dynamic_index_in_dim(wp, 1 - c, 1, keepdims=False).reshape(WC, D)
-
-    (shifted, qkv), _ = call(
-        qkv_kernel, "ln_qkv",
-        (sds((L, D), bf16), sds((L, 3 * WC), bf16)), (tok, mod, wq, qkv_bias),
-        grid=(4,),
-        in_specs=[rows(LB, D), full((8, D)), full((D, 3 * WC)), full((1, 3 * WC))],
-        out_specs=(rows(LB, D), rows(LB, 3 * WC)),
-        flops=2 * L * D * 3 * WC, nbytes=12e6,
-    )
-    vmem = pl.BlockSpec(memory_space=pltpu.VMEM)
-    mixed, _ = call(
+    (mixed, shifted2, attn), _ = call(
         functools.partial(attn_kernel, 256), "attn",
-        sds((L, WC), bf16), (qkv, head_on),
-        in_specs=[vmem, SMEM],
-        scratch=[vm(L, HD)] * 3,
-        flops=16e9, nbytes=5e6,
-    )
-    mixed_other = send(mixed, PERM_C)
-    (shifted2, attn), _ = call(
-        proj_kernel, "proj_ln",
-        (sds((L, D), bf16), sds((LH, D), f32)),
-        (mixed, mixed_other, wp_mine, wp_other, proj_bias.astype(f32).reshape(1, D), tok, mod),
-        grid=(4,),
-        in_specs=[rows(LB, WC), pl.BlockSpec((LB, WC), lambda i: ((i + 2) % 4, 0)), full((WC, D)), full((WC, D)),
-                  full((1, D)), rows(LB, D), full((8, D))],
-        out_specs=(rows(LB, D), pl.BlockSpec((LB, D), lambda i: (jnp.minimum(i, 1), 0))),
-        flops=2 * L * D * D, nbytes=12e6,
+        (sds((L, WC), bf16), sds((L, D), bf16), sds((LH, D), f32)),
+        (qkv, hmask, wp, proj_bias.astype(f32).reshape(1, D), tok, mod),
+        in_specs=[vmem, vmem, ANY, vmem, ANY, vmem],
+        out_specs=[ANY, vmem, vmem],
+        scratch=[vm(HC, L, HD)] * 3 + [vm(L, WC), vm(L, WC), vm(2, 4, DC, D), vm(L, D),
+                 pltpu.SemaphoreType.DMA((2, 4)), pltpu.SemaphoreType.DMA((4,))],
+        peers=("c",), cid=11, flops=16e9, nbytes=5e6,
     )
 
     firsts, kepts, sums1, results, before = [], [], [], [], []
@@ -908,13 +997,13 @@
         (sds((LH, D), f32), sds((2, LB, D), bf16), sds((L, WC), bf16), slot_a, slot_a, slot_b, slot_b,
          sds((8, D), f32), sds((8, D), f32)),
         (before[1], ds2_r, before[0], branch_r, attn, tok, g_all, kept, mod, fc2_bias.astype(f32).reshape(1, D),
-         mixed, wp_mine),
+         mixed, wp),
         grid=(4,),
-        in_specs=[row] * 7 + [rows(n, 1), full((8, D)), full((1, D)), once(L, WC), once(WC, D)],
+        in_specs=[row] * 7 + [rows(n, 1), full((8, D)), full((1, D)), once(L, WC), ANY],
         out_specs=(row, ANY, full((L, WC)), full(slot_a.shape), full(slot_a.shape), full(slot_b.shape),
                    full(slot_b.shape), full((8, D)), full((8, D))),
-        scratch=[vm(L, D), vm(LH, D), vm(4, WC, TD), pltpu.SemaphoreType.DMA((2, 4)), pltpu.SemaphoreType.DMA((2, 2)),
-                 pltpu.SemaphoreType.DMA],
+        scratch=[vm(L, D), vm(LH, D), vm(4, WC, TD), vm(4, DC, D), pltpu.SemaphoreType.DMA((2, 4)),
+                 pltpu.SemaphoreType.DMA((2, 2)), pltpu.SemaphoreType.DMA((2,))],
         peers=("c", "t0", "t1"), cid=3,
         jobs=[FirstSum(*slots), SecondSum(*firsts[1], *kepts[1]), ThirdSum(*results[0])],
         flops=4 * L * D * WC, nbytes=20e6,
@@ -925,9 +1014,8 @@
     finals = [given[2][0]]
     dqkv, given = call(
         functools.partial(attn_back_kernel, 512), "attn_back",
-        sds((L, 3 * WC), bf16), (qkv, dh, head_on),
-        in_specs=[vmem, vmem, SMEM],
-        scratch=[vm(L, HD)] * 4 + [vm(L, HD, dtype=f32)] * 3,
+        sds((L, 3 * WC), bf16), (qkv, dh, hmask),
+        scratch=[vm(HC, L, HD)] * 4 + [vm(HC, L, HD, dtype=f32)] * 2,
         cid=4, jobs=[FirstSum(*slots_p), SecondSum(*firsts[2], *kepts[2]), ThirdSum(*results[1])],
         flops=30e9, nbytes=9e6,
     )
@@ -978,9 +1066,9 @@
     )
     final_q = given[0][0]
 
-    every = every.reshape(16, 8, D)[:, :6].reshape(16, 6 * D)
-    ada_cols = ada_weight.shape[1]
-    cond_all = jax.nn.silu(step_embedding(every_step, D)).astype(bf16).astype(f32)
+    every = every.reshape(16, 8, D)
+    cond_all = jax.nn.silu(step_embedding(every[:, 6, 0], D)).astype(bf16).astype(f32)
+    every = every[:, :6].reshape(16, 6 * D)
     cond_rows = lax.dynamic_slice_in_dim(cond_all, b * DC, DC, 1)
     columns = lax.dynamic_slice_in_dim(every, t * ada_cols, ada_cols, 1)
     grad_ada_weight = lax.dot_general(

time: 486 us -> 432 us (0.89)
  starting transfers between devices: 15.8 us -> 0 us
  local copies, waits for them, and re-layouts: 39 us -> 23.4 us
  blocking collectives: 9.17 us -> 0 us
  other arithmetic: 12.8 us -> 4.63 us
    ppermute x11 -> x0, starting transfers between devices: 15.8 us -> none  [send(): return lax.ppermute(value, BOTH, perm)]
    unnamed x1 -> x0, blocking collectives: 9.17 us -> none
    unnamed x81 -> x45, local copies, waits for them, and re-layouts: 9.42 us -> 14.9 us
    pallas_call x14 -> x12, Pallas kernels: 390 us -> 394 us  [call(): pl.pallas_call(run, out_shape=out_shape + [o for j in jobs for o in j.out...]
  transfers between devices with their start and end apart: 11 -> 0, of which waited for: 1 -> 0; matrix products, arithmetic and copies ran while one was open for 7% -> 0% of each run, Pallas kernels for 11% -> 0%
where the time goes in v3:
time: 432 us; the launch traced here: 425 us
  Pallas kernels  394 us (91%)
  local copies, waits for them, and re-layouts  23.4 us (5%)
  other arithmetic  4.63 us (1%)
    pallas_call x12, Pallas kernels, call(): pl.pallas_call(run, out_shape=out_shape + [o for j in jobs for o in j.out...  394 us
    unnamed x45, local copies, waits for them, and re-layouts  14.9 us

profile of v3, /device:TPU:0, one launch (start us, length us, event | category | flops | bytes accessed | tf_op | source)
XLA Modules:
  0.0 425.4 jit_solution(12523560998047840217)
XLA Ops:
  0.7 6.5 %copy.45.refs_3_ = bf16[1152,1728]{1,0:T(8,128)(2,1)} copy(bf16[1152,1728]{0,1:T(8,128)(2,1)} %param.34) | data formatting | bytes 7962624 | tf_op args[16]
  13.1 42.2 %front.1 = (bf16[1024,1152]{1,0:T(8,128)(2,1)}, bf16[1024,1152]{1,0:T(8,128)(2,1)}, bf16[1024,1152]{1,0:T(8,128)(2,1)}, bf16[1024,1728]{1,0:T(8,128)(2,1)}, bf16...) custom-call(bf16[2,256,1152]{2,1,0:T(8,128)(2,1)} %refs_0_.1, ...), custom_call_target="tpu_custom_call" | custom-call | flops 4076863488 | bytes 50000000 | tf_op jit(solution)/shard_map/front/pallas_call | solution.py:281
  55.9 30.7 %attn.1 = (bf16[1024,576]{1,0:T(8,128)(2,1)}, bf16[1024,1152]{1,0:T(8,128)(2,1)}, f32[512,1152]{1,0:T(8,128)}) custom-call(bf16[1024,1728]{1,0:T(8,128)(2,1)} %get-tuple-element.108.refs_0_, f32[1,576]{1,0:T(1,128)} %get-tuple-element.109.refs_1_.refs_2_, bf16[4,2,144,1152]{3,2,1,0:T(8,128)(2,1)} %bitcast.21, f32[1,1152]{1,0:T(1,128)} %reshape.114.refs_3_, ...), custom_call_target="tpu_custom_call" | custom-call | flops 16000000000 | bytes 5000000 | tf_op jit(solution)/shard_map/attn/pallas_call | solution.py:281
  86.7 21.5 %mlp0.1 = (bf16[2,4,432,128]{3,2,1,0:T(8,128)(2,1)}, bf16[2,4,432,128]{3,2,1,0:T(8,128)(2,1)}, bf16[2,4,432,128]{3,2,1,0:T(8,128)(2,1)}, bf16[2,4,432,128]{3,2,1...) custom-call(bf16[1024,1152]{1,0:T(8,128)(2,1)} %get-tuple-element.11, ...), custom_call_target="tpu_custom_call" | custom-call | flops 10871635968 | bytes 20000000 | tf_op jit(solution)/shard_map/mlp0/pallas_call | solution.py:281
  108.1 28.4 %mlp1.1 = (bf16[2,4,432,128]{3,2,1,0:T(8,128)(2,1)}, bf16[2,4,432,128]{3,2,1,0:T(8,128)(2,1)}, bf16[2,4,432,128]{3,2,1,0:T(8,128)(2,1)}, bf16[2,4,432,128]{3,2,1...) custom-call(bf16[1024,1152]{1,0:T(8,128)(2,1)} %get-tuple-element.11, ...), custom_call_target="tpu_custom_call" | custom-call | flops 10871635968 | bytes 20000000 | tf_op jit(solution)/shard_map/mlp1/pallas_call | solution.py:281
  136.5 38.4 %mlp2.1 = (bf16[2,4,432,128]{3,2,1,0:T(8,128)(2,1)}, bf16[2,4,432,128]{3,2,1,0:T(8,128)(2,1)}, bf16[2,4,432,128]{3,2,1,0:T(8,128)(2,1)}, bf16[2,4,432,128]{3,2,1...) custom-call(bf16[1024,1152]{1,0:T(8,128)(2,1)} %get-tuple-element.11, ...), custom_call_target="tpu_custom_call" | custom-call | flops 10871635968 | bytes 20000000 | tf_op jit(solution)/shard_map/mlp2/pallas_call | solution.py:281
  175.0 0.7 pad_maximum_fusion
  176.5 51.6 %middle.1 = (f32[512,1152]{1,0:T(8,128)}, bf16[2,256,1152]{2,1,0:T(8,128)(2,1)}, bf16[1024,576]{1,0:T(8,128)(2,1)}, bf16[2,4,176,128]{3,2,1,0:T(8,128)(2,1)}, bf...) custom-call(bf16[512,1152]{1,0:T(8,128)(2,1)} %get-tuple-element.134, ...), custom_call_target="tpu_custom_call" | custom-call | flops 2717908992 | bytes 20000000 | tf_op jit(solution)/shard_map/middle/pallas_call | solution.py:281
  228.1 0.8 slice_reduce_fusion.1
  230.0 47.6 %attn_back.1 = (bf16[1024,1728]{1,0:T(8,128)(2,1)}, bf16[4,176,128]{2,1,0:T(8,128)(2,1)}, bf16[4,176,128]{2,1,0:T(8,128)(2,1)}, bf16[4,160,128]{2,1,0:T(8,128)(2...) custom-call(bf16[1024,1728]{1,0:T(8,128)(2,1)} %get-tuple-element.10, ...), custom_call_target="tpu_custom_call" | custom-call | flops 30000001024 | bytes 9000000 | tf_op jit(solution)/shard_map/attn_back/pallas_call | solution.py:281
  277.6 28.0 %qkv_grad.1 = (bf16[2,4,512,128]{3,2,1,0:T(8,128)(2,1)}, bf16[2,4,512,128]{3,2,1,0:T(8,128)(2,1)}, bf16[2,4,512,128]{3,2,1,0:T(8,128)(2,1)}, bf16[2,4,512,128]{3...) custom-call(bf16[1024,1152]{1,0:T(8,128)(2,1)} %get-tuple-element.166.refs_0_, ...), custom_call_target="tpu_custom_call" | custom-call | flops 4076863488 | bytes 12000000 | tf_op jit(solution)/shard_map/qkv_grad/pallas_call | solution.py:281
  305.7 43.9 %tail.1 = (bf16[2,256,1152]{2,1,0:T(8,128)(2,1)}, f32[8,1152]{1,0:T(8,128)}, bf16[4,512,128]{2,1,0:T(8,128)(2,1)}, bf16[4,512,128]{2,1,0:T(8,128)(2,1)}, bf16[4,...) custom-call(bf16[1024,1728]{1,0:T(8,128)(2,1)} %get-tuple-element.162.refs_1_.refs_0_, ...), custom_call_target="tpu_custom_call" | custom-call | flops 4076863488 | bytes 12000000 | tf_op jit(solution)/shard_map/tail/pallas_call | solution.py:281
  349.6 18.5 %square.1 = (f32[4,8,1152]{2,1,0:T(8,128)}, bf16[3,1024,128]{2,1,0:T(8,128)(2,1)}, f32[1024,128]{1,0:T(8,128)}) custom-call(f32[8,1152]{1,0:T(8,128)} %get-tuple-element.189.refs_0_, bf16[4,512,128]{2,1,0:T(8,128)(2,1)} %get-tuple-element.190.refs_1_, bf16[4,512,128]{2,1,0:T(8,128)(2,1)} %get-tuple-element.191.refs_2_, ...), custom_call_target="tpu_custom_call" | custom-call | tf_op jit(solution)/shard_map/square/pallas_call | solution.py:281
  368.1 37.5 %every.1 = (f32[4,4,8,1152]{3,2,1,0:T(8,128)}, f32[1024,128]{1,0:T(8,128)}) custom-call(f32[4,8,1152]{2,1,0:T(8,128)} %get-tuple-element.194.refs_0_, bf16[3,1024,128]{2,1,0:T(8,128)(2,1)} %get-tuple-element.195.refs_1_, f32[1024,128]{1,0:T(8,128)} %get-tuple-element.196.refs_2_), custom_call_target="tpu_custom_call" | custom-call | tf_op jit(solution)/shard_map/every/pallas_call | solution.py:281
  405.6 1.2 copy.49
  406.7 1.0 slice_reduce_fusion
  408.0 1.7 fusion
  409.7 5.4 %finish.1 = (f32[144,864]{1,0:T(8,128)}, f32[144,288]{1,0:T(8,128)}, f32[144,1152]{1,0:T(8,128)}, f32[576,288]{1,0:T(8,128)}) custom-call(f32[864,128]{1,0:T(8,128)} %get-tuple-element.185.refs_0_, f32[864,128]{1,0:T(8,128)} %get-tuple-element.186.refs_1_, f32[864,128]{1,0:T(8,128)} %get-tuple-element.187.refs_2_, f32[336,128]{1,0:T(8,128)} %get-tuple-element.188.refs_3_, ...), custom_call_target="tpu_custom_call" | custom-call | bytes 6000000 | tf_op jit(solution)/shard_map/finish/pallas_call | solution.py:281
  415.1 2.4 copy.48
  418.2 0.7 slice_bitcast_fusion
  420.1 1.6 convert_element_type.4
  421.7 1.0 copy.57
  422.7 0.8 copy.58
  424.2 0.8 copy.60
  (69 shorter events, 10.5 us)
Async XLA Ops:
  0.6 6.6 %copy-start.12 = (s32[8,36]{1,0:T(8,128)S(1)}, s32[8,36]{1,0:T(8,128)}, u32[]{:S(2)}) copy-start(s32[8,36]{1,0:T(8,128)} %param.23) | copy-start | bytes 3460
  0.7 7.3 %copy-start.5 = (bf16[4608]{0:T(1024)(128)(2,1)S(1)}, bf16[4608]{0:T(1024)(128)(2,1)}, u32[]{:S(2)}) copy-start(bf16[4608]{0:T(1024)(128)(2,1)} %param.31) | copy-start | bytes 27652
  0.7 7.9 %copy-start.16 = (s32[2,256]{1,0:T(2,128)S(1)}, s32[2,256]{1,0:T(2,128)}, u32[]{:S(2)}) copy-start(s32[2,256]{1,0:T(2,128)} %param.24) | copy-start | bytes 6148
  0.7 8.6 %copy-start.17 = (s32[2]{0:T(128)S(1)}, s32[2]{0:T(128)}, u32[]{:S(2)}) copy-start(s32[2]{0:T(128)} %param.20) | copy-start | bytes 28
  0.7 9.4 %copy-start.7 = (s32[8,16]{1,0:T(8,128)S(1)}, s32[8,16]{1,0:T(8,128)}, u32[]{:S(2)}) copy-start(s32[8,16]{1,0:T(8,128)} %param.22) | copy-start | bytes 1540
  0.7 10.0 %copy-start.13 = (bf16[1728]{0:T(1024)(128)(2,1)S(1)}, bf16[1728]{0:T(1024)(128)(2,1)}, u32[]{:S(2)}) copy-start(bf16[1728]{0:T(1024)(128)(2,1)} %param.35) | copy-start | bytes 10372
  0.7 10.6 %copy-start.8 = (bf16[1152]{0:T(1024)(128)(2,1)S(1)}, bf16[1152]{0:T(1024)(128)(2,1)}, u32[]{:S(2)}) copy-start(bf16[1152]{0:T(1024)(128)(2,1)} %param.26) | copy-start | bytes 6916
  0.7 11.2 %copy-start.9 = (bf16[1152]{0:T(1024)(128)(2,1)S(1)}, bf16[1152]{0:T(1024)(128)(2,1)}, u32[]{:S(2)}) copy-start(bf16[1152]{0:T(1024)(128)(2,1)} %param.27) | copy-start | bytes 6916
  13.1 42.2 %copy-start.10 = (bf16[1152]{0:T(1024)(128)(2,1)S(1)}, bf16[1152]{0:T(1024)(128)(2,1)}, u32[]{:S(2)}) copy-start(bf16[1152]{0:T(1024)(128)(2,1)} %param.29) | copy-start | bytes 6916
  136.5 38.5 %copy-start.14 = (f32[1,768]{1,0:T(1,128)S(1)}, f32[1,768]{1,0:T(1,128)}, u32[]{:S(2)}) copy-start(f32[1,768]{1,0:T(1,128)} %get-tuple-element.167) | copy-start | bytes 9220
  136.5 38.5 %copy-start.15 = (f32[1,768]{1,0:T(1,128)S(1)}, f32[1,768]{1,0:T(1,128)}, u32[]{:S(2)}) copy-start(f32[1,768]{1,0:T(1,128)} %get-tuple-element.168) | copy-start | bytes 9220
  136.5 39.4 %copy-start.11 = (bf16[1152]{0:T(1024)(128)(2,1)S(1)}, bf16[1152]{0:T(1024)(128)(2,1)}, u32[]{:S(2)}) copy-start(bf16[1152]{0:T(1024)(128)(2,1)} %param.33) | copy-start | bytes 6916
  176.5 52.5 %copy-start.6 = (f32[1,1152]{1,0:T(1,128)S(1)}, f32[1,1152]{1,0:T(1,128)}, u32[]{:S(2)}) copy-start(f32[1,1152]{1,0:T(1,128)} %get-tuple-element.170) | copy-start | bytes 13828
  408.0 12.1 %copy-start = (bf16[2,256,1152]{2,1,0:T(8,128)(2,1)S(1)}, bf16[2,256,1152]{2,1,0:T(8,128)(2,1)}, u32[]{:S(2)}) copy-start(bf16[2,256,1152]{2,1,0:T(8,128)(2,1)} %get-tuple-element.184) | copy-start | bytes 3538948
  415.1 6.6 %copy-start.1 = (bf16[2,256,1152]{2,1,0:T(8,128)(2,1)S(1)}, bf16[2,256,1152]{2,1,0:T(8,128)(2,1)}, u32[]{:S(2)}) copy-start(bf16[2,256,1152]{2,1,0:T(8,128)(2,1)} %get-tuple-element.263) | copy-start | bytes 3538948
  420.1 2.6 copy-start.3
  421.7 1.8 copy-start.4
  421.7 2.5 copy-start.2

commit v4 on v3

--- a/solution.py
+++ b/solution.py
@@ -186,16 +186,7 @@
 
     def finish(self, ins, outs, scratch):
         zs, zk, local = scratch[6], scratch[7], scratch[9]
-        start = 0
-        for k, r in enumerate(self.rows):
-            kv, qv, rv = scratch[3 * k : 3 * k + 3]
-            for j in range(4):
-                total = kv[j].astype(f32) + qv[j].astype(f32) + rv[j].astype(f32)
-                if j == 0:
-                    zk[start : start + r, :] = total
-                else:
-                    zs[j - 1, start : start + r, :] = total.astype(bf16)
-            start += r
+        layer_sums([scratch[0:3], scratch[3:6]], zs, zk)
         return [
             pltpu.make_async_copy(zs, outs[0], local.at[4]),
             pltpu.make_async_copy(zk, outs[1], local.at[5]),
@@ -222,8 +213,154 @@
         return [pltpu.make_async_copy(kept, outs[0], local.at[1])]
 
 
+def layer_sums(streams, zs, zk):
+    start = 0
+    for kv, qv, rv in streams:
+        rows_ = rv.shape[1]
+        for j in range(4):
+            total = kv[j].astype(f32) + qv[j].astype(f32) + rv[j].astype(f32)
+            if j == 0:
+                zk[start : start + rows_, :] = total
+            else:
+                zs[j - 1, start : start + rows_, :] = total.astype(bf16)
+        start += rows_
+
+
+class SecondThird(SecondSum):
+    peers = ("x", "y", "z1", "z2", "z3")
+
+    def __init__(self, *args):
+        super().__init__(*args)
+        total = sum(self.rows)
+        self.outs = [jax.ShapeDtypeStruct((total, LANES), f32)]
+        self.scratch += [vm(3, total, LANES), pltpu.SemaphoreType.DMA((2, 3))]
+
+    def third(self, scratch):
+        zs, got, sems = scratch[6], scratch[10], scratch[11]
+        return [remote(zs.at[k], got.at[k], sems, k, f"z{k + 1}") for k in (2, 1, 0)]
+
+    def tick(self, ins, outs, scratch):
+        for group in super().plan(ins, outs, scratch[:10]):
+            for copy in group:
+                copy.wait()
+        layer_sums([scratch[0:3], scratch[3:6]], scratch[6], scratch[7])
+        for copy in self.third(scratch):
+            copy.start()
+
+    def plan(self, ins, outs, scratch):
+        return super().plan(ins, outs, scratch[:10])
+
+    def settle(self, ins, outs, scratch):
+        return self.third(scratch)
+
+    def finish(self, ins, outs, scratch):
+        kept, local, got = scratch[7], scratch[9], scratch[10]
+        kept[...] = kept[...] + got[0].astype(f32) + got[1].astype(f32) + got[2].astype(f32)
+        return [pltpu.make_async_copy(kept, outs[0], local.at[5])]
+
+
+class FirstSecond:
+    peers = ("x", "y")
+
+    def __init__(self, keep_a, sent_a, keep_b, sent_b):
+        self.ins = [keep_a, sent_a, keep_b, sent_b]
+        self.rows = [keep_a.shape[2], keep_b.shape[2]]
+        total = sum(self.rows)
+        self.outs = [jax.ShapeDtypeStruct((3, total, LANES), bf16), jax.ShapeDtypeStruct((total, LANES), f32)]
+        self.scratch = []
+        for r in self.rows:
+            self.scratch += [vm(2, 4, r, LANES), vm(2, 4, r, LANES), vm(4, r, LANES), vm(4, r, LANES)]
+        self.scratch += [vm(3, total, LANES), vm(total, LANES, dtype=f32)]
+        self.scratch += [pltpu.SemaphoreType.DMA((2, 6)), pltpu.SemaphoreType.DMA((4,))]
+
+    def plan(self, ins, outs, scratch):
+        ka, sa, kb, sb = ins
+        sems, local = scratch[10:]
+        far = [
+            remote(sa.at[1], scratch[1].at[1], sems, 0, "x"),
+            remote(sb.at[1], scratch[5].at[1], sems, 1, "y"),
+            remote(sa.at[0], scratch[1].at[0], sems, 2, "x"),
+            remote(sb.at[0], scratch[5].at[0], sems, 3, "y"),
+        ]
+        near = [pltpu.make_async_copy(k, scratch[4 * j], local.at[j]) for j, k in enumerate((ka, kb))]
+        return far, near
+
+    def second(self, scratch):
+        sems = scratch[10]
+        return [remote(scratch[4 * j + 2], scratch[4 * j + 3], sems, 4 + j, name) for j, name in enumerate("yx")]
+
+    def tick(self, ins, outs, scratch):
+        for group in self.plan(ins, outs, scratch):
+            for copy in group:
+                copy.wait()
+        for j in range(2):
+            kv, rv, on = scratch[4 * j : 4 * j + 3]
+            on[...] = (kv[1].astype(f32) + rv[1].astype(f32)).astype(bf16)
+        for copy in self.second(scratch):
+            copy.start()
+
+    def settle(self, ins, outs, scratch):
+        return self.second(scratch)
+
+    def finish(self, ins, outs, scratch):
+        zs, zk, local = scratch[8], scratch[9], scratch[11]
+        layer_sums([(scratch[j].at[0], scratch[j + 1].at[0], scratch[j + 3]) for j in (0, 4)], zs, zk)
+        return [
+            pltpu.make_async_copy(zs, outs[0], local.at[2]),
+            pltpu.make_async_copy(zk, outs[1], local.at[3]),
+        ]
+
+
+class GoHome:
+    peers = ("t0", "t1")
+
+    def __init__(self, values):
+        self.ins = [values]
+        self.outs = [jax.ShapeDtypeStruct((2, LB, D), values.dtype)]
+        self.scratch = [pltpu.SemaphoreType.DMA((2, 2)), pltpu.SemaphoreType.DMA]
+
+    def plan(self, ins, outs, scratch):
+        return [], []
+
+    def tick(self, ins, outs, scratch):
+        home_start(*self.copies(ins, outs, scratch))
+
+    def copies(self, ins, outs, scratch):
+        return homeward(ins[0].at[pl.ds(0, LB)], ins[0].at[pl.ds(LB, LB)], outs[0], *scratch)
+
+    def settle(self, ins, outs, scratch):
+        home_wait(*self.copies(ins, outs, scratch))
+        return []
+
+    def finish(self, ins, outs, scratch):
+        return []
+
+
+def homeward(first, second, dst, sems, local):
+    x = place()[3]
+    return (
+        remote(first, dst.at[x], sems, 0, "t0"),
+        pltpu.make_async_copy(first, dst.at[x], local),
+        remote(second, dst.at[x], sems, 1, "t1"),
+    )
+
+
+def home_start(away, stay, second):
+    _, c, y, _ = place()
+    pl.when(c != y)(away.start)
+    pl.when(c == y)(stay.start)
+    second.start()
+
+
+def home_wait(away, stay, second):
+    _, c, y, _ = place()
+    pl.when(c != y)(away.wait)
+    pl.when(c == y)(stay.wait)
+    second.wait()
+
+
 def call(kernel, name, out_shape, args, in_specs=None, out_specs=None, scratch=(), grid=None,
-         peers=(), jobs=(), cid=None, flops=0, nbytes=0):
+         peers=(), jobs=(), cid=None, ticks=False, flops=0, nbytes=0):
     whole = pl.BlockSpec(memory_space=pltpu.VMEM)
     single = not isinstance(out_shape, (tuple, list))
     out_shape = [out_shape] if single else list(out_shape)
@@ -255,7 +392,7 @@
         def end():
             last = []
             for j, *r in bound:
-                far, near = j.plan(*r)
+                far, near = (j.settle(*r), []) if hasattr(j, "tick") else j.plan(*r)
                 for copy in far:
                     copy.wait()
                 for copy in near:
@@ -267,9 +404,14 @@
             for copy in last:
                 copy.wait()
 
+        def tick():
+            for j, *r in bound:
+                if hasattr(j, "tick"):
+                    j.tick(*r)
+
         if grid is None:
             begin()
-            kernel(*groups[0], *groups[2], *groups[4])
+            kernel(*groups[0], *groups[2], *groups[4], **({"tick": tick} if ticks else {}))
             end()
         else:
             pl.when(pl.program_id(0) == 0)(begin)
@@ -367,7 +509,7 @@
     condition = jax.nn.silu(jnp.concatenate([jnp.cos(angles), jnp.sin(angles)], axis=1))
     condition = jnp.concatenate([condition, jnp.zeros_like(condition)], axis=0).astype(bf16)
     loads[0].wait()
-    m4[...] = dot_nn(condition, adav[...])[:8] + ada_b[...].astype(f32)
+    m4[...] = dot_nt(condition, adav[...])[:8] + ada_b[...].astype(f32)
     moves = []
     for k in range(4):
         to = (y + k // 2) % 2 * 2 + (x + k) % 2
@@ -636,7 +778,7 @@
 
 
 def middle_kernel(ds, ds_r, br, br_r, attn, tok, g, kept, mod, bias2, mixed, wp,
-                  d_resid_o, out, dh_o, pka, psa, pkb, psb, sums_o, sum_o, da, ob, t1, wpv, csems, tsems, lsems):
+                  d_resid_o, out_o, dh_o, pka, psa, pkb, psb, sums_o, sum_o, da, t1, wpv, csems, lsem):
     i = pl.program_id(0)
     n = LH // 4
     z, c, y, x = place()
@@ -646,7 +788,7 @@
     normed2, inverse2 = normalize(resid)
     ds2 = ds[...].astype(f32) + ds_r[...].astype(f32)
     kb = kept[...] * (br[...].astype(f32) + br_r[...].astype(f32) + bias2[...])
-    ob[part, :] = (resid + mod[5:6, :] * kb).astype(bf16)
+    out_o[...] = (resid + mod[5:6, :] * kb).astype(bf16)
     d_resid = gf + normalize_back(ds2 * (1.0 + mod[4:5, :]), normed2, inverse2)
     d_resid_o[...] = d_resid
     da[part, :] = (mod[2:3, :] * d_resid).astype(bf16)
@@ -664,21 +806,10 @@
     crossing = [
         remote(da.at[pl.ds(n * k, n)], da.at[pl.ds(LH + n * k, n)], csems, k, "c") for k in range(4)
     ]
-    home0 = remote(ob.at[pl.ds(0, LB)], out.at[x], tsems, 0, "t0")
-    stay0 = pltpu.make_async_copy(ob.at[pl.ds(0, LB)], out.at[x], lsems.at[0])
-    load = pltpu.make_async_copy(wp.at[:, c], wpv, lsems.at[1])
+    load = pltpu.make_async_copy(wp.at[:, c], wpv, lsem)
     pl.when(i == 0)(load.start)
-    home1 = remote(ob.at[pl.ds(LB, LB)], out.at[x], tsems, 1, "t1")
     for k in range(4):
-
-        @pl.when(i == k)
-        def _():
-            crossing[k].start()
-            if k == 1:
-                pl.when(c != y)(home0.start)
-                pl.when(c == y)(stay0.start)
-            if k == 3:
-                home1.start()
+        pl.when(i == k)(crossing[k].start)
 
     @pl.when(i == 3)
     def _():
@@ -705,12 +836,9 @@
                     tails = [block[q * k : q * (k + 1), 2 * LANES :] for k in range(3)]
                     tails.append(jnp.zeros((q, 32), bf16))
                     b[rx, rz, 2 * DC - PA :, :] = jnp.concatenate(tails, axis=1)
-        pl.when(c != y)(home0.wait)
-        pl.when(c == y)(stay0.wait)
-        home1.wait()
-
-
-def attn_back_kernel(step, qkv, dh, hmask, out, qh, kh, vh, doh, dk, dv):
+
+
+def attn_back_kernel(step, qkv, dh, hmask, out, qh, kh, vh, doh, dk, dv, tick):
     scale = LOG2E / math.sqrt(HD)
     for h in range(HC):
         for k, ref in enumerate((qh, kh, vh)):
@@ -738,29 +866,47 @@
         out[part, :WC] = (jnp.concatenate(outs, axis=1) * (1.0 / math.sqrt(HD))).astype(bf16)
         return carry
 
-    lax.fori_loop(0, L // step, body, 0)
+    lax.fori_loop(0, L // step // 2, body, 0)
+    tick()
+    lax.fori_loop(L // step // 2, L // step, body, 0)
     for h in range(HC):
         out[:, WC + HD * h : WC + HD * (h + 1)] = (dk[h] * (1.0 / math.sqrt(HD))).astype(bf16)
         out[:, 2 * WC + HD * h : 2 * WC + HD * (h + 1)] = dv[h].astype(bf16)
 
 
-def qkv_grad_kernel(shifted, dqkv, extra, ka, sa, kb, sb, t1):
+def end_kernel(shifted, dqkv, extra, wq, d_resid, tok, mod, sums_mid, f0, f1, f2, sent_p, kept_p, freq,
+               grad, gq_o, gp_o, g1_o, g2_o, ada_o, ada_bias_o, line_o,
+               t1, ka, sa, kb, sb, ra, rb, ona, onb, r2a, r2b, zs, zk, zr, wqv, dres, tokv, fv, far, got, gb,
+               item, item_r, out_shares, square, every, row_out, row_in, mine, theirs, mine_q, theirs_q, pk, pr,
+               qsems, csems, tsems, ssems, psems, lsems):
     z, c, y, x = place()
+    t, b = 2 * y + x, 2 * z + c
+    loads = [
+        pltpu.make_async_copy(src, dst, lsems.at[k])
+        for k, (src, dst) in enumerate(
+            ((wq, wqv), (d_resid, dres), (tok.at[pl.ds(0, LH)], tokv), (f0, fv.at[0]), (f1, fv.at[1]),
+             (f2, fv.at[2]), (kept_p, pk))
+        )
+    ]
+    third_p = [remote(sent_p.at[k], pr.at[k], psems, k, f"z{k + 1}") for k in (2, 1, 0)]
+    for copy in third_p + loads:
+        copy.start()
+
     for k in range(4):
-        grad = dot_tn(shifted[:, DZ * k : DZ * (k + 1)], dqkv[...]).astype(bf16)
-        for t in range(4):
-            t1[t, DZ * k : DZ * (k + 1), :] = grad[:, 3 * DC * t : 3 * DC * (t + 1)]
+        p = dot_tn(shifted[:, DZ * k : DZ * (k + 1)], dqkv[...]).astype(bf16)
+        for j in range(4):
+            t1[j, DZ * k : DZ * (k + 1), :] = p[:, 3 * DC * j : 3 * DC * (j + 1)]
     sums = dot_nn(jnp.ones((16, L), bf16), dqkv[...])[0:1, :]
-    for zs in range(4):
-        for ts in range(4):
-            piece = DC * zs + DC // 4 * ts
+    for z_ in range(4):
+        for t_ in range(4):
+            piece = DC * z_ + DC // 4 * t_
             qsum = sums[:, piece : piece + DC // 4]
             vsum = sums[:, 2 * WC + piece : 2 * WC + piece + DC // 4]
             row1 = jnp.concatenate([jnp.zeros((1, 88), f32), qsum, jnp.zeros((1, 4), f32)], axis=1)
             row2 = jnp.concatenate([vsum, jnp.zeros((1, LANES - DC // 4), f32)], axis=1)
             add = jnp.concatenate([jnp.zeros((1, LANES), f32), row1, row2, jnp.zeros((13, LANES), f32)], axis=0)
-            rz, ry, rx = flip(z, zs), (ts // 2 + y) % 2, (ts % 2 + x) % 2
-            block = (extra[zs, ts] + add).astype(bf16)
+            rz, ry, rx = flip(z, z_), (t_ // 2 + y) % 2, (t_ % 2 + x) % 2
+            block = (extra[z_, t_] + add).astype(bf16)
 
             @pl.when(ry == 0)
             def _():
@@ -775,7 +921,7 @@
         for ry in range(2):
             for rx in range(2):
                 tt = (ry + y) % 2 * 2 + (rx + x) % 2
-                a, b = (ka, sa)[rx], (kb, sb)[ry]
+                one, two = (ka, sa)[rx], (kb, sb)[ry]
                 parts = [
                     t1[tt, pl.ds(pl.multiple_of(zz * DZ + (rc + c) % 2 * DC, 16), DC), :] for rc in range(2)
                 ]
@@ -785,124 +931,158 @@
                 for k, strip in enumerate(strips):
                     first = DC * k
                     if first + DC <= QA:
-                        a[ry, rz, first : first + DC, :] = strip
+                        one[ry, rz, first : first + DC, :] = strip
                     elif first >= QA:
-                        b[rx, rz, first - QA : first - QA + DC, :] = strip
+                        two[rx, rz, first - QA : first - QA + DC, :] = strip
                     else:
-                        a[ry, rz, first:, :] = strip[: QA - first]
-                        b[rx, rz, : first + DC - QA, :] = strip[QA - first :]
-
-
-def tail_kernel(dqkv, w, d_resid, tok, mod, sums_mid, grad, item_o, got, far, gb, other, csems, tsems, lsem):
-    i = pl.program_id(0)
-    c, y, x = place()[1:]
-    d_shifted = dot_nt(dqkv[...], w[...])
+                        one[ry, rz, first:, :] = strip[: QA - first]
+                        two[rx, rz, : first + DC - QA, :] = strip[QA - first :]
+    first_q = [
+        remote(sa.at[1], ra.at[1], qsems, 0, "x"), remote(sb.at[1], rb.at[1], qsems, 1, "y"),
+        remote(sa.at[0], ra.at[0], qsems, 2, "x"), remote(sb.at[0], rb.at[0], qsems, 3, "y"),
+    ]
+    for copy in first_q:
+        copy.start()
+
+    loads[0].wait()
     crossing = [remote(far.at[k], got.at[k], csems, k, "c") for k in range(2)]
-    sums_over = remote(item_o, other, csems, 2, "c")
-    home0 = remote(gb.at[0], grad.at[x], tsems, 0, "t0")
-    stay0 = pltpu.make_async_copy(gb.at[0], grad.at[x], lsem)
-    home1 = remote(gb.at[1], grad.at[x], tsems, 1, "t1")
     for k in range(2):
-
-        @pl.when(i == k)
-        def _():
-            far[k] = d_shifted.astype(bf16)
-            crossing[k].start()
-
-        @pl.when(i == k + 2)
-        def _():
-            crossing[k].wait()
-            total = d_shifted + got[k].astype(f32)
-            normed, inverse = normalize(tok[...].astype(f32))
-            back = d_resid[...] + normalize_back(total * (1.0 + mod[1:2, :]), normed, inverse)
-            gb[k] = back.astype(bf16)
-            sums = [jnp.sum(p, axis=0, keepdims=True) for p in (total, total * normed)]
-            if k == 0:
-                pl.when(c != y)(home0.start)
-                pl.when(c == y)(stay0.start)
-                item_o[...] = jnp.concatenate(sums + [sums_mid[0:4, :], mod[6:8, :]], axis=0)
-            else:
-                home1.start()
-                item_o[0:2, :] += jnp.concatenate(sums, axis=0)
-                sums_over.start()
-                sums_over.wait()
-                item_o[...] += other[...]
-                pl.when(c != y)(home0.wait)
-                pl.when(c == y)(stay0.wait)
-                home1.wait()
-
-
-def square_kernel(item, square, sems, lsem):
-    t = lax.axis_index("tok")
-    here = pltpu.make_async_copy(item, square.at[t], lsem)
-    copies = [remote(item, square.at[t], sems, k, name) for k, name in enumerate(("x", "y", "xy"))]
-    here.start()
-    for copy in copies:
+        far[k] = dot_nt(dqkv[LH + LB * k : LH + LB * (k + 1), :], wqv[...]).astype(bf16)
+        crossing[k].start()
+    loads[1].wait()
+    loads[2].wait()
+    total_sums = sums_mid[0:4, :]
+    token_sums = jnp.zeros((2, D), f32)
+    for k in range(2):
+        part = slice(LB * k, LB * (k + 1))
+        mine_rows = dot_nt(dqkv[part, :], wqv[...])
+        crossing[k].wait()
+        total = mine_rows + got[k].astype(f32)
+        normed, inverse = normalize(tokv[part, :].astype(f32))
+        back = dres[part, :] + normalize_back(total * (1.0 + mod[1:2, :]), normed, inverse)
+        gb[k] = back.astype(bf16)
+        token_sums += jnp.concatenate(
+            [jnp.sum(v, axis=0, keepdims=True) for v in (total, total * normed)], axis=0
+        )
+    item[...] = jnp.concatenate([token_sums, total_sums, mod[6:8, :]], axis=0)
+    over = remote(item, item_r, csems, 2, "c")
+    over.start()
+
+    for k in (3, 4, 5, 6):
+        loads[k].wait()
+    for f in range(NF):
+        mine[G1R * f : G1R * (f + 1), :] = fv[f, :G1R, :].astype(bf16)
+    swap = remote(mine, theirs, csems, 3, "c")
+    swap.start()
+    over.wait()
+    v = item[...] + item_r[...]
+    n = D // 2
+    stamp = v[6:7, :LANES]
+    pieces = ([v[0:1], v[1:2, :n]], [v[1:2, n:], v[2:3]], [v[3:4], v[4:5, :n]], [v[4:5, n:], v[5:6]])
+    for j in range(4):
+        out_shares[j] = jnp.concatenate(pieces[j] + [stamp], axis=1)
+    for j in range(4):
+        to = (y + j // 2) % 2 * 2 + (x + j) % 2
+        if j == 0:
+            square[t] = out_shares[t]
+    meeting = [
+        remote(out_shares.at[(y + j // 2) % 2 * 2 + (x + j) % 2], square.at[t], ssems, j - 1, ("x", "y", "xy")[j - 1])
+        for j in (1, 2, 3)
+    ]
+    for copy in meeting:
         copy.start()
-    here.wait()
-    for copy in copies:
-        copy.wait()
-
-
-def every_kernel(square, every, sems, lsem):
-    z = place()[0]
-    here = pltpu.make_async_copy(square, every.at[z], lsem)
-    copies = [remote(square, every.at[z], sems, k, f"z{k + 1}") for k in range(3)]
-    here.start()
-    for copy in copies:
-        copy.start()
-    here.wait()
-    for copy in copies:
-        copy.wait()
-
-
-def finish_kernel(f0, f1, f2, fp, fq, gq_o, gp_o, g1_o, g2_o, mine, theirs, sems):
-    c = place()[1]
-    for f, ref in enumerate((f0, f1, f2)):
-        mine[G1R * f : G1R * (f + 1), :] = ref[:G1R, :].astype(bf16)
-    mine[NF * G1R :, :] = fq[: 7 * DC, :].astype(bf16)
-    copy = remote(mine, theirs, sems, 0, "c")
-    copy.start()
-
-    def place_columns(own, q, first):
-        columns = jnp.concatenate(q, axis=1)
+
+    def own_columns(q, firsts, own):
+        columns = jnp.concatenate(q, axis=1) if q else None
         for core in range(2):
 
             @pl.when(c == core)
             def _():
                 at = core if own else 1 - core
-                for k in range(3):
-                    gq_o[:, DZ * k + DC * at : DZ * k + DC * (at + 1)] = columns[:, DC * k : DC * (k + 1)]
-                for f in range(NF):
+                if q:
+                    for k in range(3):
+                        gq_o[:, DZ * k + DC * at : DZ * k + DC * (at + 1)] = columns[:, DC * k : DC * (k + 1)]
+                for f, pair in enumerate(firsts):
                     start = FF // 8 * at + FZ * f
-                    g1_o[:, start : start + FZ] = jnp.concatenate(first[f], axis=1)
-
-    q = fq[...]
-    place_columns(
-        True,
-        [q[0:DC], q[2 * DC : 3 * DC], q[4 * DC : 5 * DC], q[6 * DC : 7 * DC, : DC // 3]],
-        [[f[:DC, :], f[2 * DC : 3 * DC, : FZ - LANES]] for f in (f0, f1, f2)],
-    )
-    for f, ref in enumerate((f0, f1, f2)):
-        part = ref[G1R:, :]
+                    g1_o[:, start : start + FZ] = jnp.concatenate(pair, axis=1)
+
+    own_columns(None, [[fv[f, :DC, :], fv[f, 2 * DC : 3 * DC, : FZ - LANES]] for f in range(NF)], True)
+    for f in range(NF):
+        part = fv[f, G1R:, :]
         tail = part[2 * FZ :]
         tail = jnp.concatenate([tail[:, 32 * k : 32 * (k + 1)] for k in range(4)], axis=0)
         g2_o[FZ * f : FZ * (f + 1), :] = jnp.concatenate([part[:FZ], part[FZ : 2 * FZ], tail], axis=1)
-    part = fp[...]
+
+    for copy in first_q:
+        copy.wait()
+    for kv, rv, on in ((ka, ra, ona), (kb, rb, onb)):
+        on[...] = (kv[1].astype(f32) + rv[1].astype(f32)).astype(bf16)
+    second_q = [remote(ona, r2a, qsems, 4, "y"), remote(onb, r2b, qsems, 5, "x")]
+    for copy in second_q:
+        copy.start()
+    for copy in third_p + meeting:
+        copy.wait()
+    spread_z = [remote(square, every.at[z], ssems, 2 + k, f"z{k}") for k in (1, 2, 3)]
+    every[z] = square[...]
+    for copy in spread_z:
+        copy.start()
+    part = pk[...] + pr[0].astype(f32) + pr[1].astype(f32) + pr[2].astype(f32)
     tail = part[2 * DC :]
     tail = jnp.concatenate([tail[:, 32 * k : 32 * (k + 1)] for k in range(3)], axis=0)
     gp_o[...] = jnp.concatenate([part[:DC], part[DC : 2 * DC], tail], axis=1)
-    copy.wait()
-    got = theirs[...].astype(f32)
-    q = got[NF * G1R :]
-    place_columns(
-        False,
-        [q[DC : 2 * DC], q[3 * DC : 4 * DC], q[5 * DC : 6 * DC], q[6 * DC :, 64 : 64 + DC // 3]],
+    swap.wait()
+    own_columns(
+        None,
         [
-            [got[G1R * f + DC : G1R * f + 2 * DC], got[G1R * f + 2 * DC : G1R * (f + 1), FZ - LANES :]]
+            [theirs[G1R * f + DC : G1R * f + 2 * DC, :].astype(f32),
+             theirs[G1R * f + 2 * DC : G1R * (f + 1), FZ - LANES :].astype(f32)]
             for f in range(NF)
         ],
-    )
+        False,
+    )
+
+    for copy in second_q:
+        copy.wait()
+    layer_sums([(ka.at[0], ra.at[0], r2a), (kb.at[0], rb.at[0], r2b)], zs, zk)
+    third_q = [remote(zs.at[k], zr.at[k], qsems, 6 + k, f"z{k + 1}") for k in (2, 1, 0)]
+    for copy in third_q:
+        copy.start()
+    home = homeward(gb.at[0], gb.at[1], grad, tsems, lsems.at[7])
+    home_start(*home)
+
+    for copy in spread_z:
+        copy.wait()
+    columns = jnp.concatenate([every[i, j] for i in range(4) for j in range(4)], axis=0)
+    width = 3 * D // 2
+    angles = columns[:, width : width + 1] * freq[b % 4]
+    cond = jax.nn.silu(jnp.where(b < 4, jnp.cos(angles), jnp.sin(angles))).astype(bf16).astype(f32)
+    columns = columns[:, :width]
+    ada_o[...] = lax.dot_general(
+        cond, columns, (((0,), (0,)), ((), ())), precision=lax.Precision.HIGHEST, preferred_element_type=f32
+    )
+    row = jnp.sum(columns, axis=0, keepdims=True)
+    row_out[0] = row
+    row_in[t] = row
+    rows_ = [remote(row_out.at[0], row_in.at[t], ssems, 6 + j, name) for j, name in enumerate(("x", "y", "xy"))]
+    for copy in rows_:
+        copy.start()
+    for copy in rows_:
+        copy.wait()
+    row = row_in[z]
+    ada_bias_o[...] = jnp.where(c == 0, row[:, : width // 2], row[:, width // 2 :])
+
+    for copy in third_q:
+        copy.wait()
+    q = zk[...] + zr[0].astype(f32) + zr[1].astype(f32) + zr[2].astype(f32)
+    mine_q[...] = q[: 7 * DC].astype(bf16)
+    swap = remote(mine_q, theirs_q, csems, 4, "c")
+    swap.start()
+    line_o[...] = q[7 * DC :]
+    own_columns([q[0:DC], q[2 * DC : 3 * DC], q[4 * DC : 5 * DC], q[6 * DC : 7 * DC, : DC // 3]], [], True)
+    swap.wait()
+    q = theirs_q[...].astype(f32)
+    own_columns([q[DC : 2 * DC], q[3 * DC : 4 * DC], q[5 * DC : 6 * DC], q[6 * DC :, 64 : 64 + DC // 3]], [], False)
+    home_wait(*home)
 
 
 def one_item_per_chip(
@@ -927,11 +1107,11 @@
         (sds((L, D), bf16), sds((L, D), bf16), sds((L, D), bf16), sds((L, 3 * WC), bf16), sds((D, 3 * WC), bf16),
          sds((NF, D, FB), bf16), sds((8, D), f32), sds((L, 1), f32), sds((1, WC), f32), sds((NF, 1, FB), f32),
          sds((NF, 1, FB), f32)),
-        (tokens, cotangent, ints, ada_weight, ada_bias.reshape(1, ada_cols), freq, head_masks.T, channel_masks.T,
+        (tokens, cotangent, ints, ada_weight.T, ada_bias.reshape(1, ada_cols), freq, head_masks.T, channel_masks.T,
          w_qkv, w_fc1, q_bias.reshape(1, D), v_bias.reshape(1, D), fc1_bias.reshape(1, FF)),
         in_specs=[ANY, ANY, vmem, ANY, vmem, vmem, vmem, vmem, ANY, ANY, vmem, vmem, vmem],
         out_specs=[ANY, ANY, vmem, vmem, ANY, ANY] + [vmem] * 5,
-        scratch=[vm(L, D), vm(L, D), vm(D, 3 * D), vm(D, 3 * WC), vm(D, FF), vm(NF, D, FB), vm(D, ada_cols),
+        scratch=[vm(L, D), vm(L, D), vm(D, 3 * D), vm(D, 3 * WC), vm(D, FF), vm(NF, D, FB), vm(ada_cols, D),
                  vm(8, LANES, dtype=jnp.int32), vm(8, ada_cols, dtype=f32), vm(3, 8, ada_cols, dtype=f32),
                  vm(4, 8, ada_cols, dtype=f32), pltpu.SemaphoreType.DMA((2, 5)), pltpu.SemaphoreType.DMA((2, 4)),
                  pltpu.SemaphoreType.DMA((2, 3)), pltpu.SemaphoreType.DMA((6,))],
@@ -994,21 +1174,20 @@
     slot_a, slot_b = sds((2, 4, PA, LANES), bf16), sds((2, 4, PR - PA, LANES), bf16)
     own, given = call(
         middle_kernel, "middle",
-        (sds((LH, D), f32), sds((2, LB, D), bf16), sds((L, WC), bf16), slot_a, slot_a, slot_b, slot_b,
+        (sds((LH, D), f32), sds((LH, D), bf16), sds((L, WC), bf16), slot_a, slot_a, slot_b, slot_b,
          sds((8, D), f32), sds((8, D), f32)),
         (before[1], ds2_r, before[0], branch_r, attn, tok, g_all, kept, mod, fc2_bias.astype(f32).reshape(1, D),
          mixed, wp),
         grid=(4,),
         in_specs=[row] * 7 + [rows(n, 1), full((8, D)), full((1, D)), once(L, WC), ANY],
-        out_specs=(row, ANY, full((L, WC)), full(slot_a.shape), full(slot_a.shape), full(slot_b.shape),
+        out_specs=(row, row, full((L, WC)), full(slot_a.shape), full(slot_a.shape), full(slot_b.shape),
                    full(slot_b.shape), full((8, D)), full((8, D))),
-        scratch=[vm(L, D), vm(LH, D), vm(4, WC, TD), vm(4, DC, D), pltpu.SemaphoreType.DMA((2, 4)),
-                 pltpu.SemaphoreType.DMA((2, 2)), pltpu.SemaphoreType.DMA((2,))],
-        peers=("c", "t0", "t1"), cid=3,
+        scratch=[vm(L, D), vm(4, WC, TD), vm(4, DC, D), pltpu.SemaphoreType.DMA((2, 4)), pltpu.SemaphoreType.DMA],
+        peers=("c",), cid=3,
         jobs=[FirstSum(*slots), SecondSum(*firsts[1], *kepts[1]), ThirdSum(*results[0])],
         flops=4 * L * D * WC, nbytes=20e6,
     )
-    d_resid, output, dh, *slots_p, sums_mid, sum_attn = own
+    d_resid, out_rows, dh, *slots_p, sums_mid, sum_attn = own
     firsts.append(given[0])
     results.append(given[1])
     finals = [given[2][0]]
@@ -1016,79 +1195,47 @@
         functools.partial(attn_back_kernel, 512), "attn_back",
         sds((L, 3 * WC), bf16), (qkv, dh, hmask),
         scratch=[vm(HC, L, HD)] * 4 + [vm(HC, L, HD, dtype=f32)] * 2,
-        cid=4, jobs=[FirstSum(*slots_p), SecondSum(*firsts[2], *kepts[2]), ThirdSum(*results[1])],
+        cid=4, ticks=True,
+        jobs=[SecondThird(*firsts[2], *kepts[2]), FirstSecond(*slots_p), ThirdSum(*results[1]), GoHome(out_rows)],
         flops=30e9, nbytes=9e6,
     )
-    first_p = given[0]
-    results.append(given[1])
-    finals.append(given[2][0])
+    finals += [given[2][0], given[0][0]]
+    sent_p, kept_p = given[1]
+    output = given[3][0]
     sum_fc1 = jnp.concatenate(sums1, axis=0).reshape(NF, 4, FZ).transpose(1, 0, 2).reshape(4, 4, FF // 32)
     own_part = lambda v: core_half(v, 4, 2, 4, D // 32)
     line = jnp.concatenate(
         [sum_fc1, own_part(sum2), own_part(sum_attn[0]), jnp.zeros((4, 4, 3 * LANES - FF // 32 - D // 16), f32)], axis=2
     ).reshape(4, 4, 3, LANES)
     extra = jnp.concatenate([line, jnp.zeros((4, 4, 13, LANES), f32)], axis=2)
-    slot_q = sds((2, 4, QA, LANES), bf16)
-    slots_q, given = call(
-        qkv_grad_kernel, "qkv_grad",
-        (slot_q,) * 4, (shifted, dqkv, extra),
-        scratch=[vm(4, D, 3 * DC)],
-        cid=5, jobs=[SecondSum(*first_p, slots_p[0], slots_p[2]), ThirdSum(*results[2])],
-        flops=2 * L * D * 3 * WC, nbytes=12e6,
-    )
-    result_p = given[0]
-    finals.append(given[1][0])
-    near = pl.BlockSpec((LB, D), lambda i: (jnp.maximum(i - 2, 0), 0))
-    (grad_rows, item), given = call(
-        tail_kernel, "tail",
-        (sds((2, LB, D), bf16), sds((8, D), f32)),
-        (dqkv, wq, d_resid, tok, mod, sums_mid),
-        grid=(4,),
-        in_specs=[pl.BlockSpec((LB, 3 * WC), lambda i: ((i + 2) % 4, 0)), once(D, 3 * WC), near, near, full((8, D)),
-                  full((8, D))],
-        out_specs=(ANY, full((8, D))),
-        scratch=[vm(2, LB, D), vm(2, LB, D), vm(2, LB, D), vm(8, D, dtype=f32), pltpu.SemaphoreType.DMA((2, 3)),
-                 pltpu.SemaphoreType.DMA((2, 2)), pltpu.SemaphoreType.DMA],
-        peers=("c", "t0", "t1"), cid=6, jobs=[FirstSum(*slots_q), ThirdSum(*result_p)],
-        flops=2 * L * D * 3 * WC, nbytes=12e6,
-    )
-    first_q, final_p = given[0], given[1][0]
+    slot_q = vm(2, 4, QA, LANES)
+    fourth = vm(4, QA, LANES)
+    width = ada_cols + LANES
+    dma = pltpu.SemaphoreType.DMA
+    (grad_rows, gq, gp, g1, g2, grad_ada_weight, grad_ada_bias, line), _ = call(
+        end_kernel, "end",
+        (sds((2, LB, D), bf16), sds((DC, 3 * TD), f32), sds((DC, TD), f32), sds((DC, FF // 4), f32),
+         sds((FF // 8, TD), f32), sds((DC, ada_cols), f32), sds((1, ada_cols // 2), f32), sds((16, LANES), f32)),
+        (shifted, dqkv, extra, wq, d_resid, tok, mod, sums_mid, *finals, sent_p, kept_p, freq.reshape(4, 1, DC)),
+        in_specs=[vmem] * 3 + [ANY] * 3 + [vmem] * 2 + [ANY] * 5 + [vmem],
+        out_specs=[ANY] + [vmem] * 7,
+        scratch=[vm(4, D, 3 * DC)] + [slot_q] * 6 + [fourth] * 4
+        + [vm(3, QR, LANES), vm(QR, LANES, dtype=f32), vm(3, QR, LANES), vm(D, 3 * WC), vm(LH, D, dtype=f32),
+           vm(LH, D), vm(NF, G1R + G2R, LANES, dtype=f32)] + [vm(2, LB, D)] * 3
+        + [vm(8, D, dtype=f32)] * 2 + [vm(4, 1, width, dtype=f32)] * 2
+        + [vm(4, 4, 1, width, dtype=f32), vm(1, 1, ada_cols, dtype=f32), vm(4, 1, ada_cols, dtype=f32)]
+        + [vm(NF * G1R, LANES)] * 2 + [vm(7 * DC, LANES)] * 2 + [vm(PR, LANES, dtype=f32), vm(3, PR, LANES)]
+        + [dma((2, 9)), dma((2, 5)), dma((2, 2)), dma((2, 9)), dma((2, 3)), dma((8,))],
+        peers=("c", "t0", "t1", "x", "y", "xy", "z1", "z2", "z3"), cid=5,
+        flops=4 * L * D * 3 * WC, nbytes=30e6,
+    )
     grad_tokens = grad_rows.astype(f32)
-    square, given = call(
-        square_kernel, "square", sds((4, 8, D), f32), (item,),
-        scratch=[pltpu.SemaphoreType.DMA((2, 3)), pltpu.SemaphoreType.DMA],
-        peers=("x", "y", "xy"), cid=7, jobs=[SecondSum(*first_q, slots_q[0], slots_q[2])],
-    )
-    every, given = call(
-        every_kernel, "every", sds((4, 4, 8, D), f32), (square,),
-        scratch=[pltpu.SemaphoreType.DMA((2, 3)), pltpu.SemaphoreType.DMA],
-        peers=("z1", "z2", "z3"), cid=8, jobs=[ThirdSum(*given[0])],
-    )
-    final_q = given[0][0]
-
-    every = every.reshape(16, 8, D)
-    cond_all = jax.nn.silu(step_embedding(every[:, 6, 0], D)).astype(bf16).astype(f32)
-    every = every[:, :6].reshape(16, 6 * D)
-    cond_rows = lax.dynamic_slice_in_dim(cond_all, b * DC, DC, 1)
-    columns = lax.dynamic_slice_in_dim(every, t * ada_cols, ada_cols, 1)
-    grad_ada_weight = lax.dot_general(
-        cond_rows, columns, (((0,), (0,)), ((), ())), precision=lax.Precision.HIGHEST
-    )
-    bias_cols = 6 * D // 8
-    grad_ada_bias = jnp.sum(lax.dynamic_slice_in_dim(every, b * bias_cols, bias_cols, 1), axis=0)
-
-    (gq, gp, g1, g2), _ = call(
-        finish_kernel, "finish",
-        (sds((DC, 3 * TD), f32), sds((DC, TD), f32), sds((DC, FF // 4), f32), sds((FF // 8, TD), f32)),
-        (*finals, final_p, final_q),
-        scratch=[vm(NF * G1R + 7 * DC, LANES), vm(NF * G1R + 7 * DC, LANES), pltpu.SemaphoreType.DMA((2, 1))],
-        peers=("c",), cid=9, nbytes=6e6,
-    )
-    line = final_q[7 * DC :].reshape(-1)
+    line = line.reshape(-1)
     n1, n = FF // 32, D // 32
     b_fc1, b_fc2, b_proj = line[:n1], line[n1 : n1 + n], line[n1 + n : n1 + 2 * n]
     b_q, b_v = line[n1 + 2 * n : n1 + 3 * n], line[2 * LANES : 2 * LANES + n]
-    return (output, grad_tokens, gq, b_q, b_v, gp, b_proj, g1, b_fc1, g2, b_fc2, grad_ada_weight, grad_ada_bias)
+    return (output, grad_tokens, gq, b_q, b_v, gp, b_proj, g1, b_fc1, g2, b_fc2, grad_ada_weight,
+            grad_ada_bias.reshape(-1))
 
 
 def gelu_tanh(values):

time: 432 us -> 355 us (0.82)
  Pallas kernels: 394 us -> 321 us
    pallas_call x12 -> x8, Pallas kernels: 394 us -> 321 us  [call(): pl.pallas_call(run, out_shape=out_shape + [o for j in jobs for o in j.out...]
    unnamed x45 -> x32, local copies, waits for them, and re-layouts: 14.9 us -> 8.24 us
where the time goes in v4:
time: 355 us; the launch traced here: 350 us
  Pallas kernels  321 us (90%)
  local copies, waits for them, and re-layouts  20 us (6%)
  other arithmetic  6.99 us (2%)
    pallas_call x8, Pallas kernels, call(): pl.pallas_call(run, out_shape=out_shape + [o for j in jobs for o in j.out...  321 us
    unnamed x32, local copies, waits for them, and re-layouts  8.24 us

profile of v4, /device:TPU:0, one launch (start us, length us, event | category | flops | bytes accessed | tf_op | source)
XLA Modules:
  0.0 349.8 jit_solution(11363436484830481092)
XLA Ops:
  0.6 1.4 copy.36
  2.0 1.3 reshape.113.refs_12_
  4.7 0.7 add_bitcast_fusion
  6.2 1.4 copy.35
  7.5 1.3 reshape.110.refs_4_
  8.8 1.3 reshape.111.refs_10_
  10.1 1.3 reshape.112.refs_11_
  12.0 42.2 %front.1 = (bf16[1024,1152]{1,0:T(8,128)(2,1)}, bf16[1024,1152]{1,0:T(8,128)(2,1)}, bf16[1024,1152]{1,0:T(8,128)(2,1)}, bf16[1024,1728]{1,0:T(8,128)(2,1)}, bf16...) custom-call(bf16[2,256,1152]{2,1,0:T(8,128)(2,1)} %refs_0_.1, ...), custom_call_target="tpu_custom_call" | custom-call | flops 4076863488 | bytes 50000000 | tf_op jit(solution)/shard_map/front/pallas_call | solution.py:423
  54.7 30.7 %attn.1 = (bf16[1024,576]{1,0:T(8,128)(2,1)}, bf16[1024,1152]{1,0:T(8,128)(2,1)}, f32[512,1152]{1,0:T(8,128)}) custom-call(bf16[1024,1728]{1,0:T(8,128)(2,1)} %get-tuple-element.91.refs_0_, f32[1,576]{1,0:T(1,128)} %get-tuple-element.92.refs_1_.refs_2_, bf16[4,2,144,1152]{3,2,1,0:T(8,128)(2,1)} %bitcast.18, f32[1,1152]{1,0:T(1,128)} %reshape.127.refs_3_, ...), custom_call_target="tpu_custom_call" | custom-call | flops 16000000000 | bytes 5000000 | tf_op jit(solution)/shard_map/attn/pallas_call | solution.py:423
  85.5 21.6 %mlp0.1 = (bf16[2,4,432,128]{3,2,1,0:T(8,128)(2,1)}, bf16[2,4,432,128]{3,2,1,0:T(8,128)(2,1)}, bf16[2,4,432,128]{3,2,1,0:T(8,128)(2,1)}, bf16[2,4,432,128]{3,2,1...) custom-call(bf16[1024,1152]{1,0:T(8,128)(2,1)} %get-tuple-element.95, ...), custom_call_target="tpu_custom_call" | custom-call | flops 10871635968 | bytes 20000000 | tf_op jit(solution)/shard_map/mlp0/pallas_call | solution.py:423
  107.0 28.3 %mlp1.1 = (bf16[2,4,432,128]{3,2,1,0:T(8,128)(2,1)}, bf16[2,4,432,128]{3,2,1,0:T(8,128)(2,1)}, bf16[2,4,432,128]{3,2,1,0:T(8,128)(2,1)}, bf16[2,4,432,128]{3,2,1...) custom-call(bf16[1024,1152]{1,0:T(8,128)(2,1)} %get-tuple-element.95, ...), custom_call_target="tpu_custom_call" | custom-call | flops 10871635968 | bytes 20000000 | tf_op jit(solution)/shard_map/mlp1/pallas_call | solution.py:423
  135.4 38.6 %mlp2.1 = (bf16[2,4,432,128]{3,2,1,0:T(8,128)(2,1)}, bf16[2,4,432,128]{3,2,1,0:T(8,128)(2,1)}, bf16[2,4,432,128]{3,2,1,0:T(8,128)(2,1)}, bf16[2,4,432,128]{3,2,1...) custom-call(bf16[1024,1152]{1,0:T(8,128)(2,1)} %get-tuple-element.95, ...), custom_call_target="tpu_custom_call" | custom-call | flops 10871635968 | bytes 20000000 | tf_op jit(solution)/shard_map/mlp2/pallas_call | solution.py:423
  175.5 38.5 %middle.1 = (f32[512,1152]{1,0:T(8,128)}, bf16[512,1152]{1,0:T(8,128)(2,1)}, bf16[1024,576]{1,0:T(8,128)(2,1)}, bf16[2,4,176,128]{3,2,1,0:T(8,128)(2,1)}, bf16[2...) custom-call(bf16[512,1152]{1,0:T(8,128)(2,1)} %get-tuple-element.117, ...), custom_call_target="tpu_custom_call" | custom-call | flops 2717908992 | bytes 20000000 | tf_op jit(solution)/shard_map/middle/pallas_call | solution.py:423
  214.0 0.8 slice_reduce_fusion
  216.0 47.7 %attn_back.1 = (bf16[1024,1728]{1,0:T(8,128)(2,1)}, f32[864,128]{1,0:T(8,128)}, bf16[3,336,128]{2,1,0:T(8,128)(2,1)}, f32[336,128]{1,0:T(8,128)}, f32[864,128]{1,0:T(8,128)}, /*index=5*/bf16[2,256,1152]{2,1,0:T(8,128)(2,1)}) custom-call(bf16[1024,1728]{1,0:T(8,128)(2,1)} %get-tuple-element.91.refs_0_, bf16[1024,576]{1,0:T(8,128)(2,1)} %get-tuple-element.133.refs_1_, ...), custom_call_target="tpu_custom_call" | custom-call | flops 30000001024 | bytes 9000000 | tf_op jit(solution)/shard_map/attn_back/pallas_call | solution.py:423
  264.3 73.5 %end.1 = (bf16[2,256,1152]{2,1,0:T(8,128)(2,1)}, f32[144,864]{1,0:T(8,128)}, f32[144,288]{1,0:T(8,128)}, f32[144,1152]{1,0:T(8,128)}, f32[576,288]{1,0:T(8,128)}...) custom-call(bf16[1024,1152]{1,0:T(8,128)(2,1)} %get-tuple-element.146.refs_0_, ...), custom_call_target="tpu_custom_call" | custom-call | flops 8153726976 | bytes 30000000 | tf_op jit(solution)/shard_map/end/pallas_call | solution.py:423
  337.8 3.0 convert_element_type.2
  340.8 1.2 copy.39
  342.6 1.4 fusion
  344.0 1.2 slice.27
  345.3 1.0 copy.48
  346.3 0.8 copy.49
  347.8 0.8 copy.51
  348.6 1.0 copy.52
  (48 shorter events, 7.2 us)
Async XLA Ops:
  12.0 42.2 %copy-start.7 = (bf16[1152]{0:T(1024)(128)(2,1)S(1)}, bf16[1152]{0:T(1024)(128)(2,1)}, u32[]{:S(2)}) copy-start(bf16[1152]{0:T(1024)(128)(2,1)} %param.29) | copy-start | bytes 6916
  135.4 38.6 %copy-start.10 = (f32[1,768]{1,0:T(1,128)S(1)}, f32[1,768]{1,0:T(1,128)}, u32[]{:S(2)}) copy-start(f32[1,768]{1,0:T(1,128)} %get-tuple-element.148) | copy-start | bytes 9220
  135.4 38.6 %copy-start.11 = (f32[1,768]{1,0:T(1,128)S(1)}, f32[1,768]{1,0:T(1,128)}, u32[]{:S(2)}) copy-start(f32[1,768]{1,0:T(1,128)} %get-tuple-element.149) | copy-start | bytes 9220
  135.4 39.5 %copy-start.8 = (bf16[1152]{0:T(1024)(128)(2,1)S(1)}, bf16[1152]{0:T(1024)(128)(2,1)}, u32[]{:S(2)}) copy-start(bf16[1152]{0:T(1024)(128)(2,1)} %param.33) | copy-start | bytes 6916
  175.5 39.4 %copy-start.6 = (f32[1,1152]{1,0:T(1,128)S(1)}, f32[1,1152]{1,0:T(1,128)}, u32[]{:S(2)}) copy-start(f32[1,1152]{1,0:T(1,128)} %get-tuple-element.151) | copy-start | bytes 13828
  337.8 3.0 copy-start.2
  337.8 4.2 %copy-start.9 = (f32[1,864]{1,0:T(1,128)S(1)}, f32[1,864]{1,0:T(1,128)}, u32[]{:S(2)}) copy-start(f32[1,864]{1,0:T(1,128)} %get-tuple-element.168) | copy-start | bytes 10372
  337.8 7.4 %copy-start = (bf16[2,256,1152]{2,1,0:T(8,128)(2,1)S(1)}, bf16[2,256,1152]{2,1,0:T(8,128)(2,1)}, u32[]{:S(2)}) copy-start(bf16[2,256,1152]{2,1,0:T(8,128)(2,1)} %get-tuple-element.214) | copy-start | bytes 3538948
  340.8 5.5 %copy-start.4 = (f32[144,864]{1,0:T(8,128)S(1)}, f32[144,864]{1,0:T(8,128)}, u32[]{:S(2)}) copy-start(f32[144,864]{1,0:T(8,128)} %get-tuple-element.216) | copy-start | bytes 1492996
  340.8 6.3 %copy-start.5 = (f32[144,288]{1,0:T(8,128)S(1)}, f32[144,288]{1,0:T(8,128)}, u32[]{:S(2)}) copy-start(f32[144,288]{1,0:T(8,128)} %get-tuple-element.219) | copy-start | bytes 497668
  340.8 6.9 %copy-start.3 = (f32[144,1152]{1,0:T(8,128)S(1)}, f32[144,1152]{1,0:T(8,128)}, u32[]{:S(2)}) copy-start(f32[144,1152]{1,0:T(8,128)} %get-tuple-element.221) | copy-start | bytes 1990660
  345.3 3.3 copy-start.1

commit v5 on v4

--- a/solution.py
+++ b/solution.py
@@ -3,6 +3,7 @@
 
 import jax
 import jax.numpy as jnp
+import numpy as np
 from jax import lax
 from jax.experimental import pallas as pl
 from jax.experimental.pallas import tpu as pltpu
@@ -181,7 +182,8 @@
         oa, qa, ob, qb, ka, kb = ins
         kav, qav, rav, kbv, qbv, rbv, _, _, sems, local = scratch
         far = [remote(oa, rav, sems, 0, "y"), remote(ob, rbv, sems, 1, "x")]
-        pairs = [(ka.at[0], kav), (qa, qav), (kb.at[0], kbv), (qb, qbv)]
+        whole = len(ka.shape) == 4
+        pairs = [(ka.at[0] if whole else ka, kav), (qa, qav), (kb.at[0] if whole else kb, kbv), (qb, qbv)]
         return far, [pltpu.make_async_copy(a, b, local.at[k]) for k, (a, b) in enumerate(pairs)]
 
     def finish(self, ins, outs, scratch):
@@ -454,9 +456,9 @@
     return lax.broadcasted_iota(jnp.int32, (n, 1), 0)
 
 
-def front_kernel(tokens, cotangent, ints, ada_w, ada_b, freq, heads_t, channels_t, w_qkv, w_fc1, q_bias, v_bias, b1,
-                 tok_o, cot_o, shifted_o, qkv_o, wq_o, w1_o, mod_o, kept_o, hmask_o, chan_o, b1_o,
-                 tk, ck, wqv, wqc, w1v, w1c, adav, ints_other, m4, to_send, shares, csems, tsems, ssems, lsems):
+def front_kernel(tokens, cotangent, timesteps, bucket_ids, skips, ada_w, ada_b, head_masks, channel_masks, w_qkv, w_fc1,
+                 q_bias, v_bias, b1, freq, tok_o, cot_o, shifted_o, qkv_o, wq_o, w1_o, mod_o, kept_o, hmask_o, chan_o, b1_o,
+                 tk, ck, wqv, wqc, w1v, w1c, adav, ints, ints_other, m4, to_send, shares, csems, tsems, ssems, lsems):
     z, c, y, x = place()
     t = 2 * y + x
     loads = [
@@ -492,6 +494,10 @@
 
     tok_moves, cot_moves = arrivals(tokens, tk, 0), arrivals(cotangent, ck, 1)
     leave(*tok_moves)
+    halves = [skips[:, :LANES], skips[:, LANES:]]
+    ints[0:4, :] = jnp.concatenate([halves[0][0:1], halves[1][0:1], halves[0][1:2], halves[1][1:2]], axis=0)
+    for k, value in enumerate((timesteps[0], timesteps[1], bucket_ids[0], 0)):
+        ints[4 + k : 5 + k, :] = jnp.full((1, LANES), value, jnp.int32)
     swap = remote(ints, ints_other, csems, 4, "c")
     swap.start()
     for load in loads:
@@ -499,17 +505,16 @@
     swap.wait()
 
     mine, other = ints[...], ints_other[...]
-    mine_t, other_t = mine[4:5, :].astype(f32), other[4:5, :].astype(f32)
     r = column(8)
     steps = jnp.zeros((8, 1), f32)
     for k in range(2):
-        steps = jnp.where(r == 2 * c + k, mine_t[:, k : k + 1], steps)
-        steps = jnp.where(r == 2 * (1 - c) + k, other_t[:, k : k + 1], steps)
+        steps = jnp.where(r == 2 * c + k, mine[4 + k : 5 + k, 0:1].astype(f32), steps)
+        steps = jnp.where(r == 2 * (1 - c) + k, other[4 + k : 5 + k, 0:1].astype(f32), steps)
     angles = steps * freq[...]
     condition = jax.nn.silu(jnp.concatenate([jnp.cos(angles), jnp.sin(angles)], axis=1))
     condition = jnp.concatenate([condition, jnp.zeros_like(condition)], axis=0).astype(bf16)
     loads[0].wait()
-    m4[...] = dot_nt(condition, adav[...])[:8] + ada_b[...].astype(f32)
+    m4[...] = dot_nt(condition, adav[...])[:8] + ada_b[...].astype(f32).reshape(1, -1)
     moves = []
     for k in range(4):
         to = (y + k // 2) % 2 * 2 + (x + k) % 2
@@ -522,7 +527,7 @@
             moves[-1].start()
 
     group = jnp.where(c == y, mine, other)
-    bucket = group[4:5, 2:3]
+    bucket = group[6:7, 0:1]
     skip = jnp.where(x == 0, group[0:2], group[2:4])
     for j in range(4):
         block = 2 * ((c + j // 2) % 2) + (x + j) % 2
@@ -531,31 +536,35 @@
         kept_o[LB * j : LB * (j + 1), :] = 1.0 - jnp.max(hit, axis=1, keepdims=True)
 
     def chosen(masks):
-        lane = lax.broadcasted_iota(jnp.int32, masks.shape, 1)
-        return jnp.sum(jnp.where(lane == bucket, masks[...].astype(f32), 0.0), axis=1, keepdims=True)
+        line = lax.broadcasted_iota(jnp.int32, masks.shape, 0)
+        row = jnp.sum(jnp.where(line == bucket, masks[...].astype(f32), 0.0), axis=0, keepdims=True)
+        return jnp.broadcast_to(row, (16, masks.shape[1])).astype(bf16)
 
     def spread(on, low, width):
-        first = width * lax.broadcasted_iota(jnp.int32, (on.shape[0], low.shape[1]), 0)
-        return jnp.sum(jnp.where((low >= first) & (low < first + width), on, 0.0), axis=0, keepdims=True)
+        first = width * lax.broadcasted_iota(jnp.int32, (on.shape[1], low.shape[1]), 0)
+        return dot_nn(on, jnp.where((low >= first) & (low < first + width), 1.0, 0.0).astype(bf16))[0:1, :]
 
     lane = lax.broadcasted_iota(jnp.int32, (1, WC), 1)
     share = sum(jnp.where(lane >= DC * k, 1, 0) for k in range(1, 4))
-    hmask_o[...] = spread(chosen(heads_t), lane + DC * (share + c), HD)
-    channels = chosen(channels_t)
+    hmask_o[...] = spread(chosen(head_masks), lane + DC * (share + c), HD)
+    channels = chosen(channel_masks)
     lane = lax.broadcasted_iota(jnp.int32, (1, FB), 1)
     share = sum(jnp.where(lane >= FZ * k, 1, 0) for k in range(1, 4))
     for f in range(NF):
         low = lane + (4 * DZ - FZ) * share + FF // 8 * c + FZ * f
-        chan_o[f] = spread(channels, low, FF // channels.shape[0])
+        chan_o[f] = spread(channels, low, FF // channels.shape[1])
 
     def half(v, k, width):
-        v = v[:, 2 * width * k : 2 * width * (k + 1)].astype(f32)
+        v = v[:, 2 * width * k : 2 * width * (k + 1)]
         return jnp.where(c == 0, v[:, :width], v[:, width:])
 
-    bias = [half(q_bias[...], k, DC) for k in range(4)]
-    bias += [jnp.zeros((1, WC), f32)] + [half(v_bias[...], k, DC) for k in range(4)]
+    def line(ref):
+        return ref[...].astype(f32).reshape(1, -1)
+
+    bias = [half(line(q_bias), k, DC) for k in range(4)]
+    bias += [jnp.zeros((1, WC), f32)] + [half(line(v_bias), k, DC) for k in range(4)]
     bias = jnp.concatenate(bias, axis=1)
-    b1v = [half(b1[...], k, FF // 8) for k in range(4)]
+    b1v = [half(line(b1), k, FF // 8) for k in range(4)]
     for f in range(NF):
         b1_o[f] = jnp.concatenate([v[:, FZ * f : FZ * (f + 1)] for v in b1v], axis=1)
     loads[1].wait()
@@ -652,9 +661,10 @@
     for i in range(L // step):
         crossing(i).wait()
     w_mine, w_other = wpv[0].reshape(WC, D), wpv[1].reshape(WC, D)
+    bias_line = bias[...].astype(f32).reshape(1, D)
     for j in range(4):
         part = slice(LB * j, LB * (j + 1))
-        attn = dot_nn(mx[part, :], w_mine) + dot_nn(mo[part, :], w_other) + bias[...]
+        attn = dot_nn(mx[part, :], w_mine) + dot_nn(mo[part, :], w_other) + bias_line
         if j < 2:
             attn_o[part, :] = attn
         normed, _ = normalize(tkv[part, :].astype(f32) + mod[2:3, :] * attn)
@@ -662,119 +672,151 @@
     keep.wait()
 
 
-def pack_hidden(block1, block2, o1, o2, ry, rx, rz):
-    o1[ry, rz, : 2 * DC, :] = block1[:, :LANES]
-    o1[ry, rz, 2 * DC :, :] = jnp.concatenate([block1[:DC, LANES:], block1[DC:, LANES:]], axis=1)
-    o2[rx, rz, :FZ, :] = block2[:, :LANES]
-    o2[rx, rz, FZ : 2 * FZ, :] = block2[:, LANES : 2 * LANES]
-    q = FZ // 4
-    o2[rx, rz, 2 * FZ :, :] = jnp.concatenate([block2[q * k : q * (k + 1), 2 * LANES :] for k in range(4)], axis=1)
-
-
-def mlp_kernel(f, *refs):
-    last = f == NF - 1
-    refs = list(refs)
-    sh2, g, kept, mod, w1, b1, chan, w2 = refs[:8]
-    del refs[:8]
-    before = None
-    if f > 0:
-        before = refs[:2]
-        del refs[:2]
-    slots, branch_o, ds2_o, sum1_o, sum2_o = refs[:4], refs[4], refs[5], refs[6], refs[7]
-    del refs[:8]
-    if last:
-        got = refs[:2]
-        del refs[:2]
-    hid, dpre, dbs, w2v, t1, t2, s1k, s1s, s2k, s2s, sems = refs[:11]
-    if last:
-        far, csems = refs[11:]
-        crossing = [remote(far.at[k], got[k], csems, k, "c") for k in range(2)]
-    stages = (s1k, s1s, s2k, s2s)
-    i = pl.program_id(0)
+def mlp_kernel(sh2, g, kept, mod, w1, b1, chan, w2,
+               on_a0, q_a0, on_b0, q_b0, keep_a0, keep_b0, on_a1, q_a1, on_b1, q_b1, keep_a1, keep_b1,
+               k2a, s2a, k2b, s2b, branch_o, ds2_o, branch_r, ds2_r, sum1_o, sum2_o,
+               sh2v, gv, dbs, w1v, w2v, hid, dpre, br, ds, far, tt_, ka, sa, kb, sb, ra, rb, ona, onb,
+               fsems, csems, lsems, wsems, osems):
     z, c, y, x = place()
-
-    @pl.when(i == 0)
-    def _():
-        copy = pltpu.make_async_copy(w2.at[:, c, f], w2v, sems.at[4])
+    out0 = (on_a0, q_a0, on_b0, q_b0, keep_a0, keep_b0)
+    out1 = (on_a1, q_a1, on_b1, q_b1, keep_a1, keep_b1)
+    outs = (out0, out1)
+
+    def weights(f):
+        return [
+            pltpu.make_async_copy(w1.at[f], w1v.at[f % 2], wsems.at[0, f % 2]),
+            pltpu.make_async_copy(w2.at[:, c, f], w2v.at[f % 2], wsems.at[1, f % 2]),
+        ]
+
+    def first(f):
+        k, out = f % 2, outs[f]
+        return [
+            remote(sa.at[k, 1], ra.at[k], fsems, 4 * k, "x"), remote(sb.at[k, 1], rb.at[k], fsems, 4 * k + 1, "y"),
+            remote(sa.at[k, 0], out[1], fsems, 4 * k + 2, "x"), remote(sb.at[k, 0], out[3], fsems, 4 * k + 3, "y"),
+        ]
+
+    def stored(f):
+        k = f % 2
+        if f == NF - 1:
+            pairs = ((ka.at[k], k2a), (sa.at[k], s2a), (kb.at[k], k2b), (sb.at[k], s2b))
+        else:
+            pairs = ((ka.at[k, 0], outs[f][4]), (kb.at[k, 0], outs[f][5]))
+        return [pltpu.make_async_copy(src, dst, osems.at[k, j]) for j, (src, dst) in enumerate(pairs)]
+
+    def onward(f):
+        k = f % 2
+        for copy in first(f):
+            copy.wait()
+        for kv, rv, on in ((ka, ra, ona), (kb, rb, onb)):
+            on[k] = (kv[k, 1].astype(f32) + rv[k].astype(f32)).astype(bf16)
+        copies = [
+            pltpu.make_async_copy(src.at[k], dst, osems.at[k, 4 + j])
+            for j, (src, dst) in enumerate(((ona, outs[f][0]), (onb, outs[f][2])))
+        ]
+        for copy in copies:
+            copy.start()
+        return copies
+
+    loads = [pltpu.make_async_copy(src, dst, lsems.at[k]) for k, (src, dst) in enumerate(((g, gv), (sh2, sh2v)))]
+    for copy in loads + weights(0):
         copy.start()
-        copy.wait()
-
-    part = pl.ds(pl.multiple_of((1 - i) * LH, LH), LH)
-    w1v = w1[0]
-    w2f = w2v[...].reshape(FB, D)
-    db = (g[...].astype(f32) * mod[5:6, :] * kept[...]).astype(bf16)
-    dbs[part, :] = db
-    v = dot_nn(sh2[part, :], w1v) + b1[0]
-    v2 = v * v
-    th = jnp.tanh(GELU_K * v * (1.0 + GELU_C * v2))
-    half = 0.5 * (1.0 + th)
-    on = chan[0]
-    hidden = (v * half * on).astype(bf16)
-    hid[part, :] = hidden
-    slope = (half + (0.5 * GELU_K) * v * (1.0 - th * th) * (1.0 + (3.0 * GELU_C) * v2)) * on
-    d_pre = (dot_nt(db, w2f) * slope).astype(bf16)
-    dpre[part, :] = d_pre
-    branch, ds2 = dot_nn(hidden, w2f), dot_nt(d_pre, w1v)
-    if before is not None:
-        branch = branch + before[0][...].astype(f32)
-        ds2 = ds2 + before[1][...].astype(f32)
-    branch, ds2 = branch.astype(bf16), ds2.astype(bf16)
-    if last:
-
-        @pl.when(i == 0)
-        def _():
-            far[0] = branch
-            far[1] = ds2
-            for copy in crossing:
+    loads[0].wait()
+    sum2 = jnp.zeros((1, D), f32)
+    for j in range(4):
+        part = slice(LB * j, LB * (j + 1))
+        db = (gv[part, :].astype(f32) * mod[5:6, :] * kept[part, :]).astype(bf16)
+        dbs[part, :] = db
+        sum2 += jnp.sum(db.astype(f32), axis=0, keepdims=True)
+    sum2_o[...] = sum2
+    loads[1].wait()
+    crossing = [remote(far.at[j], dst, csems, j, "c") for j, dst in enumerate((branch_r, ds2_r))]
+    waiting = []
+    for f in range(NF):
+        for copy in weights(f):
+            copy.wait()
+        if f + 1 < NF:
+            for copy in weights(f + 1):
                 copy.start()
-
-        @pl.when(i == 1)
-        def _():
-            branch_o[...] = branch
-            ds2_o[...] = ds2
-    else:
-        branch_o[...] = branch
-        ds2_o[...] = ds2
-    s1 = jnp.sum(d_pre.astype(f32), axis=0, keepdims=True)
-    s2 = jnp.sum(db.astype(f32), axis=0, keepdims=True)
-
-    @pl.when(i == 0)
-    def _():
-        sum1_o[...] = s1
-        sum2_o[...] = s2
-
-    @pl.when(i == 1)
-    def _():
-        sum1_o[...] += s1
-        sum2_o[...] += s2
+        w1f, w2f = w1v[f % 2], w2v[f % 2].reshape(FB, D)
+        on = chan[f]
+        sum1 = jnp.zeros((1, FB), f32)
+        for side in (1, 0):
+            part = slice(LH * side, LH * (side + 1))
+            v = dot_nn(sh2v[part, :], w1f) + b1[f]
+            v2 = v * v
+            th = jnp.tanh(GELU_K * v * (1.0 + GELU_C * v2))
+            half = 0.5 * (1.0 + th)
+            hidden = (v * half * on).astype(bf16)
+            hid[part, :] = hidden
+            slope = (half + (0.5 * GELU_K) * v * (1.0 - th * th) * (1.0 + (3.0 * GELU_C) * v2)) * on
+            d_pre = (dot_nt(dbs[part, :], w2f) * slope).astype(bf16)
+            dpre[part, :] = d_pre
+            sum1 += jnp.sum(d_pre.astype(f32), axis=0, keepdims=True)
+            branch, ds2 = dot_nn(hidden, w2f), dot_nt(d_pre, w1f)
+            if f > 0:
+                branch, ds2 = branch + br[part, :], ds2 + ds[part, :]
+            if f < NF - 1:
+                br[part, :] = branch
+                ds[part, :] = ds2
+            elif side == 1:
+                far[0] = branch.astype(bf16)
+                far[1] = ds2.astype(bf16)
+                for copy in crossing:
+                    copy.start()
+            else:
+                branch_o[...] = branch.astype(bf16)
+                ds2_o[...] = ds2.astype(bf16)
+        sum1_o[f] = sum1
+        k = f % 2
         for m in range(3):
             cut = slice(m * D // 3, (m + 1) * D // 3)
-            p = dot_tn(sh2[:, cut], dpre[...]).astype(bf16)
+            p = dot_tn(sh2v[:, cut], dpre[...]).astype(bf16)
             for t in range(4):
-                t1[t, cut, :] = p[:, FZ * t : FZ * (t + 1)]
-        for m in range(3):
-            cut = slice(m * FB // 3, (m + 1) * FB // 3)
-            p = dot_tn(hid[:, cut], dbs[...]).astype(bf16)
-            for t in range(4):
-                t2[t, cut, :] = p[:, TD * t : TD * (t + 1)]
+                tt_[t, cut, :FZ] = p[:, FZ * t : FZ * (t + 1)]
         for rz in range(4):
             zz = flip(z, rz)
             for ry in range(2):
                 for rx in range(2):
                     tt = (ry + y) % 2 * 2 + (rx + x) % 2
-                    one = [
-                        t1[tt, pl.ds(pl.multiple_of(zz * DZ + (rc + c) % 2 * DC, 16), DC), :] for rc in range(2)
-                    ]
-                    two = t2[tt, pl.ds(pl.multiple_of(zz * FZ, 16), FZ), :]
-                    pack_hidden(jnp.concatenate(one, axis=0), two, (s1k, s1s)[rx], (s2k, s2s)[ry], ry, rx, rz)
-        copies = [pltpu.make_async_copy(a, b, sems.at[k]) for k, (a, b) in enumerate(zip(stages, slots))]
-        for copy in copies:
+                    o = (ka, sa)[rx]
+                    tails = []
+                    for rc in range(2):
+                        block = tt_[tt, pl.ds(pl.multiple_of(zz * DZ + (rc + c) % 2 * DC, 16), DC), :FZ]
+                        o[k, ry, rz, DC * rc : DC * (rc + 1), :] = block[:, :LANES]
+                        tails.append(block[:, LANES:])
+                    o[k, ry, rz, 2 * DC :, :] = jnp.concatenate(tails, axis=1)
+        for m in range(3):
+            cut = slice(m * FB // 3, (m + 1) * FB // 3)
+            p = dot_tn(hid[:, cut], dbs[...]).astype(bf16)
+            for t in range(4):
+                tt_[t, cut, :] = p[:, TD * t : TD * (t + 1)]
+        for rz in range(4):
+            zz = flip(z, rz)
+            for ry in range(2):
+                for rx in range(2):
+                    tt = (ry + y) % 2 * 2 + (rx + x) % 2
+                    o = (kb, sb)[ry]
+                    block = tt_[tt, pl.ds(pl.multiple_of(zz * FZ, 16), FZ), :]
+                    o[k, rx, rz, :FZ, :] = block[:, :LANES]
+                    o[k, rx, rz, FZ : 2 * FZ, :] = block[:, LANES : 2 * LANES]
+                    q = FZ // 4
+                    o[k, rx, rz, 2 * FZ :, :] = jnp.concatenate(
+                        [block[q * j : q * (j + 1), 2 * LANES :] for j in range(4)], axis=1
+                    )
+        if f < NF - 1:
+            for copy in first(f):
+                copy.start()
+        for copy in stored(f):
             copy.start()
-        for copy in copies:
-            copy.wait()
-        if last:
-            for copy in crossing:
+        waiting += stored(f)
+        if f > 0:
+            waiting += onward(f - 1)
+        if f == NF - 2:
+            for copy in waiting:
                 copy.wait()
+            waiting = []
+    for copy in waiting + crossing:
+        copy.wait()
 
 
 def middle_kernel(ds, ds_r, br, br_r, attn, tok, g, kept, mod, bias2, mixed, wp,
@@ -787,7 +829,7 @@
     resid = tok[...].astype(f32) + mod[2:3, :] * at
     normed2, inverse2 = normalize(resid)
     ds2 = ds[...].astype(f32) + ds_r[...].astype(f32)
-    kb = kept[...] * (br[...].astype(f32) + br_r[...].astype(f32) + bias2[...])
+    kb = kept[...] * (br[...].astype(f32) + br_r[...].astype(f32) + bias2[...].astype(f32).reshape(1, D))
     out_o[...] = (resid + mod[5:6, :] * kb).astype(bf16)
     d_resid = gf + normalize_back(ds2 * (1.0 + mod[4:5, :]), normed2, inverse2)
     d_resid_o[...] = d_resid
@@ -874,10 +916,10 @@
         out[:, 2 * WC + HD * h : 2 * WC + HD * (h + 1)] = dv[h].astype(bf16)
 
 
-def end_kernel(shifted, dqkv, extra, wq, d_resid, tok, mod, sums_mid, f0, f1, f2, sent_p, kept_p, freq,
+def end_kernel(shifted, dqkv, extra, wq, d_resid, tok, mod, sums_mid, f0, f1, sent_2, kept_2, sent_p, kept_p, freq,
                grad, gq_o, gp_o, g1_o, g2_o, ada_o, ada_bias_o, line_o,
                t1, ka, sa, kb, sb, ra, rb, ona, onb, r2a, r2b, zs, zk, zr, wqv, dres, tokv, fv, far, got, gb,
-               item, item_r, out_shares, square, every, row_out, row_in, mine, theirs, mine_q, theirs_q, pk, pr,
+               item, item_r, out_shares, square, every, row_out, row_in, mine, theirs, mine_q, theirs_q, pk, pr, br,
                qsems, csems, tsems, ssems, psems, lsems):
     z, c, y, x = place()
     t, b = 2 * y + x, 2 * z + c
@@ -885,10 +927,11 @@
         pltpu.make_async_copy(src, dst, lsems.at[k])
         for k, (src, dst) in enumerate(
             ((wq, wqv), (d_resid, dres), (tok.at[pl.ds(0, LH)], tokv), (f0, fv.at[0]), (f1, fv.at[1]),
-             (f2, fv.at[2]), (kept_p, pk))
+             (kept_2, fv.at[2]), (kept_p, pk))
         )
     ]
-    third_p = [remote(sent_p.at[k], pr.at[k], psems, k, f"z{k + 1}") for k in (2, 1, 0)]
+    third_p = [remote(sent_2.at[k], br.at[k], psems, 3 + k, f"z{k + 1}") for k in (2, 1, 0)]
+    third_p += [remote(sent_p.at[k], pr.at[k], psems, k, f"z{k + 1}") for k in (2, 1, 0)]
     for copy in third_p + loads:
         copy.start()
 
@@ -968,12 +1011,6 @@
     over = remote(item, item_r, csems, 2, "c")
     over.start()
 
-    for k in (3, 4, 5, 6):
-        loads[k].wait()
-    for f in range(NF):
-        mine[G1R * f : G1R * (f + 1), :] = fv[f, :G1R, :].astype(bf16)
-    swap = remote(mine, theirs, csems, 3, "c")
-    swap.start()
     over.wait()
     v = item[...] + item_r[...]
     n = D // 2
@@ -1006,13 +1043,6 @@
                     start = FF // 8 * at + FZ * f
                     g1_o[:, start : start + FZ] = jnp.concatenate(pair, axis=1)
 
-    own_columns(None, [[fv[f, :DC, :], fv[f, 2 * DC : 3 * DC, : FZ - LANES]] for f in range(NF)], True)
-    for f in range(NF):
-        part = fv[f, G1R:, :]
-        tail = part[2 * FZ :]
-        tail = jnp.concatenate([tail[:, 32 * k : 32 * (k + 1)] for k in range(4)], axis=0)
-        g2_o[FZ * f : FZ * (f + 1), :] = jnp.concatenate([part[:FZ], part[FZ : 2 * FZ], tail], axis=1)
-
     for copy in first_q:
         copy.wait()
     for kv, rv, on in ((ka, ra, ona), (kb, rb, onb)):
@@ -1020,12 +1050,28 @@
     second_q = [remote(ona, r2a, qsems, 4, "y"), remote(onb, r2b, qsems, 5, "x")]
     for copy in second_q:
         copy.start()
-    for copy in third_p + meeting:
+    for copy in meeting:
         copy.wait()
     spread_z = [remote(square, every.at[z], ssems, 2 + k, f"z{k}") for k in (1, 2, 3)]
     every[z] = square[...]
     for copy in spread_z:
         copy.start()
+
+    for k in (3, 4, 5, 6):
+        loads[k].wait()
+    for copy in third_p:
+        copy.wait()
+    fv[2] = fv[2] + br[0].astype(f32) + br[1].astype(f32) + br[2].astype(f32)
+    for f in range(NF):
+        mine[G1R * f : G1R * (f + 1), :] = fv[f, :G1R, :].astype(bf16)
+    swap = remote(mine, theirs, csems, 3, "c")
+    swap.start()
+    own_columns(None, [[fv[f, :DC, :], fv[f, 2 * DC : 3 * DC, : FZ - LANES]] for f in range(NF)], True)
+    for f in range(NF):
+        part = fv[f, G1R:, :]
+        tail = part[2 * FZ :]
+        tail = jnp.concatenate([tail[:, 32 * k : 32 * (k + 1)] for k in range(4)], axis=0)
+        g2_o[FZ * f : FZ * (f + 1), :] = jnp.concatenate([part[:FZ], part[FZ : 2 * FZ], tail], axis=1)
     part = pk[...] + pr[0].astype(f32) + pr[1].astype(f32) + pr[2].astype(f32)
     tail = part[2 * DC :]
     tail = jnp.concatenate([tail[:, 32 * k : 32 * (k + 1)] for k in range(3)], axis=0)
@@ -1085,6 +1131,24 @@
     home_wait(*home)
 
 
+def final_kernel(out_rows, grad_rows, gq, gp, g1, g2, ada, ada_bias, line,
+                 out, grad, gq_o, gp_o, g1_o, g2_o, ada_o, ada_bias_o, b_fc1, b_fc2, b_proj, b_q, b_v):
+    out[...] = out_rows[...]
+    grad[...] = grad_rows[...].astype(f32)
+    gq_o[...] = gq[...]
+    gp_o[...] = gp[...]
+    g1_o[...] = g1[...]
+    g2_o[...] = jnp.transpose(g2[...])
+    ada_o[...] = ada[...]
+    ada_bias_o[...] = ada_bias[...]
+    n1, n = FF // 32 - LANES, D // 32
+    second = line[1:2, :]
+    b_fc1[...] = jnp.concatenate([line[0:1, :], second[:, :n1]], axis=1)
+    for k, ref in enumerate((b_fc2, b_proj, b_q)):
+        ref[...] = second[:, n1 + n * k : n1 + n * (k + 1)]
+    b_v[...] = line[2:3, :n]
+
+
 def one_item_per_chip(
     tokens, cotangent, timesteps, bucket_ids, head_masks, channel_masks, skip_rows,
     w_qkv, q_bias, v_bias, w_proj, proj_bias, w_fc1, fc1_bias, w_fc2, fc2_bias, ada_weight, ada_bias,
@@ -1096,23 +1160,21 @@
     def core_half(v, *dims):
         return lax.dynamic_index_in_dim(v.reshape(dims), c, 1, keepdims=False)
 
-    vmem = pl.BlockSpec(memory_space=pltpu.VMEM)
-    skips = skip_rows.reshape(-1, LANES)
-    ints = jnp.concatenate([timesteps, bucket_ids, jnp.zeros((LANES - 3,), jnp.int32)]).reshape(1, LANES)
-    ints = jnp.concatenate([skips, ints, jnp.zeros((7 - skips.shape[0], LANES), jnp.int32)], axis=0)
-    freq = jnp.exp(-math.log(10000.0) * jnp.arange(D // 2, dtype=f32) / (D // 2)).reshape(1, D // 2)
+    vmem, smem = pl.BlockSpec(memory_space=pltpu.VMEM), pl.BlockSpec(memory_space=pltpu.SMEM)
+    steps = -np.float32(math.log(10000.0)) * np.arange(D // 2, dtype=np.float32) / np.float32(D // 2)
+    freq = jnp.asarray(np.exp(steps).reshape(1, D // 2))
     ada_cols = ada_weight.shape[1]
     front, _ = call(
         front_kernel, "front",
         (sds((L, D), bf16), sds((L, D), bf16), sds((L, D), bf16), sds((L, 3 * WC), bf16), sds((D, 3 * WC), bf16),
          sds((NF, D, FB), bf16), sds((8, D), f32), sds((L, 1), f32), sds((1, WC), f32), sds((NF, 1, FB), f32),
          sds((NF, 1, FB), f32)),
-        (tokens, cotangent, ints, ada_weight.T, ada_bias.reshape(1, ada_cols), freq, head_masks.T, channel_masks.T,
-         w_qkv, w_fc1, q_bias.reshape(1, D), v_bias.reshape(1, D), fc1_bias.reshape(1, FF)),
-        in_specs=[ANY, ANY, vmem, ANY, vmem, vmem, vmem, vmem, ANY, ANY, vmem, vmem, vmem],
+        (tokens, cotangent, timesteps, bucket_ids, skip_rows, ada_weight.T, ada_bias, head_masks, channel_masks,
+         w_qkv, w_fc1, q_bias, v_bias, fc1_bias, freq),
+        in_specs=[ANY, ANY, smem, smem, vmem, ANY, vmem, vmem, vmem, ANY, ANY, vmem, vmem, vmem, vmem],
         out_specs=[ANY, ANY, vmem, vmem, ANY, ANY] + [vmem] * 5,
         scratch=[vm(L, D), vm(L, D), vm(D, 3 * D), vm(D, 3 * WC), vm(D, FF), vm(NF, D, FB), vm(ada_cols, D),
-                 vm(8, LANES, dtype=jnp.int32), vm(8, ada_cols, dtype=f32), vm(3, 8, ada_cols, dtype=f32),
+                 vm(8, LANES, dtype=jnp.int32), vm(8, LANES, dtype=jnp.int32), vm(8, ada_cols, dtype=f32), vm(3, 8, ada_cols, dtype=f32),
                  vm(4, 8, ada_cols, dtype=f32), pltpu.SemaphoreType.DMA((2, 5)), pltpu.SemaphoreType.DMA((2, 4)),
                  pltpu.SemaphoreType.DMA((2, 3)), pltpu.SemaphoreType.DMA((6,))],
         peers=("c", "t0", "t1", "x", "y", "xy"), cid=10, flops=2 * L * D * 3 * WC, nbytes=50e6,
@@ -1123,7 +1185,7 @@
     (mixed, shifted2, attn), _ = call(
         functools.partial(attn_kernel, 256), "attn",
         (sds((L, WC), bf16), sds((L, D), bf16), sds((LH, D), f32)),
-        (qkv, hmask, wp, proj_bias.astype(f32).reshape(1, D), tok, mod),
+        (qkv, hmask, wp, proj_bias, tok, mod),
         in_specs=[vmem, vmem, ANY, vmem, ANY, vmem],
         out_specs=[ANY, vmem, vmem],
         scratch=[vm(HC, L, HD)] * 3 + [vm(L, WC), vm(L, WC), vm(2, 4, DC, D), vm(L, D),
@@ -1131,43 +1193,27 @@
         peers=("c",), cid=11, flops=16e9, nbytes=5e6,
     )
 
-    firsts, kepts, sums1, results, before = [], [], [], [], []
-    half = pl.BlockSpec((LH, D), lambda i: (1 - i, 0))
     slot1, slot2 = sds((2, 4, G1R, LANES), bf16), sds((2, 4, G2R, LANES), bf16)
-    for f in range(NF):
-        jobs = []
-        if f > 0:
-            jobs.append(FirstSum(*slots))
-        if f > 1:
-            jobs.append(SecondSum(*firsts[f - 2], *kepts[f - 2]))
-        last = f == NF - 1
-        pick = lambda i, f=f: (f, 0, 0)
-        out_shape = [slot1, slot1, slot2, slot2] + [sds((LH if last else L, D), bf16)] * 2
-        out_shape += [sds((1, FB), f32), sds((1, D), f32)] + [sds((LH, D), bf16)] * (2 * last)
-        own, given = call(
-            functools.partial(mlp_kernel, f), f"mlp{f}",
-            out_shape, (shifted2, g_all, kept, mod, w1, b1, chan, w2, *before),
-            grid=(2,),
-            in_specs=[once(L, D), half, pl.BlockSpec((LH, 1), lambda i: (1 - i, 0)), full((8, D)),
-                      pl.BlockSpec((1, D, FB), pick, pipeline_mode=pl.Buffered(1)),
-                      pl.BlockSpec((1, 1, FB), pick), pl.BlockSpec((1, 1, FB), pick), ANY] + [half] * len(before),
-            out_specs=[ANY] * 4 + [full((LH, D)) if last else half] * 2 + [full((1, FB)), full((1, D))]
-            + [ANY] * (2 * last),
-            scratch=[vm(L, FB), vm(L, FB), vm(L, D), vm(4, FZ, D), vm(4, D, FZ), vm(4, FB, TD)]
-            + [vm(*s.shape) for s in (slot1, slot1, slot2, slot2)] + [pltpu.SemaphoreType.DMA((5,))]
-            + ([vm(2, LH, D), pltpu.SemaphoreType.DMA((2, 2))] if last else []),
-            peers=("c",) if last else (), jobs=jobs, cid=f,
-            flops=12 * L * D * FB, nbytes=20e6,
-        )
-        slots, before = own[:4], own[4:6]
-        kepts.append((slots[0], slots[2]))
-        sums1.append(own[6])
-        if f > 0:
-            firsts.append(given[0])
-        if f > 1:
-            results.append(given[1])
-    sum2 = own[7]
-    branch_r, ds2_r = own[8:]
+    part1, part2 = sds(slot1.shape[1:], bf16), sds(slot2.shape[1:], bf16)
+    one = [part1, part1, part2, part2, part1, part2]
+    rows_half = sds((LH, D), bf16)
+    dma = pltpu.SemaphoreType.DMA
+    own, _ = call(
+        mlp_kernel, "mlp",
+        one + one + [slot1, slot1, slot2, slot2] + [rows_half] * 4 + [sds((NF, 1, FB), f32), sds((1, D), f32)],
+        (shifted2, g_all, kept, mod, w1, b1, chan, w2),
+        in_specs=[ANY, ANY, vmem, vmem, ANY, vmem, vmem, ANY],
+        out_specs=[ANY] * 16 + [vmem, vmem, ANY, ANY, vmem, vmem],
+        scratch=[vm(L, D), vm(L, D), vm(L, D), vm(2, D, FB), vm(2, 4, FZ, D), vm(L, FB), vm(L, FB),
+                 vm(L, D, dtype=f32), vm(L, D, dtype=f32), vm(2, LH, D), vm(4, D, TD)]
+        + [vm(2, *slot1.shape)] * 2 + [vm(2, *slot2.shape)] * 2
+        + [vm(2, *p.shape) for p in (part1, part2)] * 2
+        + [dma((2, 8)), dma((2, 2)), dma((2,)), dma((2, 2)), dma((2, 6))],
+        peers=("c", "x", "y"), cid=0,
+        flops=36 * L * D * FB, nbytes=40e6,
+    )
+    second0, second1, slots = own[:6], own[6:12], own[12:16]
+    branch, ds2, branch_r, ds2_r, sum1, sum2 = own[16:]
 
     n = LH // 4
     row = rows(n, D)
@@ -1176,33 +1222,30 @@
         middle_kernel, "middle",
         (sds((LH, D), f32), sds((LH, D), bf16), sds((L, WC), bf16), slot_a, slot_a, slot_b, slot_b,
          sds((8, D), f32), sds((8, D), f32)),
-        (before[1], ds2_r, before[0], branch_r, attn, tok, g_all, kept, mod, fc2_bias.astype(f32).reshape(1, D),
+        (ds2, ds2_r, branch, branch_r, attn, tok, g_all, kept, mod, fc2_bias,
          mixed, wp),
         grid=(4,),
-        in_specs=[row] * 7 + [rows(n, 1), full((8, D)), full((1, D)), once(L, WC), ANY],
+        in_specs=[row] * 7 + [rows(n, 1), full((8, D)), vmem, once(L, WC), ANY],
         out_specs=(row, row, full((L, WC)), full(slot_a.shape), full(slot_a.shape), full(slot_b.shape),
                    full(slot_b.shape), full((8, D)), full((8, D))),
         scratch=[vm(L, D), vm(4, WC, TD), vm(4, DC, D), pltpu.SemaphoreType.DMA((2, 4)), pltpu.SemaphoreType.DMA],
         peers=("c",), cid=3,
-        jobs=[FirstSum(*slots), SecondSum(*firsts[1], *kepts[1]), ThirdSum(*results[0])],
+        jobs=[FirstSum(*slots), SecondSum(*second0)],
         flops=4 * L * D * WC, nbytes=20e6,
     )
     d_resid, out_rows, dh, *slots_p, sums_mid, sum_attn = own
-    firsts.append(given[0])
-    results.append(given[1])
-    finals = [given[2][0]]
+    first2, result0 = given
     dqkv, given = call(
         functools.partial(attn_back_kernel, 512), "attn_back",
         sds((L, 3 * WC), bf16), (qkv, dh, hmask),
         scratch=[vm(HC, L, HD)] * 4 + [vm(HC, L, HD, dtype=f32)] * 2,
         cid=4, ticks=True,
-        jobs=[SecondThird(*firsts[2], *kepts[2]), FirstSecond(*slots_p), ThirdSum(*results[1]), GoHome(out_rows)],
+        jobs=[SecondThird(*second1), SecondSum(*first2, slots[0], slots[2]), FirstSecond(*slots_p), ThirdSum(*result0),
+              GoHome(out_rows)],
         flops=30e9, nbytes=9e6,
     )
-    finals += [given[2][0], given[0][0]]
-    sent_p, kept_p = given[1]
-    output = given[3][0]
-    sum_fc1 = jnp.concatenate(sums1, axis=0).reshape(NF, 4, FZ).transpose(1, 0, 2).reshape(4, 4, FF // 32)
+    final1, (sent2, kept2), (sent_p, kept_p), final0, output = given[0][0], given[1], given[2], given[3][0], given[4][0]
+    sum_fc1 = sum1.reshape(NF, 4, FZ).transpose(1, 0, 2).reshape(4, 4, FF // 32)
     own_part = lambda v: core_half(v, 4, 2, 4, D // 32)
     line = jnp.concatenate(
         [sum_fc1, own_part(sum2), own_part(sum_attn[0]), jnp.zeros((4, 4, 3 * LANES - FF // 32 - D // 16), f32)], axis=2
@@ -1211,31 +1254,44 @@
     slot_q = vm(2, 4, QA, LANES)
     fourth = vm(4, QA, LANES)
     width = ada_cols + LANES
-    dma = pltpu.SemaphoreType.DMA
     (grad_rows, gq, gp, g1, g2, grad_ada_weight, grad_ada_bias, line), _ = call(
         end_kernel, "end",
         (sds((2, LB, D), bf16), sds((DC, 3 * TD), f32), sds((DC, TD), f32), sds((DC, FF // 4), f32),
          sds((FF // 8, TD), f32), sds((DC, ada_cols), f32), sds((1, ada_cols // 2), f32), sds((16, LANES), f32)),
-        (shifted, dqkv, extra, wq, d_resid, tok, mod, sums_mid, *finals, sent_p, kept_p, freq.reshape(4, 1, DC)),
-        in_specs=[vmem] * 3 + [ANY] * 3 + [vmem] * 2 + [ANY] * 5 + [vmem],
+        (shifted, dqkv, extra, wq, d_resid, tok, mod, sums_mid, final0, final1, sent2, kept2, sent_p, kept_p,
+         freq.reshape(4, 1, DC)),
+        in_specs=[vmem] * 3 + [ANY] * 3 + [vmem] * 2 + [ANY] * 6 + [vmem],
         out_specs=[ANY] + [vmem] * 7,
         scratch=[vm(4, D, 3 * DC)] + [slot_q] * 6 + [fourth] * 4
         + [vm(3, QR, LANES), vm(QR, LANES, dtype=f32), vm(3, QR, LANES), vm(D, 3 * WC), vm(LH, D, dtype=f32),
            vm(LH, D), vm(NF, G1R + G2R, LANES, dtype=f32)] + [vm(2, LB, D)] * 3
         + [vm(8, D, dtype=f32)] * 2 + [vm(4, 1, width, dtype=f32)] * 2
         + [vm(4, 4, 1, width, dtype=f32), vm(1, 1, ada_cols, dtype=f32), vm(4, 1, ada_cols, dtype=f32)]
-        + [vm(NF * G1R, LANES)] * 2 + [vm(7 * DC, LANES)] * 2 + [vm(PR, LANES, dtype=f32), vm(3, PR, LANES)]
-        + [dma((2, 9)), dma((2, 5)), dma((2, 2)), dma((2, 9)), dma((2, 3)), dma((8,))],
+        + [vm(NF * G1R, LANES)] * 2 + [vm(7 * DC, LANES)] * 2 + [vm(PR, LANES, dtype=f32), vm(3, PR, LANES),
+                                                                      vm(3, G1R + G2R, LANES)]
+        + [dma((2, 9)), dma((2, 5)), dma((2, 2)), dma((2, 9)), dma((2, 6)), dma((8,))],
         peers=("c", "t0", "t1", "x", "y", "xy", "z1", "z2", "z3"), cid=5,
         flops=4 * L * D * 3 * WC, nbytes=30e6,
     )
-    grad_tokens = grad_rows.astype(f32)
-    line = line.reshape(-1)
-    n1, n = FF // 32, D // 32
-    b_fc1, b_fc2, b_proj = line[:n1], line[n1 : n1 + n], line[n1 + n : n1 + 2 * n]
-    b_q, b_v = line[n1 + 2 * n : n1 + 3 * n], line[2 * LANES : 2 * LANES + n]
-    return (output, grad_tokens, gq, b_q, b_v, gp, b_proj, g1, b_fc1, g2, b_fc2, grad_ada_weight,
-            grad_ada_bias.reshape(-1))
+    thin = lambda height, width: pl.BlockSpec((height, width), lambda i: (i, 0))
+    tokens_spec = pl.BlockSpec((2, LB // 2, D), lambda i: (0, i, 0))
+    ends = [thin(DC // 2, 3 * TD), thin(DC // 2, TD), thin(DC // 2, FF // 4)]
+    bias_cols = ada_cols // 2
+    finals, _ = call(
+        final_kernel, "final",
+        (sds((2, LB, D), bf16), sds((2, LB, D), f32), sds((DC, 3 * TD), f32), sds((DC, TD), f32), sds((DC, FF // 4), f32),
+         sds((TD, FF // 8), f32), sds((DC, ada_cols), f32), sds((1, bias_cols), f32), sds((1, FF // 32), f32))
+        + (sds((1, D // 32), f32),) * 4,
+        (output, grad_rows, gq, gp, g1, g2, grad_ada_weight, grad_ada_bias, line),
+        grid=(2,),
+        in_specs=[tokens_spec, tokens_spec, *ends, full((FF // 8, TD)), thin(DC // 2, ada_cols), full((1, bias_cols)),
+                  full((16, LANES))],
+        out_specs=[tokens_spec, tokens_spec, *ends, full((TD, FF // 8)), thin(DC // 2, ada_cols), full((1, bias_cols)),
+                   full((1, FF // 32))] + [full((1, D // 32))] * 4,
+    )
+    output, grad_tokens, gq, gp, g1, g2, g_ada, *lines = finals
+    ada_b, b_fc1, b_fc2, b_proj, b_q, b_v = [v.reshape(-1) for v in lines]
+    return (output, grad_tokens, gq, b_q, b_v, gp, b_proj, g1, b_fc1, g2.T, b_fc2, g_ada, ada_b)
 
 
 def gelu_tanh(values):

time: 355 us -> 316 us (0.89)
  local copies, waits for them, and re-layouts: 20 us -> 1.96 us
  Pallas kernels: 321 us -> 306 us
  other arithmetic: 6.99 us -> 1.43 us
    pallas_call x8 -> x7, Pallas kernels: 321 us -> 306 us  [call(): pl.pallas_call(run, out_shape=out_shape + [o for j in jobs for o in j.out...]
    unnamed x32 -> x4, local copies, waits for them, and re-layouts: 8.24 us -> 0.01 us
    reshape x10 -> x3, local copies, waits for them, and re-layouts: 7.24 us -> 0.19 us  [one_item_per_chip(): sum_fc1 = sum1.reshape(NF, 4, FZ).transpose(1, 0, 2).reshape(4, 4, FF // 32)]
where the time goes in v5:
time: 316 us; the launch traced here: 311 us
  Pallas kernels  306 us (97%)
    pallas_call x7, Pallas kernels, call(): pl.pallas_call(run, out_shape=out_shape + [o for j in jobs for o in j.out...  306 us

profile of v5, /device:TPU:0, one launch (start us, length us, event | category | flops | bytes accessed | tf_op | source)
XLA Modules:
  0.0 311.2 jit_solution(16113095938794349960)
XLA Ops:
  1.3 42.2 %front.1 = (bf16[1024,1152]{1,0:T(8,128)(2,1)}, bf16[1024,1152]{1,0:T(8,128)(2,1)}, bf16[1024,1152]{1,0:T(8,128)(2,1)}, bf16[1024,1728]{1,0:T(8,128)(2,1)}, bf16...) custom-call(bf16[2,256,1152]{2,1,0:T(8,128)(2,1)} %refs_0_.1, ...), custom_call_target="tpu_custom_call" | custom-call | flops 4076863488 | bytes 50000000 | tf_op jit(solution)/shard_map/front/pallas_call | solution.py:425
  43.5 30.5 %attn.1 = (bf16[1024,576]{1,0:T(8,128)(2,1)}, bf16[1024,1152]{1,0:T(8,128)(2,1)}, f32[512,1152]{1,0:T(8,128)}) custom-call(bf16[1024,1728]{1,0:T(8,128)(2,1)} %get-tuple-element.93.refs_0_, f32[1,576]{1,0:T(1,128)} %get-tuple-element.94.refs_1_.refs_2_, bf16[4,2,144,1152]{3,2,1,0:T(8,128)(2,1)} %bitcast.19, bf16[1152]{0:T(1024)(128)(2,1)} %refs_3_.2, ...), custom_call_target="tpu_custom_call" | custom-call | flops 16000000000 | bytes 5000000 | tf_op jit(solution)/shard_map/attn/pallas_call | solution.py:425
  74.1 61.8 %mlp.1 = (bf16[4,432,128]{2,1,0:T(8,128)(2,1)}, bf16[4,432,128]{2,1,0:T(8,128)(2,1)}, bf16[4,432,128]{2,1,0:T(8,128)(2,1)}, bf16[4,432,128]{2,1,0:T(8,128)(2,1)}...) custom-call(bf16[1024,1152]{1,0:T(8,128)(2,1)} %get-tuple-element.97, ...), custom_call_target="tpu_custom_call" | custom-call | flops 32614907904 | bytes 40000000 | tf_op jit(solution)/shard_map/mlp/pallas_call | solution.py:425
  135.9 0.0 copy-start.1
  135.9 0.0 copy-start
  136.0 37.5 %middle.1 = (f32[512,1152]{1,0:T(8,128)}, bf16[512,1152]{1,0:T(8,128)(2,1)}, bf16[1024,576]{1,0:T(8,128)(2,1)}, bf16[2,4,176,128]{3,2,1,0:T(8,128)(2,1)}, bf16[2...) custom-call(bf16[512,1152]{1,0:T(8,128)(2,1)} %get-tuple-element.103, ...), custom_call_target="tpu_custom_call" | custom-call | flops 2717908992 | bytes 20000000 | tf_op jit(solution)/shard_map/middle/pallas_call | solution.py:425
  173.4 0.8 slice_reduce_fusion
  174.2 0.1 reshape_squeeze.3
  174.3 0.0 copy-done.1
  174.4 0.1 reshape.69
  174.5 0.0 copy-done
  174.6 0.1 reshape.67
  174.7 0.1 reshape.68
  174.8 0.1 pad.4.clone
  174.8 0.1 maximum_bitcast_fusion
  174.9 0.7 concatenate.7.refs_2_
  175.6 54.8 %attn_back.1 = (bf16[1024,1728]{1,0:T(8,128)(2,1)}, f32[864,128]{1,0:T(8,128)}, bf16[3,864,128]{2,1,0:T(8,128)(2,1)}, f32[864,128]{1,0:T(8,128)}, bf16[3,336,128...) custom-call(bf16[1024,1728]{1,0:T(8,128)(2,1)} %get-tuple-element.93.refs_0_, ...), custom_call_target="tpu_custom_call" | custom-call | flops 30000001024 | bytes 9000000 | tf_op jit(solution)/shard_map/attn_back/pallas_call | solution.py:425
  230.4 74.0 %end.1 = (bf16[2,256,1152]{2,1,0:T(8,128)(2,1)}, f32[144,864]{1,0:T(8,128)}, f32[144,288]{1,0:T(8,128)}, f32[144,1152]{1,0:T(8,128)}, f32[576,288]{1,0:T(8,128)}...) custom-call(bf16[1024,1152]{1,0:T(8,128)(2,1)} %get-tuple-element.138.refs_0_, ...), custom_call_target="tpu_custom_call" | custom-call | flops 8153726976 | bytes 30000000 | tf_op jit(solution)/shard_map/end/pallas_call | solution.py:425
  304.4 5.3 %final.1 = (bf16[2,256,1152]{2,1,0:T(8,128)(2,1)}, f32[2,256,1152]{2,1,0:T(8,128)}, f32[144,864]{1,0:T(8,128)}, f32[144,288]{1,0:T(8,128)}, f32[144,1152]{1,0:T(...) custom-call(bf16[2,256,1152]{2,1,0:T(8,128)(2,1)} %get-tuple-element, ...), custom_call_target="tpu_custom_call" | custom-call | tf_op jit(solution)/shard_map/final/pallas_call | solution.py:425
  309.7 1.3 reduce.3
  (6 shorter events, 0.1 us)
Async XLA Ops:
  135.9 38.4 %copy-start.1 = (f32[1,1152]{1,0:T(1,128)S(1)}, f32[1,1152]{1,0:T(1,128)}, u32[]{:S(2)}) copy-start(f32[1,1152]{1,0:T(1,128)} %get-tuple-element.141) | copy-start | bytes 13828
  135.9 38.6 %copy-start = (f32[3,1,768]{2,1,0:T(1,128)S(1)}, f32[3,1,768]{2,1,0:T(1,128)}, u32[]{:S(2)}) copy-start(f32[3,1,768]{2,1,0:T(1,128)} %get-tuple-element.140) | copy-start | bytes 27652
